TPU v7x, 32 devices: a whole 2x2x4 slice. The times are simulated.
32 devices in a mesh: tm: 4 (over x, core), space: 8 (over z, y).
Axes of the slice: x: 2, y: 2, z: 4, core: 2. Of those that a mesh axis runs over, the one named last changes fastest.
Arguments:
- initial: bfloat16 [135, 1024], P(None, 'space'), may hold values from -6 to 6
- forcing: bfloat16 [64, 135, 1024], P('tm', None, 'space'), may hold values from -2 to 2
- damping: float32 [1024], P('space'), may hold values from 0.003 to 0.1
- block_inv: bfloat16 [2, 135, 135], replicated, as said below
- coarse_inv: bfloat16 [2, 135, 135], replicated, as said below
- coupling: bfloat16 [6, 135, 135], replicated, may hold values from -0.078125 to 0.078125
- etype: int32 [8], P('space'), may hold values from 0 to 1
- send_index: int32 [1024], P('space'), may hold values from 0 to 127
- conn: int32 [6, 1024], P(None, 'space'), may hold values from 0 to 255
Outputs:
- states: bfloat16 [64, 135, 1024], P('tm', None, 'space')
Inputs may be any that keep to these rules, and one draw needn't show every extreme that they name: block_inv[0] is the inverse of a hexahedron's diagonal block, block_inv[1] that of a prism, with zero rows and columns from 90 on. coarse_inv[0] is the inverse of a hexahedron's coarse diagonal block, coarse_inv[1] that of a prism, with zero rows and columns from 90 on. `send_index`: the first 64 entries of a partition's list name the elements it sends to the partition before, the last 64 those it sends to the partition after. `conn`: entries below 128 name an element of the same partition; the next 64 name the columns received from the partition before, the last 64 those received from the partition after.
All inputs are finite; a program needn't handle non-finite values.
Results may differ from a plain program's by a relative error of at most 0.018.
Values may be sent and summed in bfloat16 or wider, within the bound.
No kernel may reach another device: no remote copies, remote signals or barrier semaphores. Data moves between devices by JAX's collectives and lax.ppermute only.
A program may use at most 64 MiB of HBM per device.

v0:
```python
import jax
import jax.numpy as jnp
from jax import lax
from jax.sharding import PartitionSpec as P

PRISM = 90
SWEEPS = 2
COARSEN = 4


def padded(cells, sides, width):
    for axis, dim in sides:
        count = lax.axis_size(axis)
        ends = count - 1
        head = lax.slice_in_dim(cells, 0, width, axis=dim)
        tail = lax.slice_in_dim(cells, cells.shape[dim] - width, cells.shape[dim], axis=dim)
        cells = jnp.concatenate(
            [
                lax.ppermute(tail, axis, [(i, (i + 1) % count) for i in range(ends)]),
                cells,
                lax.ppermute(head, axis, [((i + 1) % count, i) for i in range(ends)]),
            ],
            axis=dim,
        )
    return cells


def passed_along(array, axis, by):
    size = lax.axis_size(axis)
    pairs = [(i, i + by) for i in range(size) if 0 <= i + by < size]
    return lax.ppermute(array, axis, pairs)


def shards(initial, forcing, damping, block_inv, coarse_inv, coupling, etype, send_index, conn):
    width_rows = initial.shape[0]
    local_elems = initial.shape[1]
    block_count = etype.shape[0]
    block_length = local_elems // block_count
    halo_length = send_index.shape[0] // 2
    face_count = conn.shape[0]
    interval_count = forcing.shape[0] // COARSEN
    element_kinds = jnp.broadcast_to(etype[:, None], (block_count, block_length)).reshape(
        local_elems
    )
    face_rows = lax.broadcasted_iota(jnp.int32, (face_count, local_elems), 0)
    face_keep = (
        ((face_rows < face_count - 1) | (element_kinds[None, :] == 0))
        .astype(jnp.bfloat16)
        .reshape(-1)
    )
    conn_flat = conn.reshape(-1)
    rows_iota = lax.broadcasted_iota(jnp.int32, (width_rows, local_elems), 0)
    valid_rows = (rows_iota < PRISM) | (element_kinds[None, :] == 0)
    start_field = jnp.where(valid_rows, initial, jnp.zeros_like(initial))
    is_hex = (etype == 0)[:, None, None]
    fine_chosen = jnp.where(is_hex, block_inv[0][None], block_inv[1][None])
    coarse_chosen = jnp.where(is_hex, coarse_inv[0][None], coarse_inv[1][None])
    decay_rate = jnp.exp(-damping)
    coarse_decay = jnp.exp(-COARSEN * damping)

    def neighbours(iterate):
        batch_count = iterate.shape[0]
        outgoing = jnp.take(iterate, send_index, axis=2)
        received = padded(outgoing, (("space", 2),), halo_length)
        extended = jnp.concatenate(
            [iterate, received[:, :, :halo_length], received[:, :, 3 * halo_length :]], axis=2
        )
        gathered = jnp.take(extended, conn_flat, axis=2) * face_keep
        return gathered.reshape(batch_count, width_rows, face_count, local_elems)

    def propagate(start_states, drive_term, chosen):
        batch_count = start_states.shape[0]
        iterate = start_states
        for sweep_index in range(SWEEPS):
            coupled = jnp.einsum(
                "fij,njfk->nik", coupling, neighbours(iterate), preferred_element_type=jnp.float32
            )
            rhs_value = (drive_term - coupled).astype(jnp.bfloat16)
            blocked = rhs_value.reshape(batch_count, width_rows, block_count, block_length)
            applied = jnp.einsum(
                "bij,njbk->nibk", chosen, blocked, preferred_element_type=jnp.float32
            )
            iterate = applied.reshape(batch_count, width_rows, local_elems).astype(jnp.bfloat16)
        return iterate

    forcing_view = forcing.reshape(interval_count, COARSEN, width_rows, local_elems)

    def fine_step(states_now, step_index):
        drive_term = decay_rate * states_now.astype(jnp.float32) + forcing_view[
            :, step_index
        ].astype(jnp.float32)
        return propagate(states_now, drive_term, fine_chosen)

    first_device = lax.axis_index("tm") == 0
    leading = jnp.where(first_device, start_field, jnp.zeros_like(start_field))[None]
    zero_rest = jnp.zeros((interval_count - 1, width_rows, local_elems), jnp.bfloat16)
    states_now = jnp.concatenate([leading, zero_rest], axis=0)
    for step_index in range(COARSEN):
        states_now = fine_step(states_now, step_index)
    residuals = states_now
    device_count = lax.axis_size("tm")
    incoming = jnp.zeros((1, width_rows, local_elems), jnp.bfloat16)
    collected = []
    for turn_index in range(device_count):
        carried = incoming
        collected = []
        for interval_index in range(interval_count):
            coarse_drive_term = coarse_decay * carried.astype(jnp.float32)
            propagated = propagate(carried, coarse_drive_term, coarse_chosen)
            carried = (
                propagated.astype(jnp.float32)
                + residuals[interval_index : interval_index + 1].astype(jnp.float32)
            ).astype(jnp.bfloat16)
            collected.append(carried)
        if turn_index + 1 < device_count:
            incoming = passed_along(carried, "tm", 1)
    coarse_values = jnp.concatenate(collected, axis=0)
    leading = jnp.where(first_device, start_field[None], incoming)
    states_now = jnp.concatenate([leading, coarse_values[:-1]], axis=0)
    produced = []
    for step_index in range(COARSEN - 1):
        states_now = fine_step(states_now, step_index)
        produced.append(states_now)
    produced.append(coarse_values)
    return jnp.stack(produced, axis=1).reshape(forcing.shape[0], width_rows, local_elems)


def solution(mesh):
    in_specs = (
        P(None, "space"),
        P("tm", None, "space"),
        P("space"),
        P(),
        P(),
        P(),
        P("space"),
        P("space"),
        P(None, "space"),
    )
    out_specs = P("tm", None, "space")
    return jax.shard_map(shards, mesh=mesh, in_specs=in_specs, out_specs=out_specs, check_vma=False)
```

profile of v0, /device:TPU:6, one launch (start us, length us, event | category | flops | bytes accessed | tf_op | source)
XLA Modules:
  0.0 721.2 jit_solution(6646601420529029519)
XLA Ops:
  4.4 3.6 collective-permute-start.4
  11.4 4.3 collective-permute-start
  28.7 4.8 collective-permute-start.6
  57.9 4.0 collective-permute-done.9
  119.5 3.8 collective-permute-start.2
  135.4 4.7 collective-permute-start.16
  164.9 3.5 collective-permute-done.19
  184.6 3.4 collective-permute-done.21
  195.4 3.6 collective-permute-start.23
  209.0 3.7 collective-permute-start.25
  226.4 3.5 collective-permute-done.27
  236.6 3.8 collective-permute-start.29
  250.0 3.9 collective-permute-start.31
  262.3 3.3 collective-permute-done.32
  268.7 3.9 collective-permute-start.34
  282.2 4.1 collective-permute-start.36
  295.6 3.9 collective-permute-start.38
  309.0 3.9 collective-permute-start.40
  322.4 3.9 collective-permute-start.42
  335.9 3.9 collective-permute-start.44
  349.3 3.9 collective-permute-start.46
  362.7 4.1 collective-permute-start.48
  375.0 3.3 collective-permute-done.49
  381.4 3.9 collective-permute-start.51
  394.8 3.9 collective-permute-start.53
  408.3 3.9 collective-permute-start.55
  421.7 3.9 collective-permute-start.57
  435.1 3.9 collective-permute-start.59
  448.5 4.3 collective-permute-start.61
  462.0 3.9 collective-permute-start.63
  475.4 3.9 collective-permute-start.65
  487.7 3.3 collective-permute-done.66
  494.1 3.9 collective-permute-start.68
  507.5 3.9 collective-permute-start.70
  520.9 3.9 collective-permute-start.72
  534.4 4.1 collective-permute-start.74
  547.8 3.9 collective-permute-start.76
  561.2 3.9 collective-permute-start.78
  574.6 3.9 collective-permute-start.92
  588.1 3.9 collective-permute-start.94
  602.5 4.1 collective-permute-start.80
  622.1 3.9 collective-permute-start.82
  641.3 3.9 collective-permute-start.84
  649.7 3.3 gather_fusion.81
  660.7 4.2 collective-permute-start.86
  678.3 4.2 collective-permute-start.87
  686.1 5.0 collective-permute-done.88
  707.5 4.2 collective-permute-done.90
  (698 shorter events, 527.8 us)
Async XLA Ops:
  4.4 14.9 %collective-permute-start.4 = (bf16[4,135,64]{2,1,0:T(8,128)(2,1)S(1)}, bf16[4,135,64]{2,1,0:T(8,128)(2,1)S(1)}, u32[]{:S(2)}, u32[]{:S(2)}) collective-permute-start(bf16[4,135,64]{2,1,0:T(8,128)(2,1)S(1)} %get-tuple-element.35), channel_id=1, source_target_pairs={{0,1},{1,2},{2,3},{3,4},{4,5},{5,6},{6,7},{8,9},{9,10},{10,11},{11... | collective-permute-start | bytes 207368 | tf_op jit(solution)/shard_map/ppermute | solution.py:19
  8.0 11.3 %collective-permute-start.5 = (bf16[4,135,64]{2,1,0:T(8,128)(2,1)S(1)}, bf16[4,135,64]{2,1,0:T(8,128)(2,1)S(1)}, u32[]{:S(2)}, u32[]{:S(2)}) collective-permute-start(bf16[4,135,64]{2,1,0:T(8,128)(2,1)S(1)} %get-tuple-element.36), channel_id=1, source_target_pairs={{1,0},{2,1},{3,2},{4,3},{5,4},{6,5},{7,6},{9,8},{10,9},{11,10},{12... | collective-permute-start | bytes 207368 | tf_op jit(solution)/shard_map/ppermute | solution.py:21
  11.4 24.1 %collective-permute-start = (bf16[1,135,64]{1,2,0:T(8,128)(2,1)S(1)}, bf16[1,135,64]{1,2,0:T(8,128)(2,1)S(1)}, u32[]{:S(2)}, u32[]{:S(2)}) collective-permute-start(bf16[1,135,64]{1,2,0:T(8,128)(2,1)S(1)} %get-tuple-element.43), channel_id=1, source_target_pairs={{0,1},{1,2},{2,3},{3,4},{4,5},{5,6},{6,7},{8,9},{9,10},{10,11},{11... | collective-permute-start | bytes 51848 | tf_op jit(solution)/shard_map/ppermute | solution.py:19
  15.7 19.8 %collective-permute-start.1 = (bf16[1,135,64]{1,2,0:T(8,128)(2,1)S(1)}, bf16[1,135,64]{1,2,0:T(8,128)(2,1)}, u32[]{:S(2)}, u32[]{:S(2)}) collective-permute-start(bf16[1,135,64]{1,2,0:T(8,128)(2,1)S(1)} %get-tuple-element.44), channel_id=1, source_target_pairs={{1,0},{2,1},{3,2},{4,3},{5,4},{6,5},{7,6},{9,8},{10,9},{11,10},{12... | collective-permute-start | bytes 51848 | tf_op jit(solution)/shard_map/ppermute | solution.py:21
  28.7 10.9 %collective-permute-start.6 = (bf16[4,135,64]{2,1,0:T(8,128)(2,1)S(1)}, bf16[4,135,64]{2,1,0:T(8,128)(2,1)S(1)}, u32[]{:S(2)}, u32[]{:S(2)}) collective-permute-start(bf16[4,135,64]{2,1,0:T(8,128)(2,1)S(1)} %get-tuple-element.33), channel_id=1, source_target_pairs={{0,1},{1,2},{2,3},{3,4},{4,5},{5,6},{6,7},{8,9},{9,10},{10,11},{11... | collective-permute-start | bytes 207368 | tf_op jit(solution)/shard_map/ppermute | solution.py:19
  33.6 7.8 %collective-permute-start.7 = (bf16[4,135,64]{2,1,0:T(8,128)(2,1)S(1)}, bf16[4,135,64]{2,1,0:T(8,128)(2,1)S(1)}, u32[]{:S(2)}, u32[]{:S(2)}) collective-permute-start(bf16[4,135,64]{2,1,0:T(8,128)(2,1)S(1)} %get-tuple-element.34), channel_id=1, source_target_pairs={{1,0},{2,1},{3,2},{4,3},{5,4},{6,5},{7,6},{9,8},{10,9},{11,10},{12... | collective-permute-start | bytes 207368 | tf_op jit(solution)/shard_map/ppermute | solution.py:21
  50.9 6.9 collective-permute-start.8
  54.0 7.8 %collective-permute-start.9 = (bf16[4,135,64]{2,1,0:T(8,128)(2,1)S(1)}, bf16[4,135,64]{2,1,0:T(8,128)(2,1)S(1)}, u32[]{:S(2)}, u32[]{:S(2)}) collective-permute-start(bf16[4,135,64]{2,1,0:T(8,128)(2,1)S(1)} %get-tuple-element.32), channel_id=1, source_target_pairs={{1,0},{2,1},{3,2},{4,3},{5,4},{6,5},{7,6},{9,8},{10,9},{11,10},{12... | collective-permute-start | bytes 207368 | tf_op jit(solution)/shard_map/ppermute | solution.py:21
  71.9 8.4 %collective-permute-start.10 = (bf16[4,135,64]{2,1,0:T(8,128)(2,1)S(1)}, bf16[4,135,64]{2,1,0:T(8,128)(2,1)S(1)}, u32[]{:S(2)}, u32[]{:S(2)}) collective-permute-start(bf16[4,135,64]{2,1,0:T(8,128)(2,1)S(1)} %get-tuple-element.29), channel_id=1, source_target_pairs={{0,1},{1,2},{2,3},{3,4},{4,5},{5,6},{6,7},{8,9},{9,10},{10,11},{11... | collective-permute-start | bytes 207368 | tf_op jit(solution)/shard_map/ppermute | solution.py:19
  74.8 7.8 %collective-permute-start.11 = (bf16[4,135,64]{2,1,0:T(8,128)(2,1)S(1)}, bf16[4,135,64]{2,1,0:T(8,128)(2,1)S(1)}, u32[]{:S(2)}, u32[]{:S(2)}) collective-permute-start(bf16[4,135,64]{2,1,0:T(8,128)(2,1)S(1)} %get-tuple-element.30), channel_id=1, source_target_pairs={{1,0},{2,1},{3,2},{4,3},{5,4},{6,5},{7,6},{9,8},{10,9},{11,10},{12... | collective-permute-start | bytes 207368 | tf_op jit(solution)/shard_map/ppermute | solution.py:21
  92.7 8.4 %collective-permute-start.12 = (bf16[4,135,64]{2,1,0:T(8,128)(2,1)S(1)}, bf16[4,135,64]{2,1,0:T(8,128)(2,1)S(1)}, u32[]{:S(2)}, u32[]{:S(2)}) collective-permute-start(bf16[4,135,64]{2,1,0:T(8,128)(2,1)S(1)} %get-tuple-element.27), channel_id=1, source_target_pairs={{0,1},{1,2},{2,3},{3,4},{4,5},{5,6},{6,7},{8,9},{9,10},{10,11},{11... | collective-permute-start | bytes 207368 | tf_op jit(solution)/shard_map/ppermute | solution.py:19
  95.7 7.8 %collective-permute-start.13 = (bf16[4,135,64]{2,1,0:T(8,128)(2,1)S(1)}, bf16[4,135,64]{2,1,0:T(8,128)(2,1)S(1)}, u32[]{:S(2)}, u32[]{:S(2)}) collective-permute-start(bf16[4,135,64]{2,1,0:T(8,128)(2,1)S(1)} %get-tuple-element.28), channel_id=1, source_target_pairs={{1,0},{2,1},{3,2},{4,3},{5,4},{6,5},{7,6},{9,8},{10,9},{11,10},{12... | collective-permute-start | bytes 207368 | tf_op jit(solution)/shard_map/ppermute | solution.py:21
  113.6 11.8 %collective-permute-start.14 = (bf16[4,135,64]{2,1,0:T(8,128)(2,1)S(1)}, bf16[4,135,64]{2,1,0:T(8,128)(2,1)S(1)}, u32[]{:S(2)}, u32[]{:S(2)}) collective-permute-start(bf16[4,135,64]{2,1,0:T(8,128)(2,1)S(1)} %get-tuple-element.25), channel_id=1, source_target_pairs={{0,1},{1,2},{2,3},{3,4},{4,5},{5,6},{6,7},{8,9},{9,10},{10,11},{11... | collective-permute-start | bytes 207368 | tf_op jit(solution)/shard_map/ppermute | solution.py:19
  116.5 8.9 %collective-permute-start.15 = (bf16[4,135,64]{2,1,0:T(8,128)(2,1)S(1)}, bf16[4,135,64]{2,1,0:T(8,128)(2,1)S(1)}, u32[]{:S(2)}, u32[]{:S(2)}) collective-permute-start(bf16[4,135,64]{2,1,0:T(8,128)(2,1)S(1)} %get-tuple-element.26), channel_id=1, source_target_pairs={{1,0},{2,1},{3,2},{4,3},{5,4},{6,5},{7,6},{9,8},{10,9},{11,10},{12... | collective-permute-start | bytes 207368 | tf_op jit(solution)/shard_map/ppermute | solution.py:21
  119.5 22.7 %collective-permute-start.2 = (bf16[1,135,64]{2,1,0:T(8,128)(2,1)S(1)}, bf16[1,135,64]{2,1,0:T(8,128)(2,1)S(1)}, u32[]{:S(2)}, u32[]{:S(2)}) collective-permute-start(bf16[1,135,64]{2,1,0:T(8,128)(2,1)S(1)} %get-tuple-element.105), channel_id=1, source_target_pairs={{0,1},{1,2},{2,3},{3,4},{4,5},{5,6},{6,7},{8,9},{9,10},{10,11},{11... | collective-permute-start | bytes 51848 | tf_op jit(solution)/shard_map/ppermute | solution.py:19
  123.3 19.0 %collective-permute-start.3 = (bf16[1,135,64]{2,1,0:T(8,128)(2,1)S(1)}, bf16[1,135,64]{2,1,0:T(8,128)(2,1)S(1)}, u32[]{:S(2)}, u32[]{:S(2)}) collective-permute-start(bf16[1,135,64]{2,1,0:T(8,128)(2,1)S(1)} %get-tuple-element.106), channel_id=1, source_target_pairs={{1,0},{2,1},{3,2},{4,3},{5,4},{6,5},{7,6},{9,8},{10,9},{11,10},{12... | collective-permute-start | bytes 51848 | tf_op jit(solution)/shard_map/ppermute | solution.py:21
  135.4 10.3 %collective-permute-start.16 = (bf16[4,135,64]{2,1,0:T(8,128)(2,1)S(1)}, bf16[4,135,64]{2,1,0:T(8,128)(2,1)S(1)}, u32[]{:S(2)}, u32[]{:S(2)}) collective-permute-start(bf16[4,135,64]{2,1,0:T(8,128)(2,1)S(1)} %get-tuple-element.23), channel_id=1, source_target_pairs={{0,1},{1,2},{2,3},{3,4},{4,5},{5,6},{6,7},{8,9},{9,10},{10,11},{11... | collective-permute-start | bytes 207368 | tf_op jit(solution)/shard_map/ppermute | solution.py:19
  140.1 7.8 %collective-permute-start.17 = (bf16[4,135,64]{2,1,0:T(8,128)(2,1)S(1)}, bf16[4,135,64]{2,1,0:T(8,128)(2,1)S(1)}, u32[]{:S(2)}, u32[]{:S(2)}) collective-permute-start(bf16[4,135,64]{2,1,0:T(8,128)(2,1)S(1)} %get-tuple-element.24), channel_id=1, source_target_pairs={{1,0},{2,1},{3,2},{4,3},{5,4},{6,5},{7,6},{9,8},{10,9},{11,10},{12... | collective-permute-start | bytes 207368 | tf_op jit(solution)/shard_map/ppermute | solution.py:21
  158.0 6.9 collective-permute-start.18
  160.6 7.8 %collective-permute-start.19 = (bf16[4,135,64]{2,1,0:T(8,128)(2,1)S(1)}, bf16[4,135,64]{2,1,0:T(8,128)(2,1)S(1)}, u32[]{:S(2)}, u32[]{:S(2)}) collective-permute-start(bf16[4,135,64]{2,1,0:T(8,128)(2,1)S(1)} %get-tuple-element.22), channel_id=1, source_target_pairs={{1,0},{2,1},{3,2},{4,3},{5,4},{6,5},{7,6},{9,8},{10,9},{11,10},{12... | collective-permute-start | bytes 207368 | tf_op jit(solution)/shard_map/ppermute | solution.py:21
  181.2 6.7 collective-permute-start.21
  195.4 6.7 collective-permute-start.23
  209.0 6.7 collective-permute-start.25
  223.1 6.7 collective-permute-start.27
  236.6 6.7 collective-permute-start.29
  250.0 6.7 collective-permute-start.31
  268.7 6.7 collective-permute-start.34
  282.2 6.7 collective-permute-start.36
  295.6 6.7 collective-permute-start.38
  309.0 6.7 collective-permute-start.40
  349.3 6.7 collective-permute-start.46
  475.4 6.7 collective-permute-start.65
  507.5 6.7 collective-permute-start.70
  520.9 6.7 collective-permute-start.72
  574.6 6.7 collective-permute-start.92
  588.1 6.8 collective-permute-start.94
  600.6 6.9 collective-permute-start.79
  602.5 7.8 %collective-permute-start.80 = (bf16[4,135,64]{2,1,0:T(8,128)(2,1)S(1)}, bf16[4,135,64]{2,1,0:T(8,128)(2,1)S(1)}, u32[]{:S(2)}, u32[]{:S(2)}) collective-permute-start(bf16[4,135,64]{2,1,0:T(8,128)(2,1)S(1)} %get-tuple-element.20), channel_id=1, source_target_pairs={{1,0},{2,1},{3,2},{4,3},{5,4},{6,5},{7,6},{9,8},{10,9},{11,10},{12... | collective-permute-start | bytes 207368 | tf_op jit(solution)/shard_map/ppermute | solution.py:21
  620.2 6.9 collective-permute-start.81
  622.1 7.8 %collective-permute-start.82 = (bf16[4,135,64]{2,1,0:T(8,128)(2,1)S(1)}, bf16[4,135,64]{2,1,0:T(8,128)(2,1)S(1)}, u32[]{:S(2)}, u32[]{:S(2)}) collective-permute-start(bf16[4,135,64]{2,1,0:T(8,128)(2,1)S(1)} %get-tuple-element.18), channel_id=1, source_target_pairs={{1,0},{2,1},{3,2},{4,3},{5,4},{6,5},{7,6},{9,8},{10,9},{11,10},{12... | collective-permute-start | bytes 207368 | tf_op jit(solution)/shard_map/ppermute | solution.py:21
  639.4 6.9 collective-permute-start.83
  641.3 7.9 %collective-permute-start.84 = (bf16[4,135,64]{2,1,0:T(8,128)(2,1)S(1)}, bf16[4,135,64]{2,1,0:T(8,128)(2,1)S(1)}, u32[]{:S(2)}, u32[]{:S(2)}) collective-permute-start(bf16[4,135,64]{2,1,0:T(8,128)(2,1)S(1)} %get-tuple-element.16), channel_id=1, source_target_pairs={{1,0},{2,1},{3,2},{4,3},{5,4},{6,5},{7,6},{9,8},{10,9},{11,10},{12... | collective-permute-start | bytes 207368 | tf_op jit(solution)/shard_map/ppermute | solution.py:21
  658.7 6.9 collective-permute-start.85
  660.7 8.2 %collective-permute-start.86 = (bf16[4,135,64]{2,1,0:T(8,128)(2,1)S(1)}, bf16[4,135,64]{2,1,0:T(8,128)(2,1)S(1)}, u32[]{:S(2)}, u32[]{:S(2)}) collective-permute-start(bf16[4,135,64]{2,1,0:T(8,128)(2,1)S(1)} %get-tuple-element.14), channel_id=1, source_target_pairs={{1,0},{2,1},{3,2},{4,3},{5,4},{6,5},{7,6},{9,8},{10,9},{11,10},{12... | collective-permute-start | bytes 207368 | tf_op jit(solution)/shard_map/ppermute | solution.py:21
  678.3 7.7 %collective-permute-start.87 = (bf16[4,135,64]{2,1,0:T(8,128)(2,1)S(1)}, bf16[4,135,64]{2,1,0:T(8,128)(2,1)S(1)}, u32[]{:S(2)}, u32[]{:S(2)}) collective-permute-start(bf16[4,135,64]{2,1,0:T(8,128)(2,1)S(1)} %get-tuple-element.10), channel_id=1, source_target_pairs={{0,1},{1,2},{2,3},{3,4},{4,5},{5,6},{6,7},{8,9},{9,10},{10,11},{11... | collective-permute-start | bytes 207368 | tf_op jit(solution)/shard_map/ppermute | solution.py:19
  682.5 8.6 %collective-permute-start.88 = (bf16[4,135,64]{2,1,0:T(8,128)(2,1)S(1)}, bf16[4,135,64]{2,1,0:T(8,128)(2,1)S(1)}, u32[]{:S(2)}, u32[]{:S(2)}) collective-permute-start(bf16[4,135,64]{2,1,0:T(8,128)(2,1)S(1)} %get-tuple-element.12), channel_id=1, source_target_pairs={{1,0},{2,1},{3,2},{4,3},{5,4},{6,5},{7,6},{9,8},{10,9},{11,10},{12... | collective-permute-start | bytes 207368 | tf_op jit(solution)/shard_map/ppermute | solution.py:21
  700.5 6.9 collective-permute-start.89
  703.8 7.8 %collective-permute-start.90 = (bf16[4,135,64]{2,1,0:T(8,128)(2,1)S(1)}, bf16[4,135,64]{2,1,0:T(8,128)(2,1)S(1)}, u32[]{:S(2)}, u32[]{:S(2)}) collective-permute-start(bf16[4,135,64]{2,1,0:T(8,128)(2,1)S(1)} %get-tuple-element.8), channel_id=1, source_target_pairs={{1,0},{2,1},{3,2},{4,3},{5,4},{6,5},{7,6},{9,8},{10,9},{11,10},{12... | collective-permute-start | bytes 207368 | tf_op jit(solution)/shard_map/ppermute | solution.py:21
  (70 other events, 478.7 us)
where the time goes:
time: 732 us; the launch traced here: 721 us
  starting transfers between devices  279 us (38%)
  local copies, waits for them, and re-layouts  232 us (32%)
  waiting for transfers between devices  143 us (20%)
  matrix products  39 us (5%)
  other arithmetic  23.2 us (3%)
    ppermute x46, starting transfers between devices, padded(): lax.ppermute(head, axis, [((i + 1) % count, i) for i in range(ends)])  163 us
    gather x60, local copies, waits for them, and re-layouts, neighbours(): gathered = jnp.take(extended, conn_flat, axis=2) * face_keep  158 us
    ppermute x46, waiting for transfers between devices, padded(): lax.ppermute(head, axis, [((i + 1) % count, i) for i in range(ends)])  122 us
    ppermute x46, starting transfers between devices, padded(): lax.ppermute(tail, axis, [(i, (i + 1) % count) for i in range(ends)])  110 us
    gather x91, local copies, waits for them, and re-layouts, neighbours(): outgoing = jnp.take(iterate, send_index, axis=2)  45.3 us
    dot_general x46, matrix products, propagate(): jnp.einsum('bij,njbk->nibk', chosen, blocked, preferred_element_type=jnp....  39 us
  transfers between devices with their start and end apart: 95, of which 58 were waited for; matrix products, arithmetic and copies ran while one was open for 4% of the time, Pallas kernels for 0%

commit v1 on v0

v1 whole, which is shorter than its diff:
```python
import functools

import jax
import jax.numpy as jnp
from jax import lax
from jax.experimental import pallas as pl
from jax.experimental.pallas import tpu as pltpu
from jax.sharding import PartitionSpec as P

PRISM = 90
SWEEPS = 2
COARSEN = 4
ROWS = 144
PROWS = 96
LANES = 128
BF = jnp.bfloat16
F32 = jnp.float32
VMEM = pl.BlockSpec(memory_space=pltpu.VMEM)
LIMIT = 56 * 1024 * 1024


def dot(a, b):
    return jnp.dot(a, b, preferred_element_type=F32)


def host_of(window, interval, space, intervals):
    stride = space // intervals
    return (interval * stride + (window % 2) % stride) % space


class Place:
    def __init__(self, space, intervals):
        stride = space // intervals
        self.window = lax.axis_index("tm")
        self.position = lax.axis_index("space")
        shifted = lax.rem(
            self.position - lax.rem(lax.rem(self.window, 2), stride) + space, space
        )
        self.active = lax.rem(shifted, stride) == 0
        self.interval = shifted // stride
        self.next_interval = lax.rem((shifted + stride - 1) // stride, intervals)
        self.number = self.window * intervals + self.interval


def over_pairs(parts, body):
    if parts <= 8:
        for pair in range(parts // 2):
            body(pair)
    else:

        @pl.loop(0, parts // 2)
        def _(pair):
            body(pair)


class Sweeper:
    def __init__(self, parts, faces, gather, listing, aux, outs, work):
        self.parts, self.faces = parts, faces
        self.gather, self.listing, self.aux = gather, listing, aux
        self.outs, self.work = outs, work

    def clear_rim(self):
        zero = jnp.zeros((ROWS, LANES), BF)
        self.outs[0] = zero
        self.outs[self.parts + 1] = zero

    def set_drive(self, state, decay_row, forcing=None):
        def body(pair):
            for side in range(2):
                part = 2 * pair + side
                drive = state[part].astype(F32) * self.aux[part, decay_row : decay_row + 1, :]
                if forcing is not None:
                    drive = drive + forcing(part).astype(F32)
                self.work[
                    pair, self.faces * ROWS :, side * LANES : (side + 1) * LANES
                ] = drive.astype(BF)

        over_pairs(self.parts, body)

    def sweep(self, source, target, table, extra=None):
        lane = lax.broadcasted_iota(jnp.int32, (ROWS, LANES), 1)

        def listed(pair):
            both = jnp.concatenate([source[2 * pair], source[2 * pair + 1]], axis=1)
            chosen = dot(both, self.listing[pair]).astype(BF)
            self.outs[2 * pair + 1] = chosen[:, :LANES]
            self.outs[2 * pair + 2] = chosen[:, LANES:]

        def gathered(pair):
            for side in range(2):
                part = 2 * pair + side
                rim = jnp.where(lane < LANES // 2, self.outs[part], self.outs[part + 2])
                extended = jnp.concatenate([source[part], rim], axis=1)
                found = dot(extended, self.gather[part]).astype(BF)
                for face in range(self.faces):
                    self.work[
                        pair,
                        face * ROWS : (face + 1) * ROWS,
                        side * LANES : (side + 1) * LANES,
                    ] = found[:, face * LANES : (face + 1) * LANES]

        def applied(pair):
            both = dot(table[...], self.work[pair])
            for side in range(2):
                part = 2 * pair + side
                result = both[:, side * LANES : (side + 1) * LANES]
                prism = jnp.concatenate(
                    [result[ROWS:], jnp.zeros((ROWS - PROWS, LANES), F32)], axis=0
                )
                kind = self.aux[part, 0:1, :]
                value = jnp.where(kind == 0.0, result[:ROWS], prism)
                if extra is not None:
                    value = value + extra[part].astype(F32)
                target[part] = value.astype(BF)

        over_pairs(self.parts, listed)
        over_pairs(self.parts, gathered)
        over_pairs(self.parts, applied)

    def step(self, state, other, table, decay_row, forcing=None, extra=None):
        self.set_drive(state, decay_row, forcing)
        places = [state, other]
        for turn in range(SWEEPS):
            last = turn + 1 == SWEEPS
            self.sweep(
                places[turn % 2], places[(turn + 1) % 2], table, extra if last else None
            )


def pack_kernel(space, intervals, forcing, initial, meta, *messages):
    place = Place(space, intervals)
    width = initial.shape[0]
    for turn in range(intervals):
        interval = lax.rem(place.next_interval + turn, intervals)
        out = messages[turn]
        for index in range(COARSEN):
            out[index, :width] = forcing[interval * COARSEN + index]
        out[COARSEN, :width] = initial[...]
        out[0, width : width + 8] = meta[0:8]
        out[1, width : width + 3] = meta[8:11]


def fine_kernel(space, intervals, width, faces, *refs):
    messages = refs[:space]
    table, residual, gather, listing, aux, forcing, start = refs[space : space + 7]
    other, outs, work = refs[space + 7 :]
    place = Place(space, intervals)

    @pl.when(place.active)
    def _():
        sweeper = Sweeper(space, faces, gather, listing, aux, outs, work)
        sweeper.clear_rim()
        rows = lax.broadcasted_iota(jnp.int32, (ROWS, LANES), 0).astype(F32)
        full = lax.broadcasted_iota(jnp.int32, (2 * LANES, LANES), 0).astype(F32)
        half = full[:LANES]
        zero = jnp.zeros((LANES, LANES), BF)
        for turn in range(space):
            part = lax.rem(place.position - turn + space, space)
            message = messages[turn]
            for index in range(COARSEN):
                forcing[part, index] = message[index]
            first = message[0, width : width + 8].astype(F32)
            second = message[1, width : width + 3].astype(F32)
            kind = first[6:7]
            damping = (second[0:1] + second[1:2]) + second[2:3]
            aux[part] = jnp.concatenate(
                [
                    kind,
                    jnp.exp(-damping),
                    jnp.exp(-COARSEN * damping),
                    jnp.zeros((5, LANES), F32),
                ],
                axis=0,
            )
            for face in range(faces):
                found = full == first[face : face + 1]
                if face == faces - 1:
                    found = found & (kind == 0.0)
                gather[part, :, face * LANES : (face + 1) * LANES] = jnp.where(
                    found, 1.0, 0.0
                ).astype(BF)
            picks = jnp.where(half == first[7:8], 1.0, 0.0).astype(BF)
            odd = lax.rem(part, 2) == 1
            left = jnp.where(odd, 0.0, 1.0).astype(BF)
            right = jnp.where(odd, 1.0, 0.0).astype(BF)
            listing[part // 2, pl.ds(pl.multiple_of(lax.rem(part, 2) * LANES, LANES), LANES), :] = (
                jnp.concatenate([picks * left, picks * right], axis=1)
            )
            limit = jnp.where(kind == 0.0, float(width), float(PRISM))
            wanted = (rows < limit) & (place.number == 0)
            start[part] = jnp.where(wanted, message[COARSEN].astype(F32), 0.0).astype(BF)

        residual[...] = start[...]

        @pl.loop(0, COARSEN)
        def _(index):
            sweeper.step(residual, other, table, 1, lambda part: forcing[part, index])


def chain_kernel(space, intervals, faces, powers, count, *refs):
    terms = refs[:count]
    table, gather, listing, aux, result, other, outs, work = refs[count:]
    place = Place(space, intervals)

    @pl.when(place.active)
    def _():
        sweeper = Sweeper(space, faces, gather, listing, aux, outs, work)
        sweeper.clear_rim()
        result[...] = terms[0][...]
        for index in range(1, count):
            if powers > 1:

                @pl.loop(0, powers - 1)
                def _(turn):
                    sweeper.step(result, other, table, 2)

            sweeper.step(result, other, table, 2, extra=terms[index])


def final_kernel(space, intervals, width, faces, *refs):
    before, residual, start, forcing = refs[:4]
    fine_table, coarse_table, gather, listing, aux = refs[4:9]
    pieces = refs[9 : 9 + space]
    states, other, outs, work = refs[9 + space :]
    place = Place(space, intervals)

    @pl.when(place.active)
    def _():
        sweeper = Sweeper(space, faces, gather, listing, aux, outs, work)
        sweeper.clear_rim()
        last = COARSEN - 1
        state = states.at[last]
        state[...] = before[...]
        sweeper.step(state, other, coarse_table, 2, extra=residual)
        first = place.number == 0
        states[0] = jnp.where(first, start[...], before[...])

        @pl.loop(0, last)
        def _(index):
            now = states.at[index]
            sweeper.step(now, other, fine_table, 1, lambda part: forcing[part, index])

            @pl.when(index + 1 < last)
            def _():
                states[index + 1] = now[...]

        for turn in range(space):
            part = lax.rem(place.position + turn, space)
            for index in range(COARSEN):
                pieces[turn][index] = states[index, part][:width]


def gather_kernel(space, intervals, *refs):
    pieces = refs[:space]
    out, sem = refs[space:]
    stride = space // intervals
    place = Place(space, intervals)
    offset = lax.rem(lax.rem(place.window, 2), stride)
    for interval in range(intervals):
        wanted = lax.rem(place.position - offset - interval * stride + 2 * space, space)
        for turn in range(space):

            @pl.when(wanted == turn)
            def _():
                pltpu.make_async_copy(
                    pieces[turn], out.at[pl.ds(interval * COARSEN, COARSEN)], sem.at[interval]
                ).start()

    for interval in range(intervals):
        pltpu.make_async_copy(
            pieces[0], out.at[pl.ds(interval * COARSEN, COARSEN)], sem.at[interval]
        ).wait()


def folded(inverse, coupling):
    width = inverse.shape[-1]
    faces = coupling.shape[0]
    products = -jnp.einsum("kij,fjl->kifl", inverse, coupling, preferred_element_type=F32)
    every = jnp.concatenate([products.astype(BF), inverse[:, :, None, :]], axis=2)
    every = jnp.pad(every, ((0, 0), (0, 0), (0, 0), (0, ROWS - width)))
    every = every.reshape(2, width, (faces + 1) * ROWS)
    return jnp.concatenate(
        [
            jnp.pad(every[0], ((0, ROWS - width), (0, 0))),
            jnp.pad(every[1, :PRISM], ((0, PROWS - PRISM), (0, 0))),
        ],
        axis=0,
    )


def shards(initial, forcing, damping, block_inv, coarse_inv, coupling, etype, send_index, conn):
    width, elems = initial.shape
    faces = conn.shape[0]
    steps = forcing.shape[0]
    intervals = steps // COARSEN
    space = lax.axis_size("space")
    windows = lax.axis_size("tm")
    stride = space // intervals
    halo = send_index.shape[0] // 2
    params = pltpu.CompilerParams(vmem_limit_bytes=LIMIT)
    state_shape = jax.ShapeDtypeStruct((space, ROWS, LANES), BF)

    kinds = jnp.broadcast_to(etype[:, None], (etype.shape[0], elems // etype.shape[0]))
    lists = jnp.concatenate([send_index[halo:], send_index[:halo]])
    high = lax.reduce_precision(damping, 8, 7)
    middle = lax.reduce_precision(damping - high, 8, 7)
    low = (damping - high) - middle
    meta = jnp.concatenate(
        [
            conn.astype(F32),
            kinds.reshape(1, elems).astype(F32),
            lists[None].astype(F32),
            high[None],
            middle[None],
            low[None],
            jnp.zeros((16 - faces - 5, elems), F32),
        ],
        axis=0,
    ).astype(BF)

    message_shape = jax.ShapeDtypeStruct((COARSEN + 1, ROWS, LANES), BF)
    messages = pl.pallas_call(
        functools.partial(pack_kernel, space, intervals),
        out_shape=[message_shape] * intervals,
        in_specs=[VMEM] * 3,
        out_specs=[VMEM] * intervals,
        compiler_params=params,
        name="pack",
    )(forcing, initial, meta)

    received = [messages[0]]
    for turn in range(1, space):
        pairs = []
        for window in range(windows):
            for interval in range(intervals):
                host = host_of(window, interval, space, intervals)
                source = (host - turn) % space
                pairs.append((window * space + source, window * space + host))
        received.append(lax.ppermute(messages[turn // stride], ("tm", "space"), pairs))

    fine_table = folded(block_inv, coupling)
    coarse_table = folded(coarse_inv, coupling)

    gather_shape = jax.ShapeDtypeStruct((space, 2 * LANES, faces * LANES), BF)
    listing_shape = jax.ShapeDtypeStruct((space // 2, 2 * LANES, 2 * LANES), BF)
    aux_shape = jax.ShapeDtypeStruct((space, 8, LANES), F32)
    forcing_shape = jax.ShapeDtypeStruct((space, COARSEN, ROWS, LANES), BF)
    scratch = [
        pltpu.VMEM((space, ROWS, LANES), BF),
        pltpu.VMEM((space + 2, ROWS, LANES), BF),
        pltpu.VMEM((space // 2, (faces + 1) * ROWS, 2 * LANES), BF),
    ]
    residual, gather, listing, aux, whole_forcing, start = pl.pallas_call(
        functools.partial(fine_kernel, space, intervals, width, faces),
        out_shape=[state_shape, gather_shape, listing_shape, aux_shape, forcing_shape, state_shape],
        in_specs=[VMEM] * (space + 1),
        out_specs=[VMEM] * 6,
        scratch_shapes=scratch,
        compiler_params=params,
        name="fine",
    )(*received, fine_table)

    def from_earlier(value, by):
        pairs = []
        for number in range(by, windows * intervals):
            target = number // intervals
            source = (number - by) // intervals
            pairs.append(
                (
                    source * space + host_of(source, (number - by) % intervals, space, intervals),
                    target * space + host_of(target, number % intervals, space, intervals),
                )
            )
        return lax.ppermute(value, ("tm", "space"), pairs)

    def chain(terms, powers, name):
        return pl.pallas_call(
            functools.partial(chain_kernel, space, intervals, faces, powers, len(terms)),
            out_shape=state_shape,
            in_specs=[VMEM] * (len(terms) + 4),
            out_specs=VMEM,
            scratch_shapes=scratch,
            compiler_params=params,
            name=name,
        )(*terms, coarse_table, gather, listing, aux)

    near = [from_earlier(residual, by) for by in range(intervals, 0, -1)]
    partial = chain(near, 1, "near")
    far = [from_earlier(partial, by * intervals) for by in range(windows - 1, 0, -1)]
    before = chain(far + [partial], intervals, "far")

    piece_shape = jax.ShapeDtypeStruct((COARSEN, width, LANES), BF)
    pieces = pl.pallas_call(
        functools.partial(final_kernel, space, intervals, width, faces),
        out_shape=[piece_shape] * space,
        in_specs=[VMEM] * 9,
        out_specs=[VMEM] * space,
        scratch_shapes=[pltpu.VMEM((COARSEN, space, ROWS, LANES), BF)] + scratch,
        compiler_params=params,
        name="final",
    )(before, residual, start, whole_forcing, fine_table, coarse_table, gather, listing, aux)

    returned = [pieces[0]]
    for turn in range(1, space):
        pairs = []
        for window in range(windows):
            for interval in range(intervals):
                host = host_of(window, interval, space, intervals)
                pairs.append((window * space + host, window * space + (host + turn) % space))
        returned.append(lax.ppermute(pieces[turn], ("tm", "space"), pairs))

    return pl.pallas_call(
        functools.partial(gather_kernel, space, intervals),
        out_shape=jax.ShapeDtypeStruct(forcing.shape, BF),
        in_specs=[pl.BlockSpec(memory_space=pl.ANY)] * space,
        out_specs=pl.BlockSpec(memory_space=pl.ANY),
        scratch_shapes=[pltpu.SemaphoreType.DMA((intervals,))],
        compiler_params=params,
        name="place",
    )(*returned)


def solution(mesh):
    in_specs = (
        P(None, "space"),
        P("tm", None, "space"),
        P("space"),
        P(),
        P(),
        P(),
        P("space"),
        P("space"),
        P(None, "space"),
    )
    out_specs = P("tm", None, "space")
    return jax.shard_map(shards, mesh=mesh, in_specs=in_specs, out_specs=out_specs, check_vma=False)
```

time: 732 us -> 191 us (0.26); the launches traced: 721 us -> 188 us
  starting transfers between devices: 279 us -> 31.6 us
  local copies, waits for them, and re-layouts: 232 us -> 18.2 us
  waiting for transfers between devices: 143 us -> 97.8 us
  matrix products: 39 us -> 0.73 us
  Pallas kernels: 0 us -> 34.4 us
  other arithmetic: 23.2 us -> 4.47 us
    ppermute x95 -> x21, starting transfers between devices: 279 us -> 31.6 us  [the longest x7 19.7 us: shards(): lax.ppermute(messages[turn // stride], ('tm', 'space'), pairs)]
    gather x151 -> x0, local copies, waits for them, and re-layouts: 204 us -> none  [the longest x60 158 us: neighbours(): gathered = jnp.take(extended, conn_flat, axis=2) * face_keep]
    ppermute x95 -> x21, waiting for transfers between devices: 143 us -> 97.8 us  [the longest x7 97.7 us: shards(): returned.append(lax.ppermute(pieces[turn], ('tm', 'space'), pairs))]
    dot_general x46 -> x2, matrix products: 39 us -> 0.73 us  [folded(): jnp.einsum('kij,fjl->kifl', inverse, coupling, preferred_element_type=F32)]
    pallas_call x0 -> x6, Pallas kernels: none -> 34.4 us  [the longest x1 18 us: shards(): pl.pallas_call(functools.partial(gather_kernel, space, intervals), out_sh...]
    mul x46 -> x0, other arithmetic: 14.1 us -> none  [neighbours(): gathered = jnp.take(extended, conn_flat, axis=2) * face_keep]
  transfers between devices with their start and end apart: 95 -> 21, of which waited for: 58 -> 4; matrix products, arithmetic and copies ran while one was open for 4% -> 7% of each run, Pallas kernels for 0% -> 0%
where the time goes in v1:
time: 191 us; the launch traced here: 188 us
  waiting for transfers between devices  97.8 us (51%)
  Pallas kernels  34.4 us (18%)
  starting transfers between devices  31.6 us (17%)
  local copies, waits for them, and re-layouts  18.2 us (10%)
  other arithmetic  4.47 us (2%)
    ppermute x7, waiting for transfers between devices, shards(): returned.append(lax.ppermute(pieces[turn], ('tm', 'space'), pairs))  97.7 us
    ppermute x7, starting transfers between devices, shards(): lax.ppermute(messages[turn // stride], ('tm', 'space'), pairs)  19.7 us
    pallas_call x1, Pallas kernels, shards(): pl.pallas_call(functools.partial(gather_kernel, space, intervals), out_sh...  18 us
    ppermute x7, starting transfers between devices, shards(): returned.append(lax.ppermute(pieces[turn], ('tm', 'space'), pairs))  7.15 us
    unnamed x39, local copies, waits for them, and re-layouts  6.71 us
    pallas_call x2, Pallas kernels, chain(): pl.pallas_call(functools.partial(chain_kernel, space, intervals, faces, p...  6.43 us
    ppermute x7, starting transfers between devices, from_earlier(): return lax.ppermute(value, ('tm', 'space'), pairs)  4.73 us
    pallas_call x1, Pallas kernels, shards(): pl.pallas_call(functools.partial(final_kernel, space, intervals, width, f...  4.01 us
  transfers between devices with their start and end apart: 21, of which 4 were waited for; matrix products, arithmetic and copies ran while one was open for 7% of the time, Pallas kernels for 0%

profile of v1, /device:TPU:6, one launch (start us, length us, event | category | flops | bytes accessed | tf_op | source)
XLA Modules:
  0.0 188.4 jit_solution(5726818599653780560)
XLA Ops:
  0.7 0.8 slice_bitcast_fusion.3
  1.5 0.7 fusion.19
  2.2 0.7 convert_convert_fusion
  2.9 2.0 %copy.20.forcing = bf16[16,135,128]{2,1,0:T(8,128)(2,1)} copy(bf16[16,135,128]{2,0,1:T(8,128)(2,1)} %param.10) | data formatting | bytes 1105920 | tf_op args[1]
  5.0 1.2 concatenate.33.meta
  6.2 2.0 %pack.1 = (bf16[5,144,128]{2,1,0:T(8,128)(2,1)}, bf16[5,144,128]{2,1,0:T(8,128)(2,1)}, bf16[5,144,128]{2,1,0:T(8,128)(2,1)}, bf16[5,144,128]{2,1,0:T(8,128)(2,1)}) custom-call(bf16[16,135,128]{2,1,0:T(8,128)(2,1)} %copy.20.forcing, bf16[135,128]{1,0:T(8,128)(2,1)} %initial.1, bf16[16,128]{1,0:T(8,128)(2,1)} %concatenate.33.meta), custom_call_target="tpu_custom_call" | custom-call | tf_op jit(solution)/shard_map/pack/pallas_call | solution.py:322
  8.2 5.1 %collective-permute-start.2 = (bf16[5,144,128]{2,1,0:T(8,128)(2,1)}, bf16[5,144,128]{2,1,0:T(8,128)(2,1)}, u32[]{:S(2)}, u32[]{:S(2)}) collective-permute-start(bf16[5,144,128]{2,1,0:T(8,128)(2,1)} %get-tuple-element.24), channel_id=1, source_target_pairs={{5,0},{7,2},{1,4},{3,6},{14,9},{8,11},{10,13},{12,15},{21,16},{23,... | collective-permute-start | bytes 552968 | tf_op jit(solution)/shard_map/ppermute | solution.py:339
  13.3 1.3 collective-permute-start.1
  14.6 3.1 %collective-permute-start.4 = (bf16[5,144,128]{2,1,0:T(8,128)(2,1)}, bf16[5,144,128]{2,1,0:T(8,128)(2,1)}, u32[]{:S(2)}, u32[]{:S(2)}) collective-permute-start(bf16[5,144,128]{2,1,0:T(8,128)(2,1)} %get-tuple-element.25), channel_id=1, source_target_pairs={{3,0},{5,2},{7,4},{1,6},{12,9},{14,11},{8,13},{10,15},{19,16},{21,... | collective-permute-start | bytes 552968 | tf_op jit(solution)/shard_map/ppermute | solution.py:339
  17.7 1.3 collective-permute-start.3
  19.0 2.5 %collective-permute-start = (bf16[5,144,128]{2,1,0:T(8,128)(2,1)}, bf16[5,144,128]{2,1,0:T(8,128)(2,1)}, u32[]{:S(2)}, u32[]{:S(2)}) collective-permute-start(bf16[5,144,128]{2,1,0:T(8,128)(2,1)} %get-tuple-element.23.refs_0_), channel_id=1, source_target_pairs={{7,0},{1,2},{3,4},{5,6},{8,9},{10,11},{12,13},{14,15},{23,16},{17,... | collective-permute-start | bytes 552968 | tf_op jit(solution)/shard_map/ppermute | solution.py:339
  21.5 0.9 copy.43
  22.5 0.7 copy.42
  24.4 2.0 %reshape.42 = bf16[2,135,1008]{2,1,0:T(8,128)(2,1)} reshape(bf16[2,135,7,144]{3,2,1,0:T(8,128)(2,1)S(1)} %copy.24) | data formatting | bytes 1088640 | tf_op jit(solution)/shard_map/reshape | solution.py:281
  26.4 0.9 slice_bitcast_fusion.1
  27.3 5.0 %collective-permute-start.6 = (bf16[5,144,128]{2,1,0:T(8,128)(2,1)}, bf16[5,144,128]{2,1,0:T(8,128)(2,1)}, u32[]{:S(2)}, u32[]{:S(2)}) collective-permute-start(bf16[5,144,128]{2,1,0:T(8,128)(2,1)} %get-tuple-element.26), channel_id=1, source_target_pairs={{1,0},{3,2},{5,4},{7,6},{10,9},{12,11},{14,13},{8,15},{17,16},{19,... | collective-permute-start | bytes 552968 | tf_op jit(solution)/shard_map/ppermute | solution.py:339
  32.4 1.3 collective-permute-start.5
  33.7 1.1 fusion.9
  35.7 2.0 %reshape.43 = bf16[2,135,1008]{2,1,0:T(8,128)(2,1)} reshape(bf16[2,135,7,144]{3,2,1,0:T(8,128)(2,1)S(1)} %copy.28) | data formatting | bytes 1088640 | tf_op jit(solution)/shard_map/reshape | solution.py:281
  38.3 0.8 fusion.10.refs_8_.refs_4_
  39.2 4.0 %fine.1 = (bf16[8,144,128]{2,1,0:T(8,128)(2,1)}, bf16[8,256,768]{2,1,0:T(8,128)(2,1)}, bf16[4,256,256]{2,1,0:T(8,128)(2,1)}, f32[8,8,128]{2,1,0:T(8,128)}, bf16[...) custom-call(bf16[5,144,128]{2,1,0:T(8,128)(2,1)} %get-tuple-element.23.refs_0_, ...), custom_call_target="tpu_custom_call" | custom-call | tf_op jit(solution)/shard_map/fine/pallas_call | solution.py:353
  43.2 0.7 collective-permute-start.10
  43.9 0.7 collective-permute-start.9
  44.6 0.7 collective-permute-start.8
  45.3 0.7 collective-permute-start.7
  46.0 0.9 slice_bitcast_fusion
  46.9 0.8 fusion.11.refs_4_.refs_5_
  47.8 0.7 copy-done.4
  48.8 3.2 %near.1.refs_3_ = bf16[8,144,128]{2,1,0:T(8,128)(2,1)} custom-call(bf16[8,144,128]{2,1,0:T(8,128)(2,1)} %copy-done.7, bf16[8,144,128]{2,1,0:T(8,128)(2,1)} %copy-done.6, bf16[8,144,128]{2,1,0:T(8,128)(2,1)} %copy-done.5, bf16[8,144,128]{2,1,0:T(8,128)(2,1)} %copy-done.4, bf16[240,1008]{1,0:T(8,128)(2,1)} %fusion.11.refs_4_.refs_5_, ...), custom_call_target="tpu_custom_call" | custom-call | tf_op jit(solution)/shard_map/near/pallas_call | solution.py:377
  52.0 0.7 collective-permute-start.13
  52.7 0.7 collective-permute-start.12
  53.4 0.7 collective-permute-start.11
  54.1 0.7 copy-done.8
  54.9 0.7 copy-done.10
  55.6 3.2 %far.1.refs_0_ = bf16[8,144,128]{2,1,0:T(8,128)(2,1)} custom-call(bf16[8,144,128]{2,1,0:T(8,128)(2,1)} %copy-done.10, bf16[8,144,128]{2,1,0:T(8,128)(2,1)} %copy-done.9, bf16[8,144,128]{2,1,0:T(8,128)(2,1)} %copy-done.8, bf16[8,144,128]{2,1,0:T(8,128)(2,1)} %near.1.refs_3_, bf16[240,1008]{1,0:T(8,128)(2,1)} %fusion.11.refs_4_.refs_5_, ...), custom_call_target="tpu_custom_call" | custom-call | tf_op jit(solution)/shard_map/far/pallas_call | solution.py:377
  58.8 4.0 %final.1 = (bf16[4,135,128]{2,1,0:T(8,128)(2,1)}, bf16[4,135,128]{2,1,0:T(8,128)(2,1)}, bf16[4,135,128]{2,1,0:T(8,128)(2,1)}, bf16[4,135,128]{2,1,0:T(8,128)(2,1...) custom-call(bf16[8,144,128]{2,1,0:T(8,128)(2,1)} %far.1.refs_0_, ...), custom_call_target="tpu_custom_call" | custom-call | tf_op jit(solution)/shard_map/final/pallas_call | solution.py:393
  62.8 1.3 collective-permute-start.14
  64.1 0.7 collective-permute-start.15
  64.8 1.3 collective-permute-start.16
  66.1 0.7 collective-permute-start.17
  66.7 1.3 collective-permute-start.18
  68.0 84.1 %collective-permute-done.14.refs_1_ = bf16[4,135,128]{2,1,0:T(8,128)(2,1)S(1)} collective-permute-done((bf16[4,135,128]{2,1,0:T(8,128)(2,1)}, bf16[4,135,128]{2,1,0:T(8,128)(2,1)S(1)}, u32[]{:S(2)}, u32[]{:S(2)}) %collective-permute-start.14) | collective-permute-done | bytes 138272 | tf_op jit(solution)/shard_map/ppermute | solution.py:410
  152.8 1.3 collective-permute-start.20
  154.1 4.7 %collective-permute-done.16.refs_3_ = bf16[4,135,128]{2,1,0:T(8,128)(2,1)S(1)} collective-permute-done((bf16[4,135,128]{2,1,0:T(8,128)(2,1)}, bf16[4,135,128]{2,1,0:T(8,128)(2,1)S(1)}, u32[]{:S(2)}, u32[]{:S(2)}) %collective-permute-start.16) | collective-permute-done | bytes 138272 | tf_op jit(solution)/shard_map/ppermute | solution.py:410
  158.9 6.0 %collective-permute-done.18.refs_5_ = bf16[4,135,128]{2,1,0:T(8,128)(2,1)S(1)} collective-permute-done((bf16[4,135,128]{2,1,0:T(8,128)(2,1)}, bf16[4,135,128]{2,1,0:T(8,128)(2,1)S(1)}, u32[]{:S(2)}, u32[]{:S(2)}) %collective-permute-start.18) | collective-permute-done | bytes 138272 | tf_op jit(solution)/shard_map/ppermute | solution.py:410
  164.9 2.9 %collective-permute-done.20.refs_7_ = bf16[4,135,128]{2,1,0:T(8,128)(2,1)S(1)} collective-permute-done((bf16[4,135,128]{2,1,0:T(8,128)(2,1)}, bf16[4,135,128]{2,1,0:T(8,128)(2,1)S(1)}, u32[]{:S(2)}, u32[]{:S(2)}) %collective-permute-start.20) | collective-permute-done | bytes 138272 | tf_op jit(solution)/shard_map/ppermute | solution.py:410
  168.4 18.0 %place.1 = bf16[16,135,128]{2,1,0:T(8,128)(2,1)} custom-call(bf16[4,135,128]{2,1,0:T(8,128)(2,1)} %get-tuple-element.33.refs_0_, bf16[4,135,128]{2,1,0:T(8,128)(2,1)} %copy-done.11, bf16[4,135,128]{2,1,0:T(8,128)(2,1)} %copy-done.12, bf16[4,135,128]{2,1,0:T(8,128)(2,1)} %copy-done.13, bf16[4,135,128]{2,1,0:T(8,128)(2,1)} %copy-done.14, ...), custom_call_target="tpu_custom_call" | custom-call | tf_op jit(solution)/shard_map/place/pallas_call | solution.py:412
  186.5 1.9 %copy.29 = bf16[16,135,128]{2,0,1:T(8,128)(2,1)} copy(bf16[16,135,128]{2,1,0:T(8,128)(2,1)} %place.1) | data formatting | bytes 1105920 | tf_op jit(solution)/shard_map/place/pallas_call | solution.py:412
  (66 shorter events, 4.5 us)
Async XLA Ops:
  0.0 23.1 %copy-start = (bf16[6,135,135]{2,1,0:T(8,128)(2,1)S(1)}, bf16[6,135,135]{2,1,0:T(8,128)(2,1)}, u32[]{:S(2)}) copy-start(bf16[6,135,135]{2,1,0:T(8,128)(2,1)} %param.14) | copy-start | bytes 656104
  0.0 23.5 %copy-start.3 = (bf16[2,135,135]{2,0,1:T(2,128)(2,1)S(1)}, bf16[2,135,135]{2,0,1:T(2,128)(2,1)}, u32[]{:S(2)}) copy-start(bf16[2,135,135]{2,0,1:T(2,128)(2,1)} %param.12) | copy-start | bytes 218704
  0.0 22.4 %copy-start.2 = (bf16[2,135,135]{2,0,1:T(2,128)(2,1)S(1)}, bf16[2,135,135]{2,0,1:T(2,128)(2,1)}, u32[]{:S(2)}) copy-start(bf16[2,135,135]{2,0,1:T(2,128)(2,1)} %param.13) | copy-start | bytes 218704
  8.2 24.2 %collective-permute-start.2 = (bf16[5,144,128]{2,1,0:T(8,128)(2,1)}, bf16[5,144,128]{2,1,0:T(8,128)(2,1)}, u32[]{:S(2)}, u32[]{:S(2)}) collective-permute-start(bf16[5,144,128]{2,1,0:T(8,128)(2,1)} %get-tuple-element.24), channel_id=1, source_target_pairs={{5,0},{7,2},{1,4},{3,6},{14,9},{8,11},{10,13},{12,15},{21,16},{23,... | collective-permute-start | bytes 552968 | tf_op jit(solution)/shard_map/ppermute | solution.py:339
  13.3 25.9 %collective-permute-start.1 = (bf16[5,144,128]{2,1,0:T(8,128)(2,1)}, bf16[5,144,128]{2,1,0:T(8,128)(2,1)}, u32[]{:S(2)}, u32[]{:S(2)}) collective-permute-start(bf16[5,144,128]{2,1,0:T(8,128)(2,1)} %get-tuple-element.24), channel_id=1, source_target_pairs={{6,0},{0,2},{2,4},{4,6},{15,9},{9,11},{11,13},{13,15},{22,16},{16,... | collective-permute-start | bytes 552968 | tf_op jit(solution)/shard_map/ppermute | solution.py:339
  14.6 24.6 %collective-permute-start.4 = (bf16[5,144,128]{2,1,0:T(8,128)(2,1)}, bf16[5,144,128]{2,1,0:T(8,128)(2,1)}, u32[]{:S(2)}, u32[]{:S(2)}) collective-permute-start(bf16[5,144,128]{2,1,0:T(8,128)(2,1)} %get-tuple-element.25), channel_id=1, source_target_pairs={{3,0},{5,2},{7,4},{1,6},{12,9},{14,11},{8,13},{10,15},{19,16},{21,... | collective-permute-start | bytes 552968 | tf_op jit(solution)/shard_map/ppermute | solution.py:339
  17.7 21.5 %collective-permute-start.3 = (bf16[5,144,128]{2,1,0:T(8,128)(2,1)}, bf16[5,144,128]{2,1,0:T(8,128)(2,1)}, u32[]{:S(2)}, u32[]{:S(2)}) collective-permute-start(bf16[5,144,128]{2,1,0:T(8,128)(2,1)} %get-tuple-element.25), channel_id=1, source_target_pairs={{4,0},{6,2},{0,4},{2,6},{13,9},{15,11},{9,13},{11,15},{20,16},{22,... | collective-permute-start | bytes 552968 | tf_op jit(solution)/shard_map/ppermute | solution.py:339
  19.0 8.3 %collective-permute-start = (bf16[5,144,128]{2,1,0:T(8,128)(2,1)}, bf16[5,144,128]{2,1,0:T(8,128)(2,1)}, u32[]{:S(2)}, u32[]{:S(2)}) collective-permute-start(bf16[5,144,128]{2,1,0:T(8,128)(2,1)} %get-tuple-element.23.refs_0_), channel_id=1, source_target_pairs={{7,0},{1,2},{3,4},{5,6},{8,9},{10,11},{12,13},{14,15},{23,16},{17,... | collective-permute-start | bytes 552968 | tf_op jit(solution)/shard_map/ppermute | solution.py:339
  24.1 11.0 %copy-start.1 = (bf16[2,135,7,144]{3,1,2,0:T(8,128)(2,1)}, bf16[2,135,7,144]{3,1,2,0:T(8,128)(2,1)S(1)}, u32[]{:S(2)}) copy-start(bf16[2,135,7,144]{3,1,2,0:T(8,128)(2,1)S(1)} %fusion.8) | copy-start | bytes 1632964
  27.3 11.9 %collective-permute-start.6 = (bf16[5,144,128]{2,1,0:T(8,128)(2,1)}, bf16[5,144,128]{2,1,0:T(8,128)(2,1)}, u32[]{:S(2)}, u32[]{:S(2)}) collective-permute-start(bf16[5,144,128]{2,1,0:T(8,128)(2,1)} %get-tuple-element.26), channel_id=1, source_target_pairs={{1,0},{3,2},{5,4},{7,6},{10,9},{12,11},{14,13},{8,15},{17,16},{19,... | collective-permute-start | bytes 552968 | tf_op jit(solution)/shard_map/ppermute | solution.py:339
  32.4 6.8 %collective-permute-start.5 = (bf16[5,144,128]{2,1,0:T(8,128)(2,1)}, bf16[5,144,128]{2,1,0:T(8,128)(2,1)}, u32[]{:S(2)}, u32[]{:S(2)}) collective-permute-start(bf16[5,144,128]{2,1,0:T(8,128)(2,1)} %get-tuple-element.26), channel_id=1, source_target_pairs={{2,0},{4,2},{6,4},{0,6},{11,9},{13,11},{15,13},{9,15},{18,16},{20,... | collective-permute-start | bytes 552968 | tf_op jit(solution)/shard_map/ppermute | solution.py:339
  35.1 2.6 %slice-start = ((bf16[2,135,7,144]{3,1,2,0:T(8,128)(2,1)}), bf16[1,135,7,144]{3,1,2,0:T(8,128)(2,1)S(1)}, s32[]{:S(2)}) async-start(bf16[2,135,7,144]{3,1,2,0:T(8,128)(2,1)} %copy-done.1), calls=%async_computation | async-start | bytes 974848 | tf_op jit(solution)/shard_map/slice | solution.py:284
  43.2 4.5 %collective-permute-start.10 = (bf16[8,144,128]{2,1,0:T(8,128)(2,1)}, bf16[8,144,128]{2,1,0:T(8,128)(2,1)S(1)}, u32[]{:S(2)}, u32[]{:S(2)}) collective-permute-start(bf16[8,144,128]{2,1,0:T(8,128)(2,1)} %get-tuple-element.27.refs_1_), channel_id=1, source_target_pairs={{0,2},{2,4},{4,6},{6,9},{9,11},{11,13},{13,15},{15,16},{16,18},{18... | collective-permute-start | bytes 884744 | tf_op jit(solution)/shard_map/ppermute | solution.py:374
  43.9 3.8 %collective-permute-start.9 = (bf16[8,144,128]{2,1,0:T(8,128)(2,1)}, bf16[8,144,128]{2,1,0:T(8,128)(2,1)S(1)}, u32[]{:S(2)}, u32[]{:S(2)}) collective-permute-start(bf16[8,144,128]{2,1,0:T(8,128)(2,1)} %get-tuple-element.27.refs_1_), channel_id=1, source_target_pairs={{0,4},{2,6},{4,9},{6,11},{9,13},{11,15},{13,16},{15,18},{16,20},{1... | collective-permute-start | bytes 884744 | tf_op jit(solution)/shard_map/ppermute | solution.py:374
  44.6 3.2 %collective-permute-start.8 = (bf16[8,144,128]{2,1,0:T(8,128)(2,1)}, bf16[8,144,128]{2,1,0:T(8,128)(2,1)S(1)}, u32[]{:S(2)}, u32[]{:S(2)}) collective-permute-start(bf16[8,144,128]{2,1,0:T(8,128)(2,1)} %get-tuple-element.27.refs_1_), channel_id=1, source_target_pairs={{0,6},{2,9},{4,11},{6,13},{9,15},{11,16},{13,18},{15,20},{16,22},{... | collective-permute-start | bytes 884744 | tf_op jit(solution)/shard_map/ppermute | solution.py:374
  45.3 2.5 %collective-permute-start.7 = (bf16[8,144,128]{2,1,0:T(8,128)(2,1)}, bf16[8,144,128]{2,1,0:T(8,128)(2,1)S(1)}, u32[]{:S(2)}, u32[]{:S(2)}) collective-permute-start(bf16[8,144,128]{2,1,0:T(8,128)(2,1)} %get-tuple-element.27.refs_1_), channel_id=1, source_target_pairs={{0,9},{2,11},{4,13},{6,15},{9,16},{11,18},{13,20},{15,22},{16,25},... | collective-permute-start | bytes 884744 | tf_op jit(solution)/shard_map/ppermute | solution.py:374
  47.7 0.7 copy-start.4
  47.8 0.8 copy-start.5
  47.8 0.9 copy-start.6
  47.8 1.0 copy-start.7
  52.0 2.1 %collective-permute-start.13 = (bf16[8,144,128]{2,1,0:T(8,128)(2,1)}, bf16[8,144,128]{2,1,0:T(8,128)(2,1)S(1)}, u32[]{:S(2)}, u32[]{:S(2)}) collective-permute-start(bf16[8,144,128]{2,1,0:T(8,128)(2,1)} %near.1.refs_3_), channel_id=1, source_target_pairs={{0,9},{2,11},{4,13},{6,15},{9,16},{11,18},{13,20},{15,22},{16,25},... | collective-permute-start | bytes 884744 | tf_op jit(solution)/shard_map/ppermute | solution.py:374
  52.7 1.4 collective-permute-start.12
  53.4 0.7 collective-permute-start.11
  54.1 0.7 copy-start.8
  54.1 0.8 copy-start.9
  54.9 0.7 copy-start.10
  62.8 89.3 %collective-permute-start.14 = (bf16[4,135,128]{2,1,0:T(8,128)(2,1)}, bf16[4,135,128]{2,1,0:T(8,128)(2,1)S(1)}, u32[]{:S(2)}, u32[]{:S(2)}) collective-permute-start(bf16[4,135,128]{2,1,0:T(8,128)(2,1)} %get-tuple-element.34), channel_id=1, source_target_pairs={{0,1},{2,3},{4,5},{6,7},{9,10},{11,12},{13,14},{15,8},{16,17},{18,... | collective-permute-start | bytes 414728 | tf_op jit(solution)/shard_map/ppermute | solution.py:410
  64.1 88.7 %collective-permute-start.15 = (bf16[4,135,128]{2,1,0:T(8,128)(2,1)}, bf16[4,135,128]{2,1,0:T(8,128)(2,1)S(1)}, u32[]{:S(2)}, u32[]{:S(2)}) collective-permute-start(bf16[4,135,128]{2,1,0:T(8,128)(2,1)} %get-tuple-element.35), channel_id=1, source_target_pairs={{0,2},{2,4},{4,6},{6,0},{9,11},{11,13},{13,15},{15,9},{16,18},{18,... | collective-permute-start | bytes 414728 | tf_op jit(solution)/shard_map/ppermute | solution.py:410
  64.8 94.1 %collective-permute-start.16 = (bf16[4,135,128]{2,1,0:T(8,128)(2,1)}, bf16[4,135,128]{2,1,0:T(8,128)(2,1)S(1)}, u32[]{:S(2)}, u32[]{:S(2)}) collective-permute-start(bf16[4,135,128]{2,1,0:T(8,128)(2,1)} %get-tuple-element.36), channel_id=1, source_target_pairs={{0,3},{2,5},{4,7},{6,1},{9,12},{11,14},{13,8},{15,10},{16,19},{18,... | collective-permute-start | bytes 414728 | tf_op jit(solution)/shard_map/ppermute | solution.py:410
  66.1 92.8 %collective-permute-start.17 = (bf16[4,135,128]{2,1,0:T(8,128)(2,1)}, bf16[4,135,128]{2,1,0:T(8,128)(2,1)S(1)}, u32[]{:S(2)}, u32[]{:S(2)}) collective-permute-start(bf16[4,135,128]{2,1,0:T(8,128)(2,1)} %get-tuple-element.37), channel_id=1, source_target_pairs={{0,4},{2,6},{4,0},{6,2},{9,13},{11,15},{13,9},{15,11},{16,20},{18,... | collective-permute-start | bytes 414728 | tf_op jit(solution)/shard_map/ppermute | solution.py:410
  66.7 98.1 %collective-permute-start.18 = (bf16[4,135,128]{2,1,0:T(8,128)(2,1)}, bf16[4,135,128]{2,1,0:T(8,128)(2,1)S(1)}, u32[]{:S(2)}, u32[]{:S(2)}) collective-permute-start(bf16[4,135,128]{2,1,0:T(8,128)(2,1)} %get-tuple-element.38), channel_id=1, source_target_pairs={{0,5},{2,7},{4,1},{6,3},{9,14},{11,8},{13,10},{15,12},{16,21},{18,... | collective-permute-start | bytes 414728 | tf_op jit(solution)/shard_map/ppermute | solution.py:410
  152.1 15.6 %copy-start.11 = (bf16[4,135,128]{2,1,0:T(8,128)(2,1)}, bf16[4,135,128]{2,1,0:T(8,128)(2,1)S(1)}, u32[]{:S(2)}) copy-start(bf16[4,135,128]{2,1,0:T(8,128)(2,1)S(1)} %collective-permute-done.14.refs_1_) | copy-start | bytes 414724
  152.1 12.7 %collective-permute-start.19 = (bf16[4,135,128]{2,1,0:T(8,128)(2,1)}, bf16[4,135,128]{2,1,0:T(8,128)(2,1)S(1)}, u32[]{:S(2)}, u32[]{:S(2)}) collective-permute-start(bf16[4,135,128]{2,1,0:T(8,128)(2,1)} %get-tuple-element.39), channel_id=1, source_target_pairs={{0,6},{2,0},{4,2},{6,4},{9,15},{11,9},{13,11},{15,13},{16,22},{18,... | collective-permute-start | bytes 414728 | tf_op jit(solution)/shard_map/ppermute | solution.py:410
  152.8 15.0 %copy-start.12 = (bf16[4,135,128]{2,1,0:T(8,128)(2,1)}, bf16[4,135,128]{2,1,0:T(8,128)(2,1)S(1)}, u32[]{:S(2)}) copy-start(bf16[4,135,128]{2,1,0:T(8,128)(2,1)S(1)} %collective-permute-done.15.refs_2_) | copy-start | bytes 414724
  152.8 14.9 %collective-permute-start.20 = (bf16[4,135,128]{2,1,0:T(8,128)(2,1)}, bf16[4,135,128]{2,1,0:T(8,128)(2,1)S(1)}, u32[]{:S(2)}, u32[]{:S(2)}) collective-permute-start(bf16[4,135,128]{2,1,0:T(8,128)(2,1)} %get-tuple-element.40), channel_id=1, source_target_pairs={{0,7},{2,1},{4,3},{6,5},{9,8},{11,10},{13,12},{15,14},{16,23},{18,... | collective-permute-start | bytes 414728 | tf_op jit(solution)/shard_map/ppermute | solution.py:410
  158.9 8.9 %copy-start.13 = (bf16[4,135,128]{2,1,0:T(8,128)(2,1)}, bf16[4,135,128]{2,1,0:T(8,128)(2,1)S(1)}, u32[]{:S(2)}) copy-start(bf16[4,135,128]{2,1,0:T(8,128)(2,1)S(1)} %collective-permute-done.16.refs_3_) | copy-start | bytes 414724
  158.9 8.9 %copy-start.14 = (bf16[4,135,128]{2,1,0:T(8,128)(2,1)}, bf16[4,135,128]{2,1,0:T(8,128)(2,1)S(1)}, u32[]{:S(2)}) copy-start(bf16[4,135,128]{2,1,0:T(8,128)(2,1)S(1)} %collective-permute-done.17.refs_4_) | copy-start | bytes 414724
  164.9 2.9 %copy-start.15 = (bf16[4,135,128]{2,1,0:T(8,128)(2,1)}, bf16[4,135,128]{2,1,0:T(8,128)(2,1)S(1)}, u32[]{:S(2)}) copy-start(bf16[4,135,128]{2,1,0:T(8,128)(2,1)S(1)} %collective-permute-done.18.refs_5_) | copy-start | bytes 414724
  164.9 2.9 %copy-start.16 = (bf16[4,135,128]{2,1,0:T(8,128)(2,1)}, bf16[4,135,128]{2,1,0:T(8,128)(2,1)S(1)}, u32[]{:S(2)}) copy-start(bf16[4,135,128]{2,1,0:T(8,128)(2,1)S(1)} %collective-permute-done.19.refs_6_) | copy-start | bytes 414724
  167.8 0.7 copy-start.17

commit v2 on v1

--- a/solution.py
+++ b/solution.py
@@ -16,7 +16,7 @@
 BF = jnp.bfloat16
 F32 = jnp.float32
 VMEM = pl.BlockSpec(memory_space=pltpu.VMEM)
-LIMIT = 56 * 1024 * 1024
+MIB = 1024 * 1024
 
 
 def dot(a, b):
@@ -127,17 +127,27 @@
             )
 
 
-def pack_kernel(space, intervals, forcing, initial, meta, *messages):
+def pack_kernel(space, intervals, forcing, initial, damping, etype, send_index, conn, *messages):
     place = Place(space, intervals)
     width = initial.shape[0]
+    faces = conn.shape[0]
+    lists = pltpu.roll(jnp.broadcast_to(send_index[...].astype(F32), (8, LANES)), LANES // 2, 1)
+    kinds = jnp.broadcast_to(etype[0].astype(F32), (1, LANES))
+    first = jnp.concatenate([conn[...].astype(F32), kinds, lists[:1]], axis=0).astype(BF)
+    rest = damping[...]
+    pieces = []
+    for _ in range(3):
+        pieces.append(rest.astype(BF))
+        rest = rest - pieces[-1].astype(F32)
+    second = jnp.concatenate(pieces, axis=0)
     for turn in range(intervals):
         interval = lax.rem(place.next_interval + turn, intervals)
         out = messages[turn]
         for index in range(COARSEN):
             out[index, :width] = forcing[interval * COARSEN + index]
         out[COARSEN, :width] = initial[...]
-        out[0, width : width + 8] = meta[0:8]
-        out[1, width : width + 3] = meta[8:11]
+        out[0, width : width + faces + 2] = first
+        out[1, width : width + 3] = second
 
 
 def fine_kernel(space, intervals, width, faces, *refs):
@@ -159,9 +169,9 @@
             message = messages[turn]
             for index in range(COARSEN):
                 forcing[part, index] = message[index]
-            first = message[0, width : width + 8].astype(F32)
+            first = message[0, width : width + faces + 2].astype(F32)
             second = message[1, width : width + 3].astype(F32)
-            kind = first[6:7]
+            kind = first[faces : faces + 1]
             damping = (second[0:1] + second[1:2]) + second[2:3]
             aux[part] = jnp.concatenate(
                 [
@@ -179,7 +189,7 @@
                 gather[part, :, face * LANES : (face + 1) * LANES] = jnp.where(
                     found, 1.0, 0.0
                 ).astype(BF)
-            picks = jnp.where(half == first[7:8], 1.0, 0.0).astype(BF)
+            picks = jnp.where(half == first[faces + 1 : faces + 2], 1.0, 0.0).astype(BF)
             odd = lax.rem(part, 2) == 1
             left = jnp.where(odd, 0.0, 1.0).astype(BF)
             right = jnp.where(odd, 1.0, 0.0).astype(BF)
@@ -197,9 +207,19 @@
             sweeper.step(residual, other, table, 1, lambda part: forcing[part, index])
 
 
-def chain_kernel(space, intervals, faces, powers, count, *refs):
-    terms = refs[:count]
-    table, gather, listing, aux, result, other, outs, work = refs[count:]
+def advance(sweeper, state, other, table, powers, extra=None):
+    if powers > 1:
+
+        @pl.loop(0, powers - 1)
+        def _(turn):
+            sweeper.step(state, other, table, 2)
+
+    sweeper.step(state, other, table, 2, extra=extra)
+
+
+def near_kernel(space, intervals, faces, *refs):
+    terms = refs[:intervals]
+    table, gather, listing, aux, result, other, outs, work = refs[intervals:]
     place = Place(space, intervals)
 
     @pl.when(place.active)
@@ -207,27 +227,42 @@
         sweeper = Sweeper(space, faces, gather, listing, aux, outs, work)
         sweeper.clear_rim()
         result[...] = terms[0][...]
-        for index in range(1, count):
-            if powers > 1:
-
-                @pl.loop(0, powers - 1)
-                def _(turn):
-                    sweeper.step(result, other, table, 2)
-
-            sweeper.step(result, other, table, 2, extra=terms[index])
-
-
-def final_kernel(space, intervals, width, faces, *refs):
-    before, residual, start, forcing = refs[:4]
-    fine_table, coarse_table, gather, listing, aux = refs[4:9]
-    pieces = refs[9 : 9 + space]
-    states, other, outs, work = refs[9 + space :]
+        for term in terms[1:]:
+            advance(sweeper, result, other, table, 1, term)
+
+
+def far_kernel(space, intervals, faces, *refs):
+    *terms, table, gather, listing, aux, result, other, outs, work = refs
     place = Place(space, intervals)
 
     @pl.when(place.active)
     def _():
         sweeper = Sweeper(space, faces, gather, listing, aux, outs, work)
         sweeper.clear_rim()
+        result[...] = sum_of(terms)
+        advance(sweeper, result, other, table, intervals)
+
+
+def sum_of(terms):
+    total = terms[0][...]
+    for term in terms[1:]:
+        total = (total.astype(F32) + term[...].astype(F32)).astype(BF)
+    return total
+
+
+def final_kernel(space, intervals, width, faces, *refs):
+    earlier, inner, partial, residual, start, forcing = refs[:6]
+    fine_table, coarse_table, gather, listing, aux = refs[6:11]
+    pieces = refs[11 : 11 + space]
+    before, states, other, outs, work = refs[11 + space :]
+    place = Place(space, intervals)
+
+    @pl.when(place.active)
+    def _():
+        sweeper = Sweeper(space, faces, gather, listing, aux, outs, work)
+        sweeper.clear_rim()
+        before[...] = sum_of([earlier, inner])
+        advance(sweeper, before, other, coarse_table, intervals, partial)
         last = COARSEN - 1
         state = states.at[last]
         state[...] = before[...]
@@ -272,20 +307,19 @@
         ).wait()
 
 
-def folded(inverse, coupling):
-    width = inverse.shape[-1]
-    faces = coupling.shape[0]
-    products = -jnp.einsum("kij,fjl->kifl", inverse, coupling, preferred_element_type=F32)
-    every = jnp.concatenate([products.astype(BF), inverse[:, :, None, :]], axis=2)
-    every = jnp.pad(every, ((0, 0), (0, 0), (0, 0), (0, ROWS - width)))
-    every = every.reshape(2, width, (faces + 1) * ROWS)
-    return jnp.concatenate(
-        [
-            jnp.pad(every[0], ((0, ROWS - width), (0, 0))),
-            jnp.pad(every[1, :PRISM], ((0, PROWS - PRISM), (0, 0))),
-        ],
-        axis=0,
-    )
+def fold_kernel(fine, coarse, coupling, fine_table, coarse_table, wide):
+    faces, width, _ = coupling.shape
+    wide[...] = jnp.zeros(wide.shape, F32)
+    for face in range(faces):
+        wide[:width, face * ROWS : face * ROWS + width] = -coupling[face].astype(F32)
+    rows = lax.broadcasted_iota(jnp.int32, (width, width), 0)
+    columns = lax.broadcasted_iota(jnp.int32, (width, width), 1)
+    wide[:width, faces * ROWS : faces * ROWS + width] = jnp.where(rows == columns, 1.0, 0.0)
+    factors = wide[:width].astype(BF)
+    for inverse, table in ((fine, fine_table), (coarse, coarse_table)):
+        table[...] = jnp.zeros(table.shape, BF)
+        table[:width] = dot(inverse[0], factors).astype(BF)
+        table[ROWS : ROWS + PRISM] = dot(inverse[1], factors)[:PRISM].astype(BF)
 
 
 def shards(initial, forcing, damping, block_inv, coarse_inv, coupling, etype, send_index, conn):
@@ -296,37 +330,18 @@
     space = lax.axis_size("space")
     windows = lax.axis_size("tm")
     stride = space // intervals
-    halo = send_index.shape[0] // 2
-    params = pltpu.CompilerParams(vmem_limit_bytes=LIMIT)
+    params = pltpu.CompilerParams(vmem_limit_bytes=min(56, 2 * space) * MIB)
     state_shape = jax.ShapeDtypeStruct((space, ROWS, LANES), BF)
-
-    kinds = jnp.broadcast_to(etype[:, None], (etype.shape[0], elems // etype.shape[0]))
-    lists = jnp.concatenate([send_index[halo:], send_index[:halo]])
-    high = lax.reduce_precision(damping, 8, 7)
-    middle = lax.reduce_precision(damping - high, 8, 7)
-    low = (damping - high) - middle
-    meta = jnp.concatenate(
-        [
-            conn.astype(F32),
-            kinds.reshape(1, elems).astype(F32),
-            lists[None].astype(F32),
-            high[None],
-            middle[None],
-            low[None],
-            jnp.zeros((16 - faces - 5, elems), F32),
-        ],
-        axis=0,
-    ).astype(BF)
 
     message_shape = jax.ShapeDtypeStruct((COARSEN + 1, ROWS, LANES), BF)
     messages = pl.pallas_call(
         functools.partial(pack_kernel, space, intervals),
         out_shape=[message_shape] * intervals,
-        in_specs=[VMEM] * 3,
+        in_specs=[VMEM] * 3 + [pl.BlockSpec(memory_space=pltpu.SMEM)] + [VMEM] * 2,
         out_specs=[VMEM] * intervals,
         compiler_params=params,
         name="pack",
-    )(forcing, initial, meta)
+    )(forcing, initial, damping[None], etype, send_index[None], conn)
 
     received = [messages[0]]
     for turn in range(1, space):
@@ -338,8 +353,16 @@
                 pairs.append((window * space + source, window * space + host))
         received.append(lax.ppermute(messages[turn // stride], ("tm", "space"), pairs))
 
-    fine_table = folded(block_inv, coupling)
-    coarse_table = folded(coarse_inv, coupling)
+    table_shape = jax.ShapeDtypeStruct((ROWS + PROWS, (faces + 1) * ROWS), BF)
+    fine_table, coarse_table = pl.pallas_call(
+        fold_kernel,
+        out_shape=[table_shape] * 2,
+        in_specs=[VMEM] * 3,
+        out_specs=[VMEM] * 2,
+        scratch_shapes=[pltpu.VMEM((ROWS, (faces + 1) * ROWS), F32)],
+        compiler_params=params,
+        name="fold",
+    )(block_inv, coarse_inv, coupling)
 
     gather_shape = jax.ShapeDtypeStruct((space, 2 * LANES, faces * LANES), BF)
     listing_shape = jax.ShapeDtypeStruct((space // 2, 2 * LANES, 2 * LANES), BF)
@@ -373,9 +396,9 @@
             )
         return lax.ppermute(value, ("tm", "space"), pairs)
 
-    def chain(terms, powers, name):
+    def chain(kernel, terms, name):
         return pl.pallas_call(
-            functools.partial(chain_kernel, space, intervals, faces, powers, len(terms)),
+            functools.partial(kernel, space, intervals, faces),
             out_shape=state_shape,
             in_specs=[VMEM] * (len(terms) + 4),
             out_specs=VMEM,
@@ -385,20 +408,40 @@
         )(*terms, coarse_table, gather, listing, aux)
 
     near = [from_earlier(residual, by) for by in range(intervals, 0, -1)]
-    partial = chain(near, 1, "near")
-    far = [from_earlier(partial, by * intervals) for by in range(windows - 1, 0, -1)]
-    before = chain(far + [partial], intervals, "far")
+    partial = chain(near_kernel, near, "near")
+    earlier, *inner = [
+        from_earlier(partial, by * intervals) for by in range(windows - 1, 0, -1)
+    ]
+    earlier = chain(far_kernel, [earlier], "far")
+    for term in inner[:-1]:
+        earlier = chain(far_kernel, [earlier, term], "far")
 
     piece_shape = jax.ShapeDtypeStruct((COARSEN, width, LANES), BF)
     pieces = pl.pallas_call(
         functools.partial(final_kernel, space, intervals, width, faces),
         out_shape=[piece_shape] * space,
-        in_specs=[VMEM] * 9,
+        in_specs=[VMEM] * 11,
         out_specs=[VMEM] * space,
-        scratch_shapes=[pltpu.VMEM((COARSEN, space, ROWS, LANES), BF)] + scratch,
+        scratch_shapes=[
+            pltpu.VMEM((space, ROWS, LANES), BF),
+            pltpu.VMEM((COARSEN, space, ROWS, LANES), BF),
+        ]
+        + scratch,
         compiler_params=params,
         name="final",
-    )(before, residual, start, whole_forcing, fine_table, coarse_table, gather, listing, aux)
+    )(
+        earlier,
+        inner[-1],
+        partial,
+        residual,
+        start,
+        whole_forcing,
+        fine_table,
+        coarse_table,
+        gather,
+        listing,
+        aux,
+    )
 
     returned = [pieces[0]]
     for turn in range(1, space):
@@ -413,7 +456,7 @@
         functools.partial(gather_kernel, space, intervals),
         out_shape=jax.ShapeDtypeStruct(forcing.shape, BF),
         in_specs=[pl.BlockSpec(memory_space=pl.ANY)] * space,
-        out_specs=pl.BlockSpec(memory_space=pl.ANY),
+        out_specs=VMEM,
         scratch_shapes=[pltpu.SemaphoreType.DMA((intervals,))],
         compiler_params=params,
         name="place",

time: 191 us -> 144 us (0.75)
  Pallas kernels: 34.4 us -> 2.28 us
  local copies, waits for them, and re-layouts: 18.2 us -> 7.68 us
  waiting for transfers between devices: 97.8 us -> 104 us
  starting transfers between devices: 31.6 us -> 26.9 us
  other arithmetic: 4.47 us -> 0 us
    pallas_call x1, Pallas kernels: 18 us -> 0.88 us  [shards(): pl.pallas_call(functools.partial(gather_kernel, space, intervals), out_sh...]
    ppermute x7, waiting for transfers between devices: 97.7 us -> 104 us  [shards(): returned.append(lax.ppermute(pieces[turn], ('tm', 'space'), pairs))]
    pallas_call x2 -> x4, Pallas kernels: 6.43 us -> 1.03 us  [the longest x1 0.76 us: shards(): pl.pallas_call(fold_kernel, out_shape=[table_shape] * 2, in_specs=[VMEM]...]
    ppermute x7, starting transfers between devices: 19.7 us -> 15 us  [shards(): lax.ppermute(messages[turn // stride], ('tm', 'space'), pairs)]
    reshape x2 -> x0, local copies, waits for them, and re-layouts: 4.01 us -> none  [folded(): every = every.reshape(2, width, (faces + 1) * ROWS)]
    pallas_call x1, Pallas kernels: 4.01 us -> 0.03 us  [shards(): pl.pallas_call(functools.partial(fine_kernel, space, intervals, width, fa...]
    pallas_call x1, Pallas kernels: 4.01 us -> 0.25 us  [shards(): pl.pallas_call(functools.partial(final_kernel, space, intervals, width, f...]
    concatenate x4 -> x0, other arithmetic: 3.04 us -> none  [the longest x2 1.68 us: folded(): jnp.concatenate([jnp.pad(every[0], ((0, ROWS - width), (0, 0))), jnp.pad(...]
  transfers between devices with their start and end apart: 21 -> 21, of which waited for: 4 -> 4; matrix products, arithmetic and copies ran while one was open for 7% -> 1% of each run, Pallas kernels for 0% -> 1%
where the time goes in v2:
time: 144 us; the launch traced here: 142 us
  waiting for transfers between devices  104 us (72%)
  starting transfers between devices  26.9 us (19%)
  local copies, waits for them, and re-layouts  7.68 us (5%)
  Pallas kernels  2.28 us (2%)
    ppermute x7, waiting for transfers between devices, shards(): returned.append(lax.ppermute(pieces[turn], ('tm', 'space'), pairs))  104 us
    ppermute x7, starting transfers between devices, shards(): lax.ppermute(messages[turn // stride], ('tm', 'space'), pairs)  15 us
    ppermute x7, starting transfers between devices, shards(): returned.append(lax.ppermute(pieces[turn], ('tm', 'space'), pairs))  7.17 us
    unnamed x13, local copies, waits for them, and re-layouts  6.8 us
    ppermute x7, starting transfers between devices, from_earlier(): return lax.ppermute(value, ('tm', 'space'), pairs)  4.76 us
  transfers between devices with their start and end apart: 21, of which 4 were waited for; matrix products, arithmetic and copies ran while one was open for 1% of the time, Pallas kernels for 1%

profile of v2, /device:TPU:6, one launch (start us, length us, event | category | flops | bytes accessed | tf_op | source)
XLA Modules:
  0.0 141.5 jit_solution(8341283518747246189)
XLA Ops:
  0.7 1.2 copy.10.forcing
  1.9 0.0 copy-start.1
  1.9 0.8 copy-done.1
  2.6 0.7 copy-done.2
  3.3 0.7 copy-done.3
  4.0 0.7 copy-done.4
  4.6 0.1 pack.1
  4.7 3.4 %collective-permute-start = (bf16[5,144,128]{2,1,0:T(8,128)(2,1)S(1)}, bf16[5,144,128]{2,1,0:T(8,128)(2,1)S(1)}, u32[]{:S(2)}, u32[]{:S(2)}) collective-permute-start(bf16[5,144,128]{2,1,0:T(8,128)(2,1)S(1)} %get-tuple-element.25.refs_0_), channel_id=1, source_target_pairs={{7,0},{1,2},{3,4},{5,6},{8,9},{10,11},{12,13},{14,15},{23,16},{17,... | collective-permute-start | bytes 552968 | tf_op jit(solution)/shard_map/ppermute | solution.py:354
  8.1 2.3 %collective-permute-start.2 = (bf16[5,144,128]{2,1,0:T(8,128)(2,1)S(1)}, bf16[5,144,128]{2,1,0:T(8,128)(2,1)S(1)}, u32[]{:S(2)}, u32[]{:S(2)}) collective-permute-start(bf16[5,144,128]{2,1,0:T(8,128)(2,1)S(1)} %get-tuple-element.26), channel_id=1, source_target_pairs={{5,0},{7,2},{1,4},{3,6},{14,9},{8,11},{10,13},{12,15},{21,16},{23,... | collective-permute-start | bytes 552968 | tf_op jit(solution)/shard_map/ppermute | solution.py:354
  10.5 0.7 collective-permute-start.1
  11.1 3.8 %collective-permute-start.4 = (bf16[5,144,128]{2,1,0:T(8,128)(2,1)S(1)}, bf16[5,144,128]{2,1,0:T(8,128)(2,1)S(1)}, u32[]{:S(2)}, u32[]{:S(2)}) collective-permute-start(bf16[5,144,128]{2,1,0:T(8,128)(2,1)S(1)} %get-tuple-element.27), channel_id=1, source_target_pairs={{3,0},{5,2},{7,4},{1,6},{12,9},{14,11},{8,13},{10,15},{19,16},{21,... | collective-permute-start | bytes 552968 | tf_op jit(solution)/shard_map/ppermute | solution.py:354
  14.9 0.7 collective-permute-start.3
  15.6 3.4 %collective-permute-start.6 = (bf16[5,144,128]{2,1,0:T(8,128)(2,1)S(1)}, bf16[5,144,128]{2,1,0:T(8,128)(2,1)S(1)}, u32[]{:S(2)}, u32[]{:S(2)}) collective-permute-start(bf16[5,144,128]{2,1,0:T(8,128)(2,1)S(1)} %get-tuple-element.28), channel_id=1, source_target_pairs={{1,0},{3,2},{5,4},{7,6},{10,9},{12,11},{14,13},{8,15},{17,16},{19,... | collective-permute-start | bytes 552968 | tf_op jit(solution)/shard_map/ppermute | solution.py:354
  19.1 0.7 collective-permute-start.5
  19.7 0.9 copy.11.fine
  20.7 0.9 copy.12.coarse
  21.6 0.0 copy-start
  21.6 1.0 copy-done
  22.6 0.8 fold.1
  23.4 0.0 collective-permute-done.1.refs_2_
  23.4 0.0 collective-permute-done.4.refs_5_
  23.4 0.0 collective-permute-done.5.refs_6_
  23.5 0.7 collective-permute-start.10
  24.1 0.7 collective-permute-start.9
  24.8 0.7 collective-permute-start.8
  25.5 0.7 collective-permute-start.7
  26.2 0.0 collective-permute-done.10.refs_3_
  26.2 0.0 collective-permute-done.9.refs_2_
  26.3 0.7 collective-permute-start.11
  27.0 0.7 collective-permute-start.12
  27.7 0.7 collective-permute-start.13
  28.4 0.0 collective-permute-done.11.refs_0_
  28.4 0.2 far.2.refs_0_
  28.6 0.3 final.1
  28.9 1.3 collective-permute-start.14
  30.2 0.7 collective-permute-start.15
  30.9 1.3 collective-permute-start.16
  32.2 0.7 collective-permute-start.17
  32.8 1.3 collective-permute-start.18
  34.1 90.0 %collective-permute-done.14.refs_1_ = bf16[4,135,128]{2,1,0:T(8,128)(2,1)S(1)} collective-permute-done((bf16[4,135,128]{2,1,0:T(8,128)(2,1)S(1)}, bf16[4,135,128]{2,1,0:T(8,128)(2,1)S(1)}, u32[]{:S(2)}, u32[]{:S(2)}) %collective-permute-start.14) | collective-permute-done | bytes 138272 | tf_op jit(solution)/shard_map/ppermute | solution.py:453
  124.1 0.7 collective-permute-start.19
  124.8 0.0 collective-permute-done.15.refs_2_
  124.8 1.3 collective-permute-start.20
  126.1 4.8 %collective-permute-done.16.refs_3_ = bf16[4,135,128]{2,1,0:T(8,128)(2,1)S(1)} collective-permute-done((bf16[4,135,128]{2,1,0:T(8,128)(2,1)S(1)}, bf16[4,135,128]{2,1,0:T(8,128)(2,1)S(1)}, u32[]{:S(2)}, u32[]{:S(2)}) %collective-permute-start.16) | collective-permute-done | bytes 138272 | tf_op jit(solution)/shard_map/ppermute | solution.py:453
  130.9 6.0 %collective-permute-done.18.refs_5_ = bf16[4,135,128]{2,1,0:T(8,128)(2,1)S(1)} collective-permute-done((bf16[4,135,128]{2,1,0:T(8,128)(2,1)S(1)}, bf16[4,135,128]{2,1,0:T(8,128)(2,1)S(1)}, u32[]{:S(2)}, u32[]{:S(2)}) %collective-permute-start.18) | collective-permute-done | bytes 138272 | tf_op jit(solution)/shard_map/ppermute | solution.py:453
  136.9 2.9 %collective-permute-done.20.refs_7_ = bf16[4,135,128]{2,1,0:T(8,128)(2,1)S(1)} collective-permute-done((bf16[4,135,128]{2,1,0:T(8,128)(2,1)S(1)}, bf16[4,135,128]{2,1,0:T(8,128)(2,1)S(1)}, u32[]{:S(2)}, u32[]{:S(2)}) %collective-permute-start.20) | collective-permute-done | bytes 138272 | tf_op jit(solution)/shard_map/ppermute | solution.py:453
  139.7 0.9 place.1
  140.6 0.9 copy.13
  (16 shorter events, 0.1 us)
Async XLA Ops:
  1.9 0.8 copy-start.1
  2.6 0.7 copy-start.2
  3.3 0.7 copy-start.3
  4.0 0.7 copy-start.4
  4.7 10.9 %collective-permute-start = (bf16[5,144,128]{2,1,0:T(8,128)(2,1)S(1)}, bf16[5,144,128]{2,1,0:T(8,128)(2,1)S(1)}, u32[]{:S(2)}, u32[]{:S(2)}) collective-permute-start(bf16[5,144,128]{2,1,0:T(8,128)(2,1)S(1)} %get-tuple-element.25.refs_0_), channel_id=1, source_target_pairs={{7,0},{1,2},{3,4},{5,6},{8,9},{10,11},{12,13},{14,15},{23,16},{17,... | collective-permute-start | bytes 552968 | tf_op jit(solution)/shard_map/ppermute | solution.py:354
  8.1 10.9 %collective-permute-start.2 = (bf16[5,144,128]{2,1,0:T(8,128)(2,1)S(1)}, bf16[5,144,128]{2,1,0:T(8,128)(2,1)S(1)}, u32[]{:S(2)}, u32[]{:S(2)}) collective-permute-start(bf16[5,144,128]{2,1,0:T(8,128)(2,1)S(1)} %get-tuple-element.26), channel_id=1, source_target_pairs={{5,0},{7,2},{1,4},{3,6},{14,9},{8,11},{10,13},{12,15},{21,16},{23,... | collective-permute-start | bytes 552968 | tf_op jit(solution)/shard_map/ppermute | solution.py:354
  10.5 12.9 %collective-permute-start.1 = (bf16[5,144,128]{2,1,0:T(8,128)(2,1)S(1)}, bf16[5,144,128]{2,1,0:T(8,128)(2,1)S(1)}, u32[]{:S(2)}, u32[]{:S(2)}) collective-permute-start(bf16[5,144,128]{2,1,0:T(8,128)(2,1)S(1)} %get-tuple-element.26), channel_id=1, source_target_pairs={{6,0},{0,2},{2,4},{4,6},{15,9},{9,11},{11,13},{13,15},{22,16},{16,... | collective-permute-start | bytes 552968 | tf_op jit(solution)/shard_map/ppermute | solution.py:354
  11.1 12.2 %collective-permute-start.4 = (bf16[5,144,128]{2,1,0:T(8,128)(2,1)S(1)}, bf16[5,144,128]{2,1,0:T(8,128)(2,1)S(1)}, u32[]{:S(2)}, u32[]{:S(2)}) collective-permute-start(bf16[5,144,128]{2,1,0:T(8,128)(2,1)S(1)} %get-tuple-element.27), channel_id=1, source_target_pairs={{3,0},{5,2},{7,4},{1,6},{12,9},{14,11},{8,13},{10,15},{19,16},{21,... | collective-permute-start | bytes 552968 | tf_op jit(solution)/shard_map/ppermute | solution.py:354
  14.9 8.5 %collective-permute-start.3 = (bf16[5,144,128]{2,1,0:T(8,128)(2,1)S(1)}, bf16[5,144,128]{2,1,0:T(8,128)(2,1)S(1)}, u32[]{:S(2)}, u32[]{:S(2)}) collective-permute-start(bf16[5,144,128]{2,1,0:T(8,128)(2,1)S(1)} %get-tuple-element.27), channel_id=1, source_target_pairs={{4,0},{6,2},{0,4},{2,6},{13,9},{15,11},{9,13},{11,15},{20,16},{22,... | collective-permute-start | bytes 552968 | tf_op jit(solution)/shard_map/ppermute | solution.py:354
  15.6 7.8 %collective-permute-start.6 = (bf16[5,144,128]{2,1,0:T(8,128)(2,1)S(1)}, bf16[5,144,128]{2,1,0:T(8,128)(2,1)S(1)}, u32[]{:S(2)}, u32[]{:S(2)}) collective-permute-start(bf16[5,144,128]{2,1,0:T(8,128)(2,1)S(1)} %get-tuple-element.28), channel_id=1, source_target_pairs={{1,0},{3,2},{5,4},{7,6},{10,9},{12,11},{14,13},{8,15},{17,16},{19,... | collective-permute-start | bytes 552968 | tf_op jit(solution)/shard_map/ppermute | solution.py:354
  19.1 4.4 %collective-permute-start.5 = (bf16[5,144,128]{2,1,0:T(8,128)(2,1)S(1)}, bf16[5,144,128]{2,1,0:T(8,128)(2,1)S(1)}, u32[]{:S(2)}, u32[]{:S(2)}) collective-permute-start(bf16[5,144,128]{2,1,0:T(8,128)(2,1)S(1)} %get-tuple-element.28), channel_id=1, source_target_pairs={{2,0},{4,2},{6,4},{0,6},{11,9},{13,11},{15,13},{9,15},{18,16},{20,... | collective-permute-start | bytes 552968 | tf_op jit(solution)/shard_map/ppermute | solution.py:354
  21.6 1.0 copy-start
  23.5 2.8 %collective-permute-start.10 = (bf16[8,144,128]{2,1,0:T(8,128)(2,1)S(1)}, bf16[8,144,128]{2,1,0:T(8,128)(2,1)S(1)}, u32[]{:S(2)}, u32[]{:S(2)}) collective-permute-start(bf16[8,144,128]{2,1,0:T(8,128)(2,1)S(1)} %get-tuple-element.30.refs_3_), channel_id=1, source_target_pairs={{0,2},{2,4},{4,6},{6,9},{9,11},{11,13},{13,15},{15,16},{16,18},{18... | collective-permute-start | bytes 884744 | tf_op jit(solution)/shard_map/ppermute | solution.py:397
  24.1 2.1 %collective-permute-start.9 = (bf16[8,144,128]{2,1,0:T(8,128)(2,1)S(1)}, bf16[8,144,128]{2,1,0:T(8,128)(2,1)S(1)}, u32[]{:S(2)}, u32[]{:S(2)}) collective-permute-start(bf16[8,144,128]{2,1,0:T(8,128)(2,1)S(1)} %get-tuple-element.30.refs_3_), channel_id=1, source_target_pairs={{0,4},{2,6},{4,9},{6,11},{9,13},{11,15},{13,16},{15,18},{16,20},{1... | collective-permute-start | bytes 884744 | tf_op jit(solution)/shard_map/ppermute | solution.py:397
  24.8 1.4 collective-permute-start.8
  25.5 0.7 collective-permute-start.7
  26.3 2.1 %collective-permute-start.11 = (bf16[8,144,128]{2,1,0:T(8,128)(2,1)S(1)}, bf16[8,144,128]{2,1,0:T(8,128)(2,1)S(1)}, u32[]{:S(2)}, u32[]{:S(2)}) collective-permute-start(bf16[8,144,128]{2,1,0:T(8,128)(2,1)S(1)} %near.1.refs_2_), channel_id=1, source_target_pairs={{0,25},{2,27},{4,29},{6,31}} | collective-permute-start | bytes 884744 | tf_op jit(solution)/shard_map/ppermute | solution.py:397
  27.0 1.6 %collective-permute-start.12 = (bf16[8,144,128]{2,1,0:T(8,128)(2,1)S(1)}, bf16[8,144,128]{2,1,0:T(8,128)(2,1)S(1)}, u32[]{:S(2)}, u32[]{:S(2)}) collective-permute-start(bf16[8,144,128]{2,1,0:T(8,128)(2,1)S(1)} %near.1.refs_2_), channel_id=1, source_target_pairs={{0,16},{2,18},{4,20},{6,22},{9,25},{11,27},{13,29},{15,31}} | collective-permute-start | bytes 884744 | tf_op jit(solution)/shard_map/ppermute | solution.py:397
  27.7 1.0 collective-permute-start.13
  28.9 95.2 %collective-permute-start.14 = (bf16[4,135,128]{2,1,0:T(8,128)(2,1)S(1)}, bf16[4,135,128]{2,1,0:T(8,128)(2,1)S(1)}, u32[]{:S(2)}, u32[]{:S(2)}) collective-permute-start(bf16[4,135,128]{2,1,0:T(8,128)(2,1)S(1)} %get-tuple-element.38), channel_id=1, source_target_pairs={{0,1},{2,3},{4,5},{6,7},{9,10},{11,12},{13,14},{15,8},{16,17},{18,... | collective-permute-start | bytes 414728 | tf_op jit(solution)/shard_map/ppermute | solution.py:453
  30.2 94.6 %collective-permute-start.15 = (bf16[4,135,128]{2,1,0:T(8,128)(2,1)S(1)}, bf16[4,135,128]{2,1,0:T(8,128)(2,1)S(1)}, u32[]{:S(2)}, u32[]{:S(2)}) collective-permute-start(bf16[4,135,128]{2,1,0:T(8,128)(2,1)S(1)} %get-tuple-element.39), channel_id=1, source_target_pairs={{0,2},{2,4},{4,6},{6,0},{9,11},{11,13},{13,15},{15,9},{16,18},{18,... | collective-permute-start | bytes 414728 | tf_op jit(solution)/shard_map/ppermute | solution.py:453
  30.9 100.0 %collective-permute-start.16 = (bf16[4,135,128]{2,1,0:T(8,128)(2,1)S(1)}, bf16[4,135,128]{2,1,0:T(8,128)(2,1)S(1)}, u32[]{:S(2)}, u32[]{:S(2)}) collective-permute-start(bf16[4,135,128]{2,1,0:T(8,128)(2,1)S(1)} %get-tuple-element.40), channel_id=1, source_target_pairs={{0,3},{2,5},{4,7},{6,1},{9,12},{11,14},{13,8},{15,10},{16,19},{18,... | collective-permute-start | bytes 414728 | tf_op jit(solution)/shard_map/ppermute | solution.py:453
  32.2 98.7 %collective-permute-start.17 = (bf16[4,135,128]{2,1,0:T(8,128)(2,1)S(1)}, bf16[4,135,128]{2,1,0:T(8,128)(2,1)S(1)}, u32[]{:S(2)}, u32[]{:S(2)}) collective-permute-start(bf16[4,135,128]{2,1,0:T(8,128)(2,1)S(1)} %get-tuple-element.41), channel_id=1, source_target_pairs={{0,4},{2,6},{4,0},{6,2},{9,13},{11,15},{13,9},{15,11},{16,20},{18,... | collective-permute-start | bytes 414728 | tf_op jit(solution)/shard_map/ppermute | solution.py:453
  32.8 104.0 %collective-permute-start.18 = (bf16[4,135,128]{2,1,0:T(8,128)(2,1)S(1)}, bf16[4,135,128]{2,1,0:T(8,128)(2,1)S(1)}, u32[]{:S(2)}, u32[]{:S(2)}) collective-permute-start(bf16[4,135,128]{2,1,0:T(8,128)(2,1)S(1)} %get-tuple-element.42), channel_id=1, source_target_pairs={{0,5},{2,7},{4,1},{6,3},{9,14},{11,8},{13,10},{15,12},{16,21},{18,... | collective-permute-start | bytes 414728 | tf_op jit(solution)/shard_map/ppermute | solution.py:453
  124.1 12.7 %collective-permute-start.19 = (bf16[4,135,128]{2,1,0:T(8,128)(2,1)S(1)}, bf16[4,135,128]{2,1,0:T(8,128)(2,1)S(1)}, u32[]{:S(2)}, u32[]{:S(2)}) collective-permute-start(bf16[4,135,128]{2,1,0:T(8,128)(2,1)S(1)} %get-tuple-element.43), channel_id=1, source_target_pairs={{0,6},{2,0},{4,2},{6,4},{9,15},{11,9},{13,11},{15,13},{16,22},{18,... | collective-permute-start | bytes 414728 | tf_op jit(solution)/shard_map/ppermute | solution.py:453
  124.8 14.9 %collective-permute-start.20 = (bf16[4,135,128]{2,1,0:T(8,128)(2,1)S(1)}, bf16[4,135,128]{2,1,0:T(8,128)(2,1)S(1)}, u32[]{:S(2)}, u32[]{:S(2)}) collective-permute-start(bf16[4,135,128]{2,1,0:T(8,128)(2,1)S(1)} %get-tuple-element.44), channel_id=1, source_target_pairs={{0,7},{2,1},{4,3},{6,5},{9,8},{11,10},{13,12},{15,14},{16,23},{18,... | collective-permute-start | bytes 414728 | tf_op jit(solution)/shard_map/ppermute | solution.py:453

commit v3 on v2

--- a/solution.py
+++ b/solution.py
@@ -13,6 +13,7 @@
 ROWS = 144
 PROWS = 96
 LANES = 128
+PICKED = 2
 BF = jnp.bfloat16
 F32 = jnp.float32
 VMEM = pl.BlockSpec(memory_space=pltpu.VMEM)
@@ -28,18 +29,30 @@
     return (interval * stride + (window % 2) % stride) % space
 
 
+def away(host, turn, window, space):
+    return (host + (turn if window % 2 == 0 else -turn)) % space
+
+
 class Place:
     def __init__(self, space, intervals):
         stride = space // intervals
         self.window = lax.axis_index("tm")
+        self.space = space
+        self.sign = 1 - 2 * lax.rem(self.window, 2)
         self.position = lax.axis_index("space")
         shifted = lax.rem(
             self.position - lax.rem(lax.rem(self.window, 2), stride) + space, space
         )
         self.active = lax.rem(shifted, stride) == 0
         self.interval = shifted // stride
-        self.next_interval = lax.rem((shifted + stride - 1) // stride, intervals)
+        below = shifted // stride
+        above = lax.rem((shifted + stride - 1) // stride, intervals)
+        self.nearest = jnp.where(self.sign > 0, below, above)
         self.number = self.window * intervals + self.interval
+
+
+    def away(self, turn):
+        return lax.rem(self.position + self.sign * turn + self.space, self.space)
 
 
 def over_pairs(parts, body):
@@ -90,14 +103,26 @@
             for side in range(2):
                 part = 2 * pair + side
                 rim = jnp.where(lane < LANES // 2, self.outs[part], self.outs[part + 2])
-                extended = jnp.concatenate([source[part], rim], axis=1)
-                found = dot(extended, self.gather[part]).astype(BF)
+                own = source[part]
+                found = dot(jnp.concatenate([own, rim], axis=1), self.gather[part]).astype(BF)
+                own, rim = own.astype(F32), rim.astype(F32)
                 for face in range(self.faces):
+                    if face < self.faces - PICKED:
+                        value = found[:, face * LANES : (face + 1) * LANES]
+                    else:
+                        row = 3 + face - (self.faces - PICKED)
+                        place = jnp.broadcast_to(
+                            self.aux[part, row : row + 1, :].astype(jnp.int32), (ROWS, LANES)
+                        )
+                        lanes = place & (LANES - 1)
+                        inner = jnp.where(place < 0, 0.0, jnp.take_along_axis(own, lanes, axis=1))
+                        outer = jnp.take_along_axis(rim, lanes, axis=1)
+                        value = jnp.where(place < LANES, inner, outer).astype(BF)
                     self.work[
                         pair,
                         face * ROWS : (face + 1) * ROWS,
                         side * LANES : (side + 1) * LANES,
-                    ] = found[:, face * LANES : (face + 1) * LANES]
+                    ] = value
 
         def applied(pair):
             both = dot(table[...], self.work[pair])
@@ -127,7 +152,17 @@
             )
 
 
-def pack_kernel(space, intervals, forcing, initial, damping, etype, send_index, conn, *messages):
+def pack_kernel(space, intervals, etype, *refs):
+    sources, refs = refs[:5], refs[5:]
+    messages, refs = refs[:intervals], refs[intervals:]
+    held, (packed, in_sem, out_sem) = refs[:5], refs[5:]
+    arriving = []
+    for index in range(5):
+        arriving.append(pltpu.make_async_copy(sources[index], held[index], in_sem.at[index]))
+        arriving[-1].start()
+    for copy in arriving:
+        copy.wait()
+    forcing, initial, damping, send_index, conn = held
     place = Place(space, intervals)
     width = initial.shape[0]
     faces = conn.shape[0]
@@ -140,14 +175,19 @@
         pieces.append(rest.astype(BF))
         rest = rest - pieces[-1].astype(F32)
     second = jnp.concatenate(pieces, axis=0)
+    leaving = []
     for turn in range(intervals):
-        interval = lax.rem(place.next_interval + turn, intervals)
-        out = messages[turn]
+        interval = lax.rem(place.nearest - place.sign * turn + intervals, intervals)
+        out = packed.at[turn]
         for index in range(COARSEN):
             out[index, :width] = forcing[interval * COARSEN + index]
         out[COARSEN, :width] = initial[...]
         out[0, width : width + faces + 2] = first
         out[1, width : width + 3] = second
+        leaving.append(pltpu.make_async_copy(out, messages[turn], out_sem.at[turn]))
+        leaving[-1].start()
+    for copy in leaving:
+        copy.wait()
 
 
 def fine_kernel(space, intervals, width, faces, *refs):
@@ -165,7 +205,7 @@
         half = full[:LANES]
         zero = jnp.zeros((LANES, LANES), BF)
         for turn in range(space):
-            part = lax.rem(place.position - turn + space, space)
+            part = place.away(turn)
             message = messages[turn]
             for index in range(COARSEN):
                 forcing[part, index] = message[index]
@@ -173,19 +213,20 @@
             second = message[1, width : width + 3].astype(F32)
             kind = first[faces : faces + 1]
             damping = (second[0:1] + second[1:2]) + second[2:3]
+            picked = [first[face : face + 1] for face in range(faces - PICKED, faces)]
+            picked[-1] = jnp.where(kind == 0.0, picked[-1], -1.0)
             aux[part] = jnp.concatenate(
                 [
                     kind,
                     jnp.exp(-damping),
                     jnp.exp(-COARSEN * damping),
-                    jnp.zeros((5, LANES), F32),
+                    *picked,
+                    jnp.zeros((5 - PICKED, LANES), F32),
                 ],
                 axis=0,
             )
-            for face in range(faces):
+            for face in range(faces - PICKED):
                 found = full == first[face : face + 1]
-                if face == faces - 1:
-                    found = found & (kind == 0.0)
                 gather[part, :, face * LANES : (face + 1) * LANES] = jnp.where(
                     found, 1.0, 0.0
                 ).astype(BF)
@@ -207,62 +248,68 @@
             sweeper.step(residual, other, table, 1, lambda part: forcing[part, index])
 
 
-def advance(sweeper, state, other, table, powers, extra=None):
-    if powers > 1:
-
-        @pl.loop(0, powers - 1)
-        def _(turn):
-            sweeper.step(state, other, table, 2)
-
-    sweeper.step(state, other, table, 2, extra=extra)
-
-
-def near_kernel(space, intervals, faces, *refs):
+def added(first, second):
+    return (first.astype(F32) + second.astype(F32)).astype(BF)
+
+
+def horner(sweeper, state, other, table, terms, known):
+    for index, term in enumerate(terms):
+
+        @pl.when(known + index >= 0)
+        def _():
+            sweeper.step(state, other, table, 2, extra=term)
+
+        @pl.when(known + index < 0)
+        def _():
+            state[...] = term[...]
+
+
+def near_kernel(space, intervals, windows, faces, *refs):
     terms = refs[:intervals]
     table, gather, listing, aux, result, other, outs, work = refs[intervals:]
+    place = Place(space, intervals)
+
+    @pl.when(place.active & (place.window + 1 < windows))
+    def _():
+        sweeper = Sweeper(space, faces, gather, listing, aux, outs, work)
+        sweeper.clear_rim()
+        result[...] = terms[0][...]
+        horner(sweeper, result, other, table, terms[1:], place.number - intervals)
+
+
+def far_kernel(space, intervals, least, faces, *refs):
+    *terms, table, gather, listing, aux, result, other, outs, work = refs
+    place = Place(space, intervals)
+
+    @pl.when(place.active & (place.window >= least))
+    def _():
+        sweeper = Sweeper(space, faces, gather, listing, aux, outs, work)
+        sweeper.clear_rim()
+        result[...] = added(terms[0][...], terms[1][...]) if len(terms) > 1 else terms[0][...]
+
+        @pl.loop(0, intervals)
+        def _(turn):
+            sweeper.step(result, other, table, 2)
+
+    @pl.when(place.window < least)
+    def _():
+        result[...] = jnp.zeros(result.shape, BF)
+
+
+def final_kernel(space, intervals, width, faces, *refs):
+    near, refs = refs[:intervals], refs[intervals:]
+    earlier, inner, residual, start, forcing = refs[:5]
+    fine_table, coarse_table, gather, listing, aux = refs[5:10]
+    pieces = refs[10 : 10 + space]
+    before, states, other, outs, work = refs[10 + space :]
     place = Place(space, intervals)
 
     @pl.when(place.active)
     def _():
         sweeper = Sweeper(space, faces, gather, listing, aux, outs, work)
         sweeper.clear_rim()
-        result[...] = terms[0][...]
-        for term in terms[1:]:
-            advance(sweeper, result, other, table, 1, term)
-
-
-def far_kernel(space, intervals, faces, *refs):
-    *terms, table, gather, listing, aux, result, other, outs, work = refs
-    place = Place(space, intervals)
-
-    @pl.when(place.active)
-    def _():
-        sweeper = Sweeper(space, faces, gather, listing, aux, outs, work)
-        sweeper.clear_rim()
-        result[...] = sum_of(terms)
-        advance(sweeper, result, other, table, intervals)
-
-
-def sum_of(terms):
-    total = terms[0][...]
-    for term in terms[1:]:
-        total = (total.astype(F32) + term[...].astype(F32)).astype(BF)
-    return total
-
-
-def final_kernel(space, intervals, width, faces, *refs):
-    earlier, inner, partial, residual, start, forcing = refs[:6]
-    fine_table, coarse_table, gather, listing, aux = refs[6:11]
-    pieces = refs[11 : 11 + space]
-    before, states, other, outs, work = refs[11 + space :]
-    place = Place(space, intervals)
-
-    @pl.when(place.active)
-    def _():
-        sweeper = Sweeper(space, faces, gather, listing, aux, outs, work)
-        sweeper.clear_rim()
-        before[...] = sum_of([earlier, inner])
-        advance(sweeper, before, other, coarse_table, intervals, partial)
+        before[...] = added(earlier[...], inner[...])
+        horner(sweeper, before, other, coarse_table, near, place.number - intervals - 1)
         last = COARSEN - 1
         state = states.at[last]
         state[...] = before[...]
@@ -280,7 +327,7 @@
                 states[index + 1] = now[...]
 
         for turn in range(space):
-            part = lax.rem(place.position + turn, space)
+            part = place.away(turn)
             for index in range(COARSEN):
                 pieces[turn][index] = states[index, part][:width]
 
@@ -292,7 +339,8 @@
     place = Place(space, intervals)
     offset = lax.rem(lax.rem(place.window, 2), stride)
     for interval in range(intervals):
-        wanted = lax.rem(place.position - offset - interval * stride + 2 * space, space)
+        host = interval * stride + offset
+        wanted = lax.rem(place.sign * (place.position - host) + 2 * space, space)
         for turn in range(space):
 
             @pl.when(wanted == turn)
@@ -333,25 +381,34 @@
     params = pltpu.CompilerParams(vmem_limit_bytes=min(56, 2 * space) * MIB)
     state_shape = jax.ShapeDtypeStruct((space, ROWS, LANES), BF)
 
+    hbm = pl.BlockSpec(memory_space=pltpu.HBM)
+    packing = [forcing, initial, damping[None], send_index[None], conn]
     message_shape = jax.ShapeDtypeStruct((COARSEN + 1, ROWS, LANES), BF)
     messages = pl.pallas_call(
         functools.partial(pack_kernel, space, intervals),
         out_shape=[message_shape] * intervals,
-        in_specs=[VMEM] * 3 + [pl.BlockSpec(memory_space=pltpu.SMEM)] + [VMEM] * 2,
-        out_specs=[VMEM] * intervals,
-        compiler_params=params,
+        in_specs=[pl.BlockSpec(memory_space=pltpu.SMEM)] + [hbm] * 5,
+        out_specs=[hbm] * intervals,
+        scratch_shapes=[pltpu.VMEM(array.shape, array.dtype) for array in packing]
+        + [
+            pltpu.VMEM((intervals, COARSEN + 1, ROWS, LANES), BF),
+            pltpu.SemaphoreType.DMA((5,)),
+            pltpu.SemaphoreType.DMA((intervals,)),
+        ],
+        compiler_params=pltpu.CompilerParams(vmem_limit_bytes=60 * MIB),
         name="pack",
-    )(forcing, initial, damping[None], etype, send_index[None], conn)
-
-    received = [messages[0]]
-    for turn in range(1, space):
+    )(etype, *packing)
+
+    received = [messages[0]] * space
+    turns = sorted(range(1, space), key=lambda turn: turn % stride == 0)
+    for turn in turns:
         pairs = []
         for window in range(windows):
             for interval in range(intervals):
                 host = host_of(window, interval, space, intervals)
-                source = (host - turn) % space
+                source = away(host, turn, window, space)
                 pairs.append((window * space + source, window * space + host))
-        received.append(lax.ppermute(messages[turn // stride], ("tm", "space"), pairs))
+        received[turn] = lax.ppermute(messages[turn // stride], ("tm", "space"), pairs)
 
     table_shape = jax.ShapeDtypeStruct((ROWS + PROWS, (faces + 1) * ROWS), BF)
     fine_table, coarse_table = pl.pallas_call(
@@ -364,7 +421,7 @@
         name="fold",
     )(block_inv, coarse_inv, coupling)
 
-    gather_shape = jax.ShapeDtypeStruct((space, 2 * LANES, faces * LANES), BF)
+    gather_shape = jax.ShapeDtypeStruct((space, 2 * LANES, (faces - PICKED) * LANES), BF)
     listing_shape = jax.ShapeDtypeStruct((space // 2, 2 * LANES, 2 * LANES), BF)
     aux_shape = jax.ShapeDtypeStruct((space, 8, LANES), F32)
     forcing_shape = jax.ShapeDtypeStruct((space, COARSEN, ROWS, LANES), BF)
@@ -396,9 +453,9 @@
             )
         return lax.ppermute(value, ("tm", "space"), pairs)
 
-    def chain(kernel, terms, name):
+    def chain(kernel, number, terms, name):
         return pl.pallas_call(
-            functools.partial(kernel, space, intervals, faces),
+            functools.partial(kernel, space, intervals, number, faces),
             out_shape=state_shape,
             in_specs=[VMEM] * (len(terms) + 4),
             out_specs=VMEM,
@@ -408,19 +465,19 @@
         )(*terms, coarse_table, gather, listing, aux)
 
     near = [from_earlier(residual, by) for by in range(intervals, 0, -1)]
-    partial = chain(near_kernel, near, "near")
+    partial = chain(near_kernel, windows, near, "near")
     earlier, *inner = [
         from_earlier(partial, by * intervals) for by in range(windows - 1, 0, -1)
     ]
-    earlier = chain(far_kernel, [earlier], "far")
-    for term in inner[:-1]:
-        earlier = chain(far_kernel, [earlier, term], "far")
+    earlier = chain(far_kernel, windows - 1, [earlier], "far")
+    for index, term in enumerate(inner[:-1]):
+        earlier = chain(far_kernel, windows - 2 - index, [earlier, term], "far")
 
     piece_shape = jax.ShapeDtypeStruct((COARSEN, width, LANES), BF)
     pieces = pl.pallas_call(
         functools.partial(final_kernel, space, intervals, width, faces),
         out_shape=[piece_shape] * space,
-        in_specs=[VMEM] * 11,
+        in_specs=[VMEM] * (intervals + 10),
         out_specs=[VMEM] * space,
         scratch_shapes=[
             pltpu.VMEM((space, ROWS, LANES), BF),
@@ -430,9 +487,9 @@
         compiler_params=params,
         name="final",
     )(
+        *near,
         earlier,
         inner[-1],
-        partial,
         residual,
         start,
         whole_forcing,
@@ -443,14 +500,15 @@
         aux,
     )
 
-    returned = [pieces[0]]
-    for turn in range(1, space):
+    returned = [pieces[0]] * space
+    for turn in turns:
         pairs = []
         for window in range(windows):
             for interval in range(intervals):
                 host = host_of(window, interval, space, intervals)
-                pairs.append((window * space + host, window * space + (host + turn) % space))
-        returned.append(lax.ppermute(pieces[turn], ("tm", "space"), pairs))
+                target = away(host, turn, window, space)
+                pairs.append((window * space + host, window * space + target))
+        returned[turn] = lax.ppermute(pieces[turn], ("tm", "space"), pairs)
 
     return pl.pallas_call(
         functools.partial(gather_kernel, space, intervals),

time: 144 us -> 131 us (0.910)
  waiting for transfers between devices: 104 us -> 91.2 us
  local copies, waits for them, and re-layouts: 7.68 us -> 5.67 us
  Pallas kernels: 2.28 us -> 4.08 us
    ppermute x7, waiting for transfers between devices: 104 us -> 89.7 us  [shards(): returned[turn] = lax.ppermute(pieces[turn], ('tm', 'space'), pairs)]
    unnamed x13 -> x7, local copies, waits for them, and re-layouts: 6.8 us -> 4.79 us
    pallas_call x1, Pallas kernels: 0.09 us -> 2.08 us  [shards(): pl.pallas_call(functools.partial(pack_kernel, space, intervals), out_shap...]
  transfers between devices with their start and end apart: 21 -> 21, of which waited for: 4 -> 5; matrix products, arithmetic and copies ran while one was open for 1% -> 1% of each run, Pallas kernels for 1% -> 1%
where the time goes in v3:
time: 131 us; the launch traced here: 129 us
  waiting for transfers between devices  91.2 us (70%)
  starting transfers between devices  26.7 us (20%)
  local copies, waits for them, and re-layouts  5.67 us (4%)
  Pallas kernels  4.08 us (3%)
    ppermute x7, waiting for transfers between devices, shards(): returned[turn] = lax.ppermute(pieces[turn], ('tm', 'space'), pairs)  89.7 us
    ppermute x7, starting transfers between devices, shards(): lax.ppermute(messages[turn // stride], ('tm', 'space'), pairs)  14.8 us
    ppermute x7, starting transfers between devices, shards(): returned[turn] = lax.ppermute(pieces[turn], ('tm', 'space'), pairs)  7.17 us
    unnamed x7, local copies, waits for them, and re-layouts  4.79 us
    ppermute x7, starting transfers between devices, from_earlier(): return lax.ppermute(value, ('tm', 'space'), pairs)  4.74 us
  transfers between devices with their start and end apart: 21, of which 5 were waited for; matrix products, arithmetic and copies ran while one was open for 1% of the time, Pallas kernels for 1%

profile of v3, /device:TPU:6, one launch (start us, length us, event | category | flops | bytes accessed | tf_op | source)
XLA Modules:
  0.0 128.7 jit_solution(15054830586630431988)
XLA Ops:
  0.7 2.0 %copy.10.refs_0_ = bf16[16,135,128]{2,1,0:T(8,128)(2,1)} copy(bf16[16,135,128]{2,0,1:T(8,128)(2,1)} %param.10) | data formatting | bytes 1105920 | tf_op args[1]
  2.7 2.1 %pack.1 = (bf16[5,144,128]{2,1,0:T(8,128)(2,1)}, bf16[5,144,128]{2,1,0:T(8,128)(2,1)}, bf16[5,144,128]{2,1,0:T(8,128)(2,1)}, bf16[5,144,128]{2,1,0:T(8,128)(2,1)}) custom-call(s32[1]{0:T(128)S(6)} %copy.14.etype, bf16[16,135,128]{2,1,0:T(8,128)(2,1)} %copy.10.refs_0_, bf16[135,128]{1,0:T(8,128)(2,1)} %refs_1_.1, f32[1,128]{1,0:T(1,128)} %bitcast.2, ...), custom_call_target="tpu_custom_call" | custom-call | tf_op jit(solution)/shard_map/pack/pallas_call | solution.py:387
  4.8 2.4 %collective-permute-start = (bf16[5,144,128]{2,1,0:T(8,128)(2,1)}, bf16[5,144,128]{2,1,0:T(8,128)(2,1)S(1)}, u32[]{:S(2)}, u32[]{:S(2)}) collective-permute-start(bf16[5,144,128]{2,1,0:T(8,128)(2,1)} %get-tuple-element.25.refs_0_), channel_id=1, source_target_pairs={{1,0},{3,2},{5,4},{7,6},{8,9},{10,11},{12,13},{14,15},{17,16},{19,... | collective-permute-start | bytes 552968 | tf_op jit(solution)/shard_map/ppermute | solution.py:411
  7.2 4.3 %collective-permute-start.2 = (bf16[5,144,128]{2,1,0:T(8,128)(2,1)}, bf16[5,144,128]{2,1,0:T(8,128)(2,1)S(1)}, u32[]{:S(2)}, u32[]{:S(2)}) collective-permute-start(bf16[5,144,128]{2,1,0:T(8,128)(2,1)} %get-tuple-element.26), channel_id=1, source_target_pairs={{3,0},{5,2},{7,4},{1,6},{14,9},{8,11},{10,13},{12,15},{19,16},{21,... | collective-permute-start | bytes 552968 | tf_op jit(solution)/shard_map/ppermute | solution.py:411
  11.6 0.7 collective-permute-start.1
  12.3 2.0 %collective-permute-start.4 = (bf16[5,144,128]{2,1,0:T(8,128)(2,1)}, bf16[5,144,128]{2,1,0:T(8,128)(2,1)S(1)}, u32[]{:S(2)}, u32[]{:S(2)}) collective-permute-start(bf16[5,144,128]{2,1,0:T(8,128)(2,1)} %get-tuple-element.27), channel_id=1, source_target_pairs={{5,0},{7,2},{1,4},{3,6},{12,9},{14,11},{8,13},{10,15},{21,16},{23,... | collective-permute-start | bytes 552968 | tf_op jit(solution)/shard_map/ppermute | solution.py:411
  14.2 0.7 collective-permute-start.3
  14.9 0.0 collective-permute-done.refs_1_
  14.9 4.1 %collective-permute-start.6 = (bf16[5,144,128]{2,1,0:T(8,128)(2,1)}, bf16[5,144,128]{2,1,0:T(8,128)(2,1)S(1)}, u32[]{:S(2)}, u32[]{:S(2)}) collective-permute-start(bf16[5,144,128]{2,1,0:T(8,128)(2,1)} %get-tuple-element.28), channel_id=1, source_target_pairs={{7,0},{1,2},{3,4},{5,6},{10,9},{12,11},{14,13},{8,15},{23,16},{17,... | collective-permute-start | bytes 552968 | tf_op jit(solution)/shard_map/ppermute | solution.py:411
  19.0 0.0 collective-permute-done.2.refs_3_
  19.0 0.7 collective-permute-start.5
  19.7 0.9 copy.11.fine
  20.6 0.9 copy.12.coarse
  21.6 0.8 fold.1
  22.4 0.0 collective-permute-done.1.refs_2_
  22.4 0.0 collective-permute-done.4.refs_5_
  22.4 0.0 collective-permute-done.3.refs_4_
  22.4 1.4 %collective-permute-done.6.refs_7_ = bf16[5,144,128]{2,1,0:T(8,128)(2,1)S(1)} collective-permute-done((bf16[5,144,128]{2,1,0:T(8,128)(2,1)}, bf16[5,144,128]{2,1,0:T(8,128)(2,1)S(1)}, u32[]{:S(2)}, u32[]{:S(2)}) %collective-permute-start.6) | collective-permute-done | bytes 184352 | tf_op jit(solution)/shard_map/ppermute | solution.py:411
  23.8 0.0 collective-permute-done.5.refs_6_
  23.8 0.9 copy-done.1
  24.8 0.7 collective-permute-start.10
  25.4 0.7 collective-permute-start.9
  26.1 0.7 collective-permute-start.8
  26.8 0.7 collective-permute-start.7
  27.5 0.0 collective-permute-done.10.refs_3_
  27.5 0.0 collective-permute-done.9.refs_2_
  27.5 0.0 collective-permute-done.8.refs_1_
  27.5 0.0 collective-permute-done.7.refs_0_
  27.6 0.7 collective-permute-start.11
  28.3 0.7 collective-permute-start.12
  29.0 0.7 collective-permute-start.13
  29.6 0.0 collective-permute-done.11.refs_0_
  29.7 0.2 far.2.refs_0_
  29.9 0.0 collective-permute-done.12.refs_1_
  30.0 0.0 collective-permute-done.13.refs_5_
  30.0 1.3 %collective-permute-start.14 = (bf16[4,135,128]{2,1,0:T(8,128)(2,1)S(1)}, bf16[4,135,128]{2,1,0:T(8,128)(2,1)S(1)}, u32[]{:S(2)}, u32[]{:S(2)}) collective-permute-start(bf16[4,135,128]{2,1,0:T(8,128)(2,1)S(1)} %get-tuple-element.38), channel_id=1, source_target_pairs={{0,1},{2,3},{4,5},{6,7},{9,8},{11,10},{13,12},{15,14},{16,17},{18,... | collective-permute-start | bytes 414728 | tf_op jit(solution)/shard_map/ppermute | solution.py:511
  31.3 0.7 collective-permute-start.15
  32.0 1.3 %collective-permute-start.16 = (bf16[4,135,128]{2,1,0:T(8,128)(2,1)S(1)}, bf16[4,135,128]{2,1,0:T(8,128)(2,1)S(1)}, u32[]{:S(2)}, u32[]{:S(2)}) collective-permute-start(bf16[4,135,128]{2,1,0:T(8,128)(2,1)S(1)} %get-tuple-element.40), channel_id=1, source_target_pairs={{0,3},{2,5},{4,7},{6,1},{9,14},{11,8},{13,10},{15,12},{16,19},{18,... | collective-permute-start | bytes 414728 | tf_op jit(solution)/shard_map/ppermute | solution.py:511
  33.3 0.7 collective-permute-start.17
  34.0 1.3 %collective-permute-start.18 = (bf16[4,135,128]{2,1,0:T(8,128)(2,1)S(1)}, bf16[4,135,128]{2,1,0:T(8,128)(2,1)S(1)}, u32[]{:S(2)}, u32[]{:S(2)}) collective-permute-start(bf16[4,135,128]{2,1,0:T(8,128)(2,1)S(1)} %get-tuple-element.42), channel_id=1, source_target_pairs={{0,5},{2,7},{4,1},{6,3},{9,12},{11,14},{13,8},{15,10},{16,21},{18,... | collective-permute-start | bytes 414728 | tf_op jit(solution)/shard_map/ppermute | solution.py:511
  35.3 76.0 %collective-permute-done.14.refs_1_ = bf16[4,135,128]{2,1,0:T(8,128)(2,1)S(1)} collective-permute-done((bf16[4,135,128]{2,1,0:T(8,128)(2,1)S(1)}, bf16[4,135,128]{2,1,0:T(8,128)(2,1)S(1)}, u32[]{:S(2)}, u32[]{:S(2)}) %collective-permute-start.14) | collective-permute-done | bytes 138272 | tf_op jit(solution)/shard_map/ppermute | solution.py:511
  111.3 0.7 collective-permute-start.19
  112.0 1.3 %collective-permute-start.20 = (bf16[4,135,128]{2,1,0:T(8,128)(2,1)S(1)}, bf16[4,135,128]{2,1,0:T(8,128)(2,1)S(1)}, u32[]{:S(2)}, u32[]{:S(2)}) collective-permute-start(bf16[4,135,128]{2,1,0:T(8,128)(2,1)S(1)} %get-tuple-element.44), channel_id=1, source_target_pairs={{0,7},{2,1},{4,3},{6,5},{9,10},{11,12},{13,14},{15,8},{16,23},{18,... | collective-permute-start | bytes 414728 | tf_op jit(solution)/shard_map/ppermute | solution.py:511
  113.3 4.7 %collective-permute-done.16.refs_3_ = bf16[4,135,128]{2,1,0:T(8,128)(2,1)S(1)} collective-permute-done((bf16[4,135,128]{2,1,0:T(8,128)(2,1)S(1)}, bf16[4,135,128]{2,1,0:T(8,128)(2,1)S(1)}, u32[]{:S(2)}, u32[]{:S(2)}) %collective-permute-start.16) | collective-permute-done | bytes 138272 | tf_op jit(solution)/shard_map/ppermute | solution.py:511
  118.0 6.0 %collective-permute-done.18.refs_5_ = bf16[4,135,128]{2,1,0:T(8,128)(2,1)S(1)} collective-permute-done((bf16[4,135,128]{2,1,0:T(8,128)(2,1)S(1)}, bf16[4,135,128]{2,1,0:T(8,128)(2,1)S(1)}, u32[]{:S(2)}, u32[]{:S(2)}) %collective-permute-start.18) | collective-permute-done | bytes 138272 | tf_op jit(solution)/shard_map/ppermute | solution.py:511
  124.1 2.9 %collective-permute-done.20.refs_7_ = bf16[4,135,128]{2,1,0:T(8,128)(2,1)S(1)} collective-permute-done((bf16[4,135,128]{2,1,0:T(8,128)(2,1)S(1)}, bf16[4,135,128]{2,1,0:T(8,128)(2,1)S(1)}, u32[]{:S(2)}, u32[]{:S(2)}) %collective-permute-start.20) | collective-permute-done | bytes 138272 | tf_op jit(solution)/shard_map/ppermute | solution.py:511
  126.9 0.9 place.1
  127.8 0.9 copy.13
  (10 shorter events, 0.1 us)
Async XLA Ops:
  0.0 21.6 %copy-start = (bf16[6,135,135]{2,1,0:T(8,128)(2,1)S(1)}, bf16[6,135,135]{2,1,0:T(8,128)(2,1)}, u32[]{:S(2)}) copy-start(bf16[6,135,135]{2,1,0:T(8,128)(2,1)} %coupling.1) | copy-start | bytes 656104
  4.8 10.1 %collective-permute-start = (bf16[5,144,128]{2,1,0:T(8,128)(2,1)}, bf16[5,144,128]{2,1,0:T(8,128)(2,1)S(1)}, u32[]{:S(2)}, u32[]{:S(2)}) collective-permute-start(bf16[5,144,128]{2,1,0:T(8,128)(2,1)} %get-tuple-element.25.refs_0_), channel_id=1, source_target_pairs={{1,0},{3,2},{5,4},{7,6},{8,9},{10,11},{12,13},{14,15},{17,16},{19,... | collective-permute-start | bytes 552968 | tf_op jit(solution)/shard_map/ppermute | solution.py:411
  7.2 11.8 %collective-permute-start.2 = (bf16[5,144,128]{2,1,0:T(8,128)(2,1)}, bf16[5,144,128]{2,1,0:T(8,128)(2,1)S(1)}, u32[]{:S(2)}, u32[]{:S(2)}) collective-permute-start(bf16[5,144,128]{2,1,0:T(8,128)(2,1)} %get-tuple-element.26), channel_id=1, source_target_pairs={{3,0},{5,2},{7,4},{1,6},{14,9},{8,11},{10,13},{12,15},{19,16},{21,... | collective-permute-start | bytes 552968 | tf_op jit(solution)/shard_map/ppermute | solution.py:411
  11.6 10.8 %collective-permute-start.1 = (bf16[5,144,128]{2,1,0:T(8,128)(2,1)}, bf16[5,144,128]{2,1,0:T(8,128)(2,1)S(1)}, u32[]{:S(2)}, u32[]{:S(2)}) collective-permute-start(bf16[5,144,128]{2,1,0:T(8,128)(2,1)} %get-tuple-element.26), channel_id=1, source_target_pairs={{2,0},{4,2},{6,4},{0,6},{15,9},{9,11},{11,13},{13,15},{18,16},{20,... | collective-permute-start | bytes 552968 | tf_op jit(solution)/shard_map/ppermute | solution.py:411
  12.3 10.1 %collective-permute-start.4 = (bf16[5,144,128]{2,1,0:T(8,128)(2,1)}, bf16[5,144,128]{2,1,0:T(8,128)(2,1)S(1)}, u32[]{:S(2)}, u32[]{:S(2)}) collective-permute-start(bf16[5,144,128]{2,1,0:T(8,128)(2,1)} %get-tuple-element.27), channel_id=1, source_target_pairs={{5,0},{7,2},{1,4},{3,6},{12,9},{14,11},{8,13},{10,15},{21,16},{23,... | collective-permute-start | bytes 552968 | tf_op jit(solution)/shard_map/ppermute | solution.py:411
  14.2 8.2 %collective-permute-start.3 = (bf16[5,144,128]{2,1,0:T(8,128)(2,1)}, bf16[5,144,128]{2,1,0:T(8,128)(2,1)S(1)}, u32[]{:S(2)}, u32[]{:S(2)}) collective-permute-start(bf16[5,144,128]{2,1,0:T(8,128)(2,1)} %get-tuple-element.27), channel_id=1, source_target_pairs={{4,0},{6,2},{0,4},{2,6},{13,9},{15,11},{9,13},{11,15},{20,16},{22,... | collective-permute-start | bytes 552968 | tf_op jit(solution)/shard_map/ppermute | solution.py:411
  14.9 8.9 %collective-permute-start.6 = (bf16[5,144,128]{2,1,0:T(8,128)(2,1)}, bf16[5,144,128]{2,1,0:T(8,128)(2,1)S(1)}, u32[]{:S(2)}, u32[]{:S(2)}) collective-permute-start(bf16[5,144,128]{2,1,0:T(8,128)(2,1)} %get-tuple-element.28), channel_id=1, source_target_pairs={{7,0},{1,2},{3,4},{5,6},{10,9},{12,11},{14,13},{8,15},{23,16},{17,... | collective-permute-start | bytes 552968 | tf_op jit(solution)/shard_map/ppermute | solution.py:411
  19.0 4.8 %collective-permute-start.5 = (bf16[5,144,128]{2,1,0:T(8,128)(2,1)}, bf16[5,144,128]{2,1,0:T(8,128)(2,1)S(1)}, u32[]{:S(2)}, u32[]{:S(2)}) collective-permute-start(bf16[5,144,128]{2,1,0:T(8,128)(2,1)} %get-tuple-element.28), channel_id=1, source_target_pairs={{6,0},{0,2},{2,4},{4,6},{11,9},{13,11},{15,13},{9,15},{22,16},{16,... | collective-permute-start | bytes 552968 | tf_op jit(solution)/shard_map/ppermute | solution.py:411
  23.8 0.9 copy-start.1
  24.8 2.7 %collective-permute-start.10 = (bf16[8,144,128]{2,1,0:T(8,128)(2,1)S(1)}, bf16[8,144,128]{2,1,0:T(8,128)(2,1)S(1)}, u32[]{:S(2)}, u32[]{:S(2)}) collective-permute-start(bf16[8,144,128]{2,1,0:T(8,128)(2,1)S(1)} %get-tuple-element.30.refs_6_), channel_id=1, source_target_pairs={{0,2},{2,4},{4,6},{6,9},{9,11},{11,13},{13,15},{15,16},{16,18},{18... | collective-permute-start | bytes 884744 | tf_op jit(solution)/shard_map/ppermute | solution.py:454
  25.4 2.1 %collective-permute-start.9 = (bf16[8,144,128]{2,1,0:T(8,128)(2,1)S(1)}, bf16[8,144,128]{2,1,0:T(8,128)(2,1)S(1)}, u32[]{:S(2)}, u32[]{:S(2)}) collective-permute-start(bf16[8,144,128]{2,1,0:T(8,128)(2,1)S(1)} %get-tuple-element.30.refs_6_), channel_id=1, source_target_pairs={{0,4},{2,6},{4,9},{6,11},{9,13},{11,15},{13,16},{15,18},{16,20},{1... | collective-permute-start | bytes 884744 | tf_op jit(solution)/shard_map/ppermute | solution.py:454
  26.1 1.4 %collective-permute-start.8 = (bf16[8,144,128]{2,1,0:T(8,128)(2,1)S(1)}, bf16[8,144,128]{2,1,0:T(8,128)(2,1)S(1)}, u32[]{:S(2)}, u32[]{:S(2)}) collective-permute-start(bf16[8,144,128]{2,1,0:T(8,128)(2,1)S(1)} %get-tuple-element.30.refs_6_), channel_id=1, source_target_pairs={{0,6},{2,9},{4,11},{6,13},{9,15},{11,16},{13,18},{15,20},{16,22},{... | collective-permute-start | bytes 884744 | tf_op jit(solution)/shard_map/ppermute | solution.py:454
  26.8 0.7 collective-permute-start.7
  27.6 2.1 %collective-permute-start.11 = (bf16[8,144,128]{2,1,0:T(8,128)(2,1)S(1)}, bf16[8,144,128]{2,1,0:T(8,128)(2,1)S(1)}, u32[]{:S(2)}, u32[]{:S(2)}) collective-permute-start(bf16[8,144,128]{2,1,0:T(8,128)(2,1)S(1)} %near.1), channel_id=1, source_target_pairs={{0,25},{2,27},{4,29},{6,31}} | collective-permute-start | bytes 884744 | tf_op jit(solution)/shard_map/ppermute | solution.py:454
  28.3 1.6 %collective-permute-start.12 = (bf16[8,144,128]{2,1,0:T(8,128)(2,1)S(1)}, bf16[8,144,128]{2,1,0:T(8,128)(2,1)S(1)}, u32[]{:S(2)}, u32[]{:S(2)}) collective-permute-start(bf16[8,144,128]{2,1,0:T(8,128)(2,1)S(1)} %near.1), channel_id=1, source_target_pairs={{0,16},{2,18},{4,20},{6,22},{9,25},{11,27},{13,29},{15,31}} | collective-permute-start | bytes 884744 | tf_op jit(solution)/shard_map/ppermute | solution.py:454
  29.0 1.0 collective-permute-start.13
  30.0 81.3 %collective-permute-start.14 = (bf16[4,135,128]{2,1,0:T(8,128)(2,1)S(1)}, bf16[4,135,128]{2,1,0:T(8,128)(2,1)S(1)}, u32[]{:S(2)}, u32[]{:S(2)}) collective-permute-start(bf16[4,135,128]{2,1,0:T(8,128)(2,1)S(1)} %get-tuple-element.38), channel_id=1, source_target_pairs={{0,1},{2,3},{4,5},{6,7},{9,8},{11,10},{13,12},{15,14},{16,17},{18,... | collective-permute-start | bytes 414728 | tf_op jit(solution)/shard_map/ppermute | solution.py:511
  31.3 80.7 %collective-permute-start.15 = (bf16[4,135,128]{2,1,0:T(8,128)(2,1)S(1)}, bf16[4,135,128]{2,1,0:T(8,128)(2,1)S(1)}, u32[]{:S(2)}, u32[]{:S(2)}) collective-permute-start(bf16[4,135,128]{2,1,0:T(8,128)(2,1)S(1)} %get-tuple-element.39), channel_id=1, source_target_pairs={{0,2},{2,4},{4,6},{6,0},{9,15},{11,9},{13,11},{15,13},{16,18},{18,... | collective-permute-start | bytes 414728 | tf_op jit(solution)/shard_map/ppermute | solution.py:511
  32.0 86.0 %collective-permute-start.16 = (bf16[4,135,128]{2,1,0:T(8,128)(2,1)S(1)}, bf16[4,135,128]{2,1,0:T(8,128)(2,1)S(1)}, u32[]{:S(2)}, u32[]{:S(2)}) collective-permute-start(bf16[4,135,128]{2,1,0:T(8,128)(2,1)S(1)} %get-tuple-element.40), channel_id=1, source_target_pairs={{0,3},{2,5},{4,7},{6,1},{9,14},{11,8},{13,10},{15,12},{16,19},{18,... | collective-permute-start | bytes 414728 | tf_op jit(solution)/shard_map/ppermute | solution.py:511
  33.3 84.7 %collective-permute-start.17 = (bf16[4,135,128]{2,1,0:T(8,128)(2,1)S(1)}, bf16[4,135,128]{2,1,0:T(8,128)(2,1)S(1)}, u32[]{:S(2)}, u32[]{:S(2)}) collective-permute-start(bf16[4,135,128]{2,1,0:T(8,128)(2,1)S(1)} %get-tuple-element.41), channel_id=1, source_target_pairs={{0,4},{2,6},{4,0},{6,2},{9,13},{11,15},{13,9},{15,11},{16,20},{18,... | collective-permute-start | bytes 414728 | tf_op jit(solution)/shard_map/ppermute | solution.py:511
  34.0 90.1 %collective-permute-start.18 = (bf16[4,135,128]{2,1,0:T(8,128)(2,1)S(1)}, bf16[4,135,128]{2,1,0:T(8,128)(2,1)S(1)}, u32[]{:S(2)}, u32[]{:S(2)}) collective-permute-start(bf16[4,135,128]{2,1,0:T(8,128)(2,1)S(1)} %get-tuple-element.42), channel_id=1, source_target_pairs={{0,5},{2,7},{4,1},{6,3},{9,12},{11,14},{13,8},{15,10},{16,21},{18,... | collective-permute-start | bytes 414728 | tf_op jit(solution)/shard_map/ppermute | solution.py:511
  111.3 12.7 %collective-permute-start.19 = (bf16[4,135,128]{2,1,0:T(8,128)(2,1)S(1)}, bf16[4,135,128]{2,1,0:T(8,128)(2,1)S(1)}, u32[]{:S(2)}, u32[]{:S(2)}) collective-permute-start(bf16[4,135,128]{2,1,0:T(8,128)(2,1)S(1)} %get-tuple-element.43), channel_id=1, source_target_pairs={{0,6},{2,0},{4,2},{6,4},{9,11},{11,13},{13,15},{15,9},{16,22},{18,... | collective-permute-start | bytes 414728 | tf_op jit(solution)/shard_map/ppermute | solution.py:511
  112.0 14.9 %collective-permute-start.20 = (bf16[4,135,128]{2,1,0:T(8,128)(2,1)S(1)}, bf16[4,135,128]{2,1,0:T(8,128)(2,1)S(1)}, u32[]{:S(2)}, u32[]{:S(2)}) collective-permute-start(bf16[4,135,128]{2,1,0:T(8,128)(2,1)S(1)} %get-tuple-element.44), channel_id=1, source_target_pairs={{0,7},{2,1},{4,3},{6,5},{9,10},{11,12},{13,14},{15,8},{16,23},{18,... | collective-permute-start | bytes 414728 | tf_op jit(solution)/shard_map/ppermute | solution.py:511

commit v4 on v3

--- a/solution.py
+++ b/solution.py
@@ -24,9 +24,18 @@
     return jnp.dot(a, b, preferred_element_type=F32)
 
 
+def rank_of(interval, intervals):
+    return (interval % 2) * (intervals // 2) + interval // 2
+
+
+def interval_at(rank, intervals):
+    half = intervals // 2
+    return lax.rem(rank, half) * 2 + rank // half
+
+
 def host_of(window, interval, space, intervals):
     stride = space // intervals
-    return (interval * stride + (window % 2) % stride) % space
+    return (rank_of(interval, intervals) * stride + (window % 2) % stride) % space
 
 
 def away(host, turn, window, space):
@@ -44,7 +53,7 @@
             self.position - lax.rem(lax.rem(self.window, 2), stride) + space, space
         )
         self.active = lax.rem(shifted, stride) == 0
-        self.interval = shifted // stride
+        self.interval = interval_at(shifted // stride, intervals)
         below = shifted // stride
         above = lax.rem((shifted + stride - 1) // stride, intervals)
         self.nearest = jnp.where(self.sign > 0, below, above)
@@ -155,7 +164,7 @@
 def pack_kernel(space, intervals, etype, *refs):
     sources, refs = refs[:5], refs[5:]
     messages, refs = refs[:intervals], refs[intervals:]
-    held, (packed, in_sem, out_sem) = refs[:5], refs[5:]
+    held, (wide, packed, in_sem, out_sem) = refs[:5], refs[5:]
     arriving = []
     for index in range(5):
         arriving.append(pltpu.make_async_copy(sources[index], held[index], in_sem.at[index]))
@@ -163,6 +172,8 @@
     for copy in arriving:
         copy.wait()
     forcing, initial, damping, send_index, conn = held
+    steps = forcing.shape[1]
+    wide[...] = forcing[...].astype(F32).reshape(wide.shape)
     place = Place(space, intervals)
     width = initial.shape[0]
     faces = conn.shape[0]
@@ -177,10 +188,12 @@
     second = jnp.concatenate(pieces, axis=0)
     leaving = []
     for turn in range(intervals):
-        interval = lax.rem(place.nearest - place.sign * turn + intervals, intervals)
+        rank = lax.rem(place.nearest - place.sign * turn + intervals, intervals)
+        interval = interval_at(rank, intervals)
         out = packed.at[turn]
         for index in range(COARSEN):
-            out[index, :width] = forcing[interval * COARSEN + index]
+            rows = pl.ds(interval * COARSEN + index, width, stride=steps)
+            out[index, :width] = wide[rows, :].astype(BF)
         out[COARSEN, :width] = initial[...]
         out[0, width : width + faces + 2] = first
         out[1, width : width + 3] = second
@@ -339,7 +352,7 @@
     place = Place(space, intervals)
     offset = lax.rem(lax.rem(place.window, 2), stride)
     for interval in range(intervals):
-        host = interval * stride + offset
+        host = rank_of(interval, intervals) * stride + offset
         wanted = lax.rem(place.sign * (place.position - host) + 2 * space, space)
         for turn in range(space):
 
@@ -382,7 +395,7 @@
     state_shape = jax.ShapeDtypeStruct((space, ROWS, LANES), BF)
 
     hbm = pl.BlockSpec(memory_space=pltpu.HBM)
-    packing = [forcing, initial, damping[None], send_index[None], conn]
+    packing = [jnp.transpose(forcing, (1, 0, 2)), initial, damping[None], send_index[None], conn]
     message_shape = jax.ShapeDtypeStruct((COARSEN + 1, ROWS, LANES), BF)
     messages = pl.pallas_call(
         functools.partial(pack_kernel, space, intervals),
@@ -391,6 +404,7 @@
         out_specs=[hbm] * intervals,
         scratch_shapes=[pltpu.VMEM(array.shape, array.dtype) for array in packing]
         + [
+            pltpu.VMEM((width * steps, LANES), F32),
             pltpu.VMEM((intervals, COARSEN + 1, ROWS, LANES), BF),
             pltpu.SemaphoreType.DMA((5,)),
             pltpu.SemaphoreType.DMA((intervals,)),

time: 131 us -> 128 us (0.977)
  waiting for transfers between devices: 91.2 us -> 89.6 us
    unnamed x7 -> x6, local copies, waits for them, and re-layouts: 4.79 us -> 3.77 us
where the time goes in v4:
time: 128 us; the launch traced here: 126 us
  waiting for transfers between devices  89.6 us (70%)
  starting transfers between devices  26.8 us (21%)
  local copies, waits for them, and re-layouts  4.65 us (4%)
  Pallas kernels  4.33 us (3%)
    ppermute x7, waiting for transfers between devices, shards(): returned[turn] = lax.ppermute(pieces[turn], ('tm', 'space'), pairs)  89.1 us
    ppermute x7, starting transfers between devices, shards(): lax.ppermute(messages[turn // stride], ('tm', 'space'), pairs)  14.8 us
    ppermute x7, starting transfers between devices, shards(): returned[turn] = lax.ppermute(pieces[turn], ('tm', 'space'), pairs)  7.17 us
    ppermute x7, starting transfers between devices, from_earlier(): return lax.ppermute(value, ('tm', 'space'), pairs)  4.74 us
    unnamed x6, local copies, waits for them, and re-layouts  3.77 us
  transfers between devices with their start and end apart: 21, of which 5 were waited for; matrix products, arithmetic and copies ran while one was open for 1% of the time, Pallas kernels for 1%

profile of v4, /device:TPU:6, one launch (start us, length us, event | category | flops | bytes accessed | tf_op | source)
XLA Modules:
  0.0 126.4 jit_solution(11363341232332798963)
XLA Ops:
  0.7 2.3 %pack.1 = (bf16[5,144,128]{2,1,0:T(8,128)(2,1)}, bf16[5,144,128]{2,1,0:T(8,128)(2,1)}, bf16[5,144,128]{2,1,0:T(8,128)(2,1)}, bf16[5,144,128]{2,1,0:T(8,128)(2,1)}) custom-call(s32[1]{0:T(128)S(6)} %copy.13.etype, bf16[135,16,128]{2,1,0:T(8,128)(2,1)} %bitcast.3, bf16[135,128]{1,0:T(8,128)(2,1)} %refs_1_.1, f32[1,128]{1,0:T(1,128)} %bitcast.4, ...), custom_call_target="tpu_custom_call" | custom-call | tf_op jit(solution)/shard_map/pack/pallas_call | solution.py:400
  3.0 2.4 %collective-permute-start = (bf16[5,144,128]{2,1,0:T(8,128)(2,1)}, bf16[5,144,128]{2,1,0:T(8,128)(2,1)S(1)}, u32[]{:S(2)}, u32[]{:S(2)}) collective-permute-start(bf16[5,144,128]{2,1,0:T(8,128)(2,1)} %get-tuple-element.25.refs_0_), channel_id=1, source_target_pairs={{1,0},{5,4},{3,2},{7,6},{8,9},{12,13},{10,11},{14,15},{17,16},{21,... | collective-permute-start | bytes 552968 | tf_op jit(solution)/shard_map/ppermute | solution.py:425
  5.4 4.3 %collective-permute-start.2 = (bf16[5,144,128]{2,1,0:T(8,128)(2,1)}, bf16[5,144,128]{2,1,0:T(8,128)(2,1)S(1)}, u32[]{:S(2)}, u32[]{:S(2)}) collective-permute-start(bf16[5,144,128]{2,1,0:T(8,128)(2,1)} %get-tuple-element.26), channel_id=1, source_target_pairs={{3,0},{7,4},{5,2},{1,6},{14,9},{10,13},{8,11},{12,15},{19,16},{23,... | collective-permute-start | bytes 552968 | tf_op jit(solution)/shard_map/ppermute | solution.py:425
  9.7 0.7 collective-permute-start.1
  10.4 2.0 %collective-permute-start.4 = (bf16[5,144,128]{2,1,0:T(8,128)(2,1)}, bf16[5,144,128]{2,1,0:T(8,128)(2,1)S(1)}, u32[]{:S(2)}, u32[]{:S(2)}) collective-permute-start(bf16[5,144,128]{2,1,0:T(8,128)(2,1)} %get-tuple-element.27), channel_id=1, source_target_pairs={{5,0},{1,4},{7,2},{3,6},{12,9},{8,13},{14,11},{10,15},{21,16},{17,... | collective-permute-start | bytes 552968 | tf_op jit(solution)/shard_map/ppermute | solution.py:425
  12.4 0.7 collective-permute-start.3
  13.1 0.0 collective-permute-done.refs_1_
  13.1 4.1 %collective-permute-start.6 = (bf16[5,144,128]{2,1,0:T(8,128)(2,1)}, bf16[5,144,128]{2,1,0:T(8,128)(2,1)S(1)}, u32[]{:S(2)}, u32[]{:S(2)}) collective-permute-start(bf16[5,144,128]{2,1,0:T(8,128)(2,1)} %get-tuple-element.28), channel_id=1, source_target_pairs={{7,0},{3,4},{1,2},{5,6},{10,9},{14,13},{12,11},{8,15},{23,16},{19,... | collective-permute-start | bytes 552968 | tf_op jit(solution)/shard_map/ppermute | solution.py:425
  17.2 0.0 collective-permute-done.2.refs_3_
  17.2 0.7 collective-permute-start.5
  17.9 0.9 copy.10.fine
  18.8 0.9 copy.11.coarse
  19.8 0.0 copy-start
  19.8 1.0 copy-done
  20.8 0.8 fold.1
  21.5 0.0 collective-permute-done.1.refs_2_
  21.5 0.0 collective-permute-done.4.refs_5_
  21.6 0.0 collective-permute-done.3.refs_4_
  21.6 0.4 collective-permute-done.6.refs_7_
  22.0 0.0 collective-permute-done.5.refs_6_
  22.0 0.9 copy-done.1
  22.9 0.7 collective-permute-start.10
  23.6 0.7 collective-permute-start.9
  24.3 0.7 collective-permute-start.8
  25.0 0.7 collective-permute-start.7
  25.7 0.0 collective-permute-done.10.refs_3_
  25.7 0.0 collective-permute-done.9.refs_2_
  25.7 0.0 collective-permute-done.8.refs_1_
  25.8 0.7 collective-permute-start.11
  26.5 0.7 collective-permute-start.12
  27.1 0.7 collective-permute-start.13
  27.8 0.2 far.2.refs_0_
  28.1 0.0 collective-permute-done.12.refs_1_
  28.2 1.3 %collective-permute-start.14 = (bf16[4,135,128]{2,1,0:T(8,128)(2,1)S(1)}, bf16[4,135,128]{2,1,0:T(8,128)(2,1)S(1)}, u32[]{:S(2)}, u32[]{:S(2)}) collective-permute-start(bf16[4,135,128]{2,1,0:T(8,128)(2,1)S(1)} %get-tuple-element.38), channel_id=1, source_target_pairs={{0,1},{4,5},{2,3},{6,7},{9,8},{13,12},{11,10},{15,14},{16,17},{20,... | collective-permute-start | bytes 414728 | tf_op jit(solution)/shard_map/ppermute | solution.py:525
  29.5 0.7 collective-permute-start.15
  30.2 1.3 %collective-permute-start.16 = (bf16[4,135,128]{2,1,0:T(8,128)(2,1)S(1)}, bf16[4,135,128]{2,1,0:T(8,128)(2,1)S(1)}, u32[]{:S(2)}, u32[]{:S(2)}) collective-permute-start(bf16[4,135,128]{2,1,0:T(8,128)(2,1)S(1)} %get-tuple-element.40), channel_id=1, source_target_pairs={{0,3},{4,7},{2,5},{6,1},{9,14},{13,10},{11,8},{15,12},{16,19},{20,... | collective-permute-start | bytes 414728 | tf_op jit(solution)/shard_map/ppermute | solution.py:525
  31.5 0.7 collective-permute-start.17
  32.2 1.3 %collective-permute-start.18 = (bf16[4,135,128]{2,1,0:T(8,128)(2,1)S(1)}, bf16[4,135,128]{2,1,0:T(8,128)(2,1)S(1)}, u32[]{:S(2)}, u32[]{:S(2)}) collective-permute-start(bf16[4,135,128]{2,1,0:T(8,128)(2,1)S(1)} %get-tuple-element.42), channel_id=1, source_target_pairs={{0,5},{4,1},{2,7},{6,3},{9,12},{13,8},{11,14},{15,10},{16,21},{20,... | collective-permute-start | bytes 414728 | tf_op jit(solution)/shard_map/ppermute | solution.py:525
  33.5 75.5 %collective-permute-done.14.refs_1_ = bf16[4,135,128]{2,1,0:T(8,128)(2,1)S(1)} collective-permute-done((bf16[4,135,128]{2,1,0:T(8,128)(2,1)S(1)}, bf16[4,135,128]{2,1,0:T(8,128)(2,1)S(1)}, u32[]{:S(2)}, u32[]{:S(2)}) %collective-permute-start.14) | collective-permute-done | bytes 138272 | tf_op jit(solution)/shard_map/ppermute | solution.py:525
  108.9 0.7 collective-permute-start.19
  109.6 0.0 collective-permute-done.15.refs_2_
  109.6 1.3 %collective-permute-start.20 = (bf16[4,135,128]{2,1,0:T(8,128)(2,1)S(1)}, bf16[4,135,128]{2,1,0:T(8,128)(2,1)S(1)}, u32[]{:S(2)}, u32[]{:S(2)}) collective-permute-start(bf16[4,135,128]{2,1,0:T(8,128)(2,1)S(1)} %get-tuple-element.44), channel_id=1, source_target_pairs={{0,7},{4,3},{2,1},{6,5},{9,10},{13,14},{11,12},{15,8},{16,23},{20,... | collective-permute-start | bytes 414728 | tf_op jit(solution)/shard_map/ppermute | solution.py:525
  110.9 4.8 %collective-permute-done.16.refs_3_ = bf16[4,135,128]{2,1,0:T(8,128)(2,1)S(1)} collective-permute-done((bf16[4,135,128]{2,1,0:T(8,128)(2,1)S(1)}, bf16[4,135,128]{2,1,0:T(8,128)(2,1)S(1)}, u32[]{:S(2)}, u32[]{:S(2)}) %collective-permute-start.16) | collective-permute-done | bytes 138272 | tf_op jit(solution)/shard_map/ppermute | solution.py:525
  115.7 6.0 %collective-permute-done.18.refs_5_ = bf16[4,135,128]{2,1,0:T(8,128)(2,1)S(1)} collective-permute-done((bf16[4,135,128]{2,1,0:T(8,128)(2,1)S(1)}, bf16[4,135,128]{2,1,0:T(8,128)(2,1)S(1)}, u32[]{:S(2)}, u32[]{:S(2)}) %collective-permute-start.18) | collective-permute-done | bytes 138272 | tf_op jit(solution)/shard_map/ppermute | solution.py:525
  121.7 0.0 collective-permute-done.19.refs_6_
  121.7 2.9 %collective-permute-done.20.refs_7_ = bf16[4,135,128]{2,1,0:T(8,128)(2,1)S(1)} collective-permute-done((bf16[4,135,128]{2,1,0:T(8,128)(2,1)S(1)}, bf16[4,135,128]{2,1,0:T(8,128)(2,1)S(1)}, u32[]{:S(2)}, u32[]{:S(2)}) %collective-permute-start.20) | collective-permute-done | bytes 138272 | tf_op jit(solution)/shard_map/ppermute | solution.py:525
  124.6 0.9 place.1
  125.5 0.9 copy.12
  (9 shorter events, 0.1 us)
Async XLA Ops:
  3.0 10.1 %collective-permute-start = (bf16[5,144,128]{2,1,0:T(8,128)(2,1)}, bf16[5,144,128]{2,1,0:T(8,128)(2,1)S(1)}, u32[]{:S(2)}, u32[]{:S(2)}) collective-permute-start(bf16[5,144,128]{2,1,0:T(8,128)(2,1)} %get-tuple-element.25.refs_0_), channel_id=1, source_target_pairs={{1,0},{5,4},{3,2},{7,6},{8,9},{12,13},{10,11},{14,15},{17,16},{21,... | collective-permute-start | bytes 552968 | tf_op jit(solution)/shard_map/ppermute | solution.py:425
  5.4 11.8 %collective-permute-start.2 = (bf16[5,144,128]{2,1,0:T(8,128)(2,1)}, bf16[5,144,128]{2,1,0:T(8,128)(2,1)S(1)}, u32[]{:S(2)}, u32[]{:S(2)}) collective-permute-start(bf16[5,144,128]{2,1,0:T(8,128)(2,1)} %get-tuple-element.26), channel_id=1, source_target_pairs={{3,0},{7,4},{5,2},{1,6},{14,9},{10,13},{8,11},{12,15},{19,16},{23,... | collective-permute-start | bytes 552968 | tf_op jit(solution)/shard_map/ppermute | solution.py:425
  9.7 11.8 %collective-permute-start.1 = (bf16[5,144,128]{2,1,0:T(8,128)(2,1)}, bf16[5,144,128]{2,1,0:T(8,128)(2,1)S(1)}, u32[]{:S(2)}, u32[]{:S(2)}) collective-permute-start(bf16[5,144,128]{2,1,0:T(8,128)(2,1)} %get-tuple-element.26), channel_id=1, source_target_pairs={{2,0},{6,4},{4,2},{0,6},{15,9},{11,13},{9,11},{13,15},{18,16},{22,... | collective-permute-start | bytes 552968 | tf_op jit(solution)/shard_map/ppermute | solution.py:425
  10.4 11.1 %collective-permute-start.4 = (bf16[5,144,128]{2,1,0:T(8,128)(2,1)}, bf16[5,144,128]{2,1,0:T(8,128)(2,1)S(1)}, u32[]{:S(2)}, u32[]{:S(2)}) collective-permute-start(bf16[5,144,128]{2,1,0:T(8,128)(2,1)} %get-tuple-element.27), channel_id=1, source_target_pairs={{5,0},{1,4},{7,2},{3,6},{12,9},{8,13},{14,11},{10,15},{21,16},{17,... | collective-permute-start | bytes 552968 | tf_op jit(solution)/shard_map/ppermute | solution.py:425
  12.4 9.2 %collective-permute-start.3 = (bf16[5,144,128]{2,1,0:T(8,128)(2,1)}, bf16[5,144,128]{2,1,0:T(8,128)(2,1)S(1)}, u32[]{:S(2)}, u32[]{:S(2)}) collective-permute-start(bf16[5,144,128]{2,1,0:T(8,128)(2,1)} %get-tuple-element.27), channel_id=1, source_target_pairs={{4,0},{0,4},{6,2},{2,6},{13,9},{9,13},{15,11},{11,15},{20,16},{16,... | collective-permute-start | bytes 552968 | tf_op jit(solution)/shard_map/ppermute | solution.py:425
  13.1 8.9 %collective-permute-start.6 = (bf16[5,144,128]{2,1,0:T(8,128)(2,1)}, bf16[5,144,128]{2,1,0:T(8,128)(2,1)S(1)}, u32[]{:S(2)}, u32[]{:S(2)}) collective-permute-start(bf16[5,144,128]{2,1,0:T(8,128)(2,1)} %get-tuple-element.28), channel_id=1, source_target_pairs={{7,0},{3,4},{1,2},{5,6},{10,9},{14,13},{12,11},{8,15},{23,16},{19,... | collective-permute-start | bytes 552968 | tf_op jit(solution)/shard_map/ppermute | solution.py:425
  17.2 4.8 %collective-permute-start.5 = (bf16[5,144,128]{2,1,0:T(8,128)(2,1)}, bf16[5,144,128]{2,1,0:T(8,128)(2,1)S(1)}, u32[]{:S(2)}, u32[]{:S(2)}) collective-permute-start(bf16[5,144,128]{2,1,0:T(8,128)(2,1)} %get-tuple-element.28), channel_id=1, source_target_pairs={{6,0},{2,4},{0,2},{4,6},{11,9},{15,13},{13,11},{9,15},{22,16},{18,... | collective-permute-start | bytes 552968 | tf_op jit(solution)/shard_map/ppermute | solution.py:425
  19.8 1.0 copy-start
  22.0 0.9 copy-start.1
  22.9 2.7 %collective-permute-start.10 = (bf16[8,144,128]{2,1,0:T(8,128)(2,1)S(1)}, bf16[8,144,128]{2,1,0:T(8,128)(2,1)S(1)}, u32[]{:S(2)}, u32[]{:S(2)}) collective-permute-start(bf16[8,144,128]{2,1,0:T(8,128)(2,1)S(1)} %get-tuple-element.30.refs_6_), channel_id=1, source_target_pairs={{0,4},{4,2},{2,6},{6,9},{9,13},{13,11},{11,15},{15,16},{16,20},{20... | collective-permute-start | bytes 884744 | tf_op jit(solution)/shard_map/ppermute | solution.py:468
  23.6 2.1 %collective-permute-start.9 = (bf16[8,144,128]{2,1,0:T(8,128)(2,1)S(1)}, bf16[8,144,128]{2,1,0:T(8,128)(2,1)S(1)}, u32[]{:S(2)}, u32[]{:S(2)}) collective-permute-start(bf16[8,144,128]{2,1,0:T(8,128)(2,1)S(1)} %get-tuple-element.30.refs_6_), channel_id=1, source_target_pairs={{0,2},{4,6},{2,9},{6,13},{9,11},{13,15},{11,16},{15,20},{16,18},{2... | collective-permute-start | bytes 884744 | tf_op jit(solution)/shard_map/ppermute | solution.py:468
  24.3 1.4 %collective-permute-start.8 = (bf16[8,144,128]{2,1,0:T(8,128)(2,1)S(1)}, bf16[8,144,128]{2,1,0:T(8,128)(2,1)S(1)}, u32[]{:S(2)}, u32[]{:S(2)}) collective-permute-start(bf16[8,144,128]{2,1,0:T(8,128)(2,1)S(1)} %get-tuple-element.30.refs_6_), channel_id=1, source_target_pairs={{0,6},{4,9},{2,13},{6,11},{9,15},{13,16},{11,20},{15,18},{16,22},{... | collective-permute-start | bytes 884744 | tf_op jit(solution)/shard_map/ppermute | solution.py:468
  25.0 0.7 collective-permute-start.7
  25.8 2.1 %collective-permute-start.11 = (bf16[8,144,128]{2,1,0:T(8,128)(2,1)S(1)}, bf16[8,144,128]{2,1,0:T(8,128)(2,1)S(1)}, u32[]{:S(2)}, u32[]{:S(2)}) collective-permute-start(bf16[8,144,128]{2,1,0:T(8,128)(2,1)S(1)} %near.1), channel_id=1, source_target_pairs={{0,25},{4,29},{2,27},{6,31}} | collective-permute-start | bytes 884744 | tf_op jit(solution)/shard_map/ppermute | solution.py:468
  26.5 1.6 %collective-permute-start.12 = (bf16[8,144,128]{2,1,0:T(8,128)(2,1)S(1)}, bf16[8,144,128]{2,1,0:T(8,128)(2,1)S(1)}, u32[]{:S(2)}, u32[]{:S(2)}) collective-permute-start(bf16[8,144,128]{2,1,0:T(8,128)(2,1)S(1)} %near.1), channel_id=1, source_target_pairs={{0,16},{4,20},{2,18},{6,22},{9,25},{13,29},{11,27},{15,31}} | collective-permute-start | bytes 884744 | tf_op jit(solution)/shard_map/ppermute | solution.py:468
  27.1 1.0 collective-permute-start.13
  28.2 80.7 %collective-permute-start.14 = (bf16[4,135,128]{2,1,0:T(8,128)(2,1)S(1)}, bf16[4,135,128]{2,1,0:T(8,128)(2,1)S(1)}, u32[]{:S(2)}, u32[]{:S(2)}) collective-permute-start(bf16[4,135,128]{2,1,0:T(8,128)(2,1)S(1)} %get-tuple-element.38), channel_id=1, source_target_pairs={{0,1},{4,5},{2,3},{6,7},{9,8},{13,12},{11,10},{15,14},{16,17},{20,... | collective-permute-start | bytes 414728 | tf_op jit(solution)/shard_map/ppermute | solution.py:525
  29.5 80.1 %collective-permute-start.15 = (bf16[4,135,128]{2,1,0:T(8,128)(2,1)S(1)}, bf16[4,135,128]{2,1,0:T(8,128)(2,1)S(1)}, u32[]{:S(2)}, u32[]{:S(2)}) collective-permute-start(bf16[4,135,128]{2,1,0:T(8,128)(2,1)S(1)} %get-tuple-element.39), channel_id=1, source_target_pairs={{0,2},{4,6},{2,4},{6,0},{9,15},{13,11},{11,9},{15,13},{16,18},{20,... | collective-permute-start | bytes 414728 | tf_op jit(solution)/shard_map/ppermute | solution.py:525
  30.2 85.5 %collective-permute-start.16 = (bf16[4,135,128]{2,1,0:T(8,128)(2,1)S(1)}, bf16[4,135,128]{2,1,0:T(8,128)(2,1)S(1)}, u32[]{:S(2)}, u32[]{:S(2)}) collective-permute-start(bf16[4,135,128]{2,1,0:T(8,128)(2,1)S(1)} %get-tuple-element.40), channel_id=1, source_target_pairs={{0,3},{4,7},{2,5},{6,1},{9,14},{13,10},{11,8},{15,12},{16,19},{20,... | collective-permute-start | bytes 414728 | tf_op jit(solution)/shard_map/ppermute | solution.py:525
  31.5 84.2 %collective-permute-start.17 = (bf16[4,135,128]{2,1,0:T(8,128)(2,1)S(1)}, bf16[4,135,128]{2,1,0:T(8,128)(2,1)S(1)}, u32[]{:S(2)}, u32[]{:S(2)}) collective-permute-start(bf16[4,135,128]{2,1,0:T(8,128)(2,1)S(1)} %get-tuple-element.41), channel_id=1, source_target_pairs={{0,4},{4,0},{2,6},{6,2},{9,13},{13,9},{11,15},{15,11},{16,20},{20,... | collective-permute-start | bytes 414728 | tf_op jit(solution)/shard_map/ppermute | solution.py:525
  32.2 89.5 %collective-permute-start.18 = (bf16[4,135,128]{2,1,0:T(8,128)(2,1)S(1)}, bf16[4,135,128]{2,1,0:T(8,128)(2,1)S(1)}, u32[]{:S(2)}, u32[]{:S(2)}) collective-permute-start(bf16[4,135,128]{2,1,0:T(8,128)(2,1)S(1)} %get-tuple-element.42), channel_id=1, source_target_pairs={{0,5},{4,1},{2,7},{6,3},{9,12},{13,8},{11,14},{15,10},{16,21},{20,... | collective-permute-start | bytes 414728 | tf_op jit(solution)/shard_map/ppermute | solution.py:525
  108.9 12.7 %collective-permute-start.19 = (bf16[4,135,128]{2,1,0:T(8,128)(2,1)S(1)}, bf16[4,135,128]{2,1,0:T(8,128)(2,1)S(1)}, u32[]{:S(2)}, u32[]{:S(2)}) collective-permute-start(bf16[4,135,128]{2,1,0:T(8,128)(2,1)S(1)} %get-tuple-element.43), channel_id=1, source_target_pairs={{0,6},{4,2},{2,0},{6,4},{9,11},{13,15},{11,13},{15,9},{16,22},{20,... | collective-permute-start | bytes 414728 | tf_op jit(solution)/shard_map/ppermute | solution.py:525
  109.6 14.9 %collective-permute-start.20 = (bf16[4,135,128]{2,1,0:T(8,128)(2,1)S(1)}, bf16[4,135,128]{2,1,0:T(8,128)(2,1)S(1)}, u32[]{:S(2)}, u32[]{:S(2)}) collective-permute-start(bf16[4,135,128]{2,1,0:T(8,128)(2,1)S(1)} %get-tuple-element.44), channel_id=1, source_target_pairs={{0,7},{4,3},{2,1},{6,5},{9,10},{13,14},{11,12},{15,8},{16,23},{20,... | collective-permute-start | bytes 414728 | tf_op jit(solution)/shard_map/ppermute | solution.py:525

commit v5 on v4

--- a/solution.py
+++ b/solution.py
@@ -36,6 +36,11 @@
 def host_of(window, interval, space, intervals):
     stride = space // intervals
     return (rank_of(interval, intervals) * stride + (window % 2) % stride) % space
+
+
+def distances(space, intervals):
+    stride = space // intervals
+    return [0] + sorted(range(1, space), key=lambda turn: turn % stride == 0)
 
 
 def away(host, turn, window, space):
@@ -346,7 +351,7 @@
 
 
 def gather_kernel(space, intervals, *refs):
-    pieces = refs[:space]
+    pieces = dict(zip(distances(space, intervals), refs))
     out, sem = refs[space:]
     stride = space // intervals
     place = Place(space, intervals)
@@ -414,8 +419,7 @@
     )(etype, *packing)
 
     received = [messages[0]] * space
-    turns = sorted(range(1, space), key=lambda turn: turn % stride == 0)
-    for turn in turns:
+    for turn in range(1, space):
         pairs = []
         for window in range(windows):
             for interval in range(intervals):
@@ -515,7 +519,8 @@
     )
 
     returned = [pieces[0]] * space
-    for turn in turns:
+    turns = distances(space, intervals)
+    for turn in turns[1:]:
         pairs = []
         for window in range(windows):
             for interval in range(intervals):
@@ -532,7 +537,7 @@
         scratch_shapes=[pltpu.SemaphoreType.DMA((intervals,))],
         compiler_params=params,
         name="place",
-    )(*returned)
+    )(*[returned[turn] for turn in turns])
 
 
 def solution(mesh):

time: 128 us -> 126 us (0.984)
  the two profiles are of different devices: /device:TPU:6 before, /device:TPU:7 now
where the time goes in v5:
time: 126 us; the launch traced here: 125 us
  Pallas kernels  50.6 us (40%)
  starting transfers between devices  40.8 us (32%)
  waiting for transfers between devices  28 us (22%)
  local copies, waits for them, and re-layouts  4.65 us (4%)
    pallas_call x1, Pallas kernels, shards(): pl.pallas_call(functools.partial(final_kernel, space, intervals, width, f...  18.5 us
    pallas_call x3, Pallas kernels, chain(): pl.pallas_call(functools.partial(kernel, space, intervals, number, faces)...  18.3 us
    ppermute x7, waiting for transfers between devices, from_earlier(): return lax.ppermute(value, ('tm', 'space'), pairs)  17.4 us
    ppermute x7, starting transfers between devices, shards(): lax.ppermute(messages[turn // stride], ('tm', 'space'), pairs)  15.6 us
    ppermute x7, starting transfers between devices, shards(): returned[turn] = lax.ppermute(pieces[turn], ('tm', 'space'), pairs)  13.4 us
    ppermute x7, starting transfers between devices, from_earlier(): return lax.ppermute(value, ('tm', 'space'), pairs)  11.8 us
    pallas_call x1, Pallas kernels, shards(): pl.pallas_call(functools.partial(fine_kernel, space, intervals, width, fa...  9.9 us
    ppermute x7, waiting for transfers between devices, shards(): returned[turn] = lax.ppermute(pieces[turn], ('tm', 'space'), pairs)  5.38 us
  transfers between devices with their start and end apart: 21, of which 11 were waited for; matrix products, arithmetic and copies ran while one was open for 1% of the time, Pallas kernels for 15%

profile of v5, /device:TPU:7, one launch (start us, length us, event | category | flops | bytes accessed | tf_op | source)
XLA Modules:
  0.0 125.1 jit_solution(1201772422898906506)
XLA Ops:
  0.7 2.3 %pack.1 = (bf16[5,144,128]{2,1,0:T(8,128)(2,1)}, bf16[5,144,128]{2,1,0:T(8,128)(2,1)}, bf16[5,144,128]{2,1,0:T(8,128)(2,1)}, bf16[5,144,128]{2,1,0:T(8,128)(2,1)}) custom-call(s32[1]{0:T(128)S(6)} %copy.13.etype, bf16[135,16,128]{2,1,0:T(8,128)(2,1)} %bitcast.3, bf16[135,128]{1,0:T(8,128)(2,1)} %refs_1_.1, f32[1,128]{1,0:T(1,128)} %bitcast.4, ...), custom_call_target="tpu_custom_call" | custom-call | tf_op jit(solution)/shard_map/pack/pallas_call | solution.py:405
  3.0 1.3 %collective-permute-start = (bf16[5,144,128]{2,1,0:T(8,128)(2,1)}, bf16[5,144,128]{2,1,0:T(8,128)(2,1)S(1)}, u32[]{:S(2)}, u32[]{:S(2)}) collective-permute-start(bf16[5,144,128]{2,1,0:T(8,128)(2,1)} %get-tuple-element.25.refs_0_), channel_id=1, source_target_pairs={{1,0},{5,4},{3,2},{7,6},{8,9},{12,13},{10,11},{14,15},{17,16},{21,... | collective-permute-start | bytes 552968 | tf_op jit(solution)/shard_map/ppermute | solution.py:429
  4.3 1.3 %collective-permute-start.2 = (bf16[5,144,128]{2,1,0:T(8,128)(2,1)}, bf16[5,144,128]{2,1,0:T(8,128)(2,1)S(1)}, u32[]{:S(2)}, u32[]{:S(2)}) collective-permute-start(bf16[5,144,128]{2,1,0:T(8,128)(2,1)} %get-tuple-element.26), channel_id=1, source_target_pairs={{3,0},{7,4},{5,2},{1,6},{14,9},{10,13},{8,11},{12,15},{19,16},{23,... | collective-permute-start | bytes 552968 | tf_op jit(solution)/shard_map/ppermute | solution.py:429
  5.6 3.2 %collective-permute-start.1 = (bf16[5,144,128]{2,1,0:T(8,128)(2,1)}, bf16[5,144,128]{2,1,0:T(8,128)(2,1)S(1)}, u32[]{:S(2)}, u32[]{:S(2)}) collective-permute-start(bf16[5,144,128]{2,1,0:T(8,128)(2,1)} %get-tuple-element.26), channel_id=1, source_target_pairs={{2,0},{6,4},{4,2},{0,6},{15,9},{11,13},{9,11},{13,15},{18,16},{22,... | collective-permute-start | bytes 552968 | tf_op jit(solution)/shard_map/ppermute | solution.py:429
  8.8 1.3 %collective-permute-start.4 = (bf16[5,144,128]{2,1,0:T(8,128)(2,1)}, bf16[5,144,128]{2,1,0:T(8,128)(2,1)S(1)}, u32[]{:S(2)}, u32[]{:S(2)}) collective-permute-start(bf16[5,144,128]{2,1,0:T(8,128)(2,1)} %get-tuple-element.27), channel_id=1, source_target_pairs={{5,0},{1,4},{7,2},{3,6},{12,9},{8,13},{14,11},{10,15},{21,16},{17,... | collective-permute-start | bytes 552968 | tf_op jit(solution)/shard_map/ppermute | solution.py:429
  10.1 4.2 %collective-permute-start.3 = (bf16[5,144,128]{2,1,0:T(8,128)(2,1)}, bf16[5,144,128]{2,1,0:T(8,128)(2,1)S(1)}, u32[]{:S(2)}, u32[]{:S(2)}) collective-permute-start(bf16[5,144,128]{2,1,0:T(8,128)(2,1)} %get-tuple-element.27), channel_id=1, source_target_pairs={{4,0},{0,4},{6,2},{2,6},{13,9},{9,13},{15,11},{11,15},{20,16},{16,... | collective-permute-start | bytes 552968 | tf_op jit(solution)/shard_map/ppermute | solution.py:429
  14.3 1.3 %collective-permute-start.6 = (bf16[5,144,128]{2,1,0:T(8,128)(2,1)}, bf16[5,144,128]{2,1,0:T(8,128)(2,1)S(1)}, u32[]{:S(2)}, u32[]{:S(2)}) collective-permute-start(bf16[5,144,128]{2,1,0:T(8,128)(2,1)} %get-tuple-element.28), channel_id=1, source_target_pairs={{7,0},{3,4},{1,2},{5,6},{10,9},{14,13},{12,11},{8,15},{23,16},{19,... | collective-permute-start | bytes 552968 | tf_op jit(solution)/shard_map/ppermute | solution.py:429
  15.6 0.0 collective-permute-done.2.refs_3_
  15.6 3.0 %collective-permute-start.5 = (bf16[5,144,128]{2,1,0:T(8,128)(2,1)}, bf16[5,144,128]{2,1,0:T(8,128)(2,1)S(1)}, u32[]{:S(2)}, u32[]{:S(2)}) collective-permute-start(bf16[5,144,128]{2,1,0:T(8,128)(2,1)} %get-tuple-element.28), channel_id=1, source_target_pairs={{6,0},{2,4},{0,2},{4,6},{11,9},{15,13},{13,11},{9,15},{22,16},{18,... | collective-permute-start | bytes 552968 | tf_op jit(solution)/shard_map/ppermute | solution.py:429
  18.6 0.9 copy.10.fine
  19.6 0.9 copy.11.coarse
  20.5 0.0 copy-start
  20.5 1.0 copy-done
  21.5 0.8 fold.1
  22.3 0.9 collective-permute-done.4.refs_5_
  23.2 2.2 %collective-permute-done.3.refs_4_ = bf16[5,144,128]{2,1,0:T(8,128)(2,1)S(1)} collective-permute-done((bf16[5,144,128]{2,1,0:T(8,128)(2,1)}, bf16[5,144,128]{2,1,0:T(8,128)(2,1)S(1)}, u32[]{:S(2)}, u32[]{:S(2)}) %collective-permute-start.3) | collective-permute-done | bytes 184352 | tf_op jit(solution)/shard_map/ppermute | solution.py:429
  25.4 1.7 %collective-permute-done.6.refs_7_ = bf16[5,144,128]{2,1,0:T(8,128)(2,1)S(1)} collective-permute-done((bf16[5,144,128]{2,1,0:T(8,128)(2,1)}, bf16[5,144,128]{2,1,0:T(8,128)(2,1)S(1)}, u32[]{:S(2)}, u32[]{:S(2)}) %collective-permute-start.6) | collective-permute-done | bytes 184352 | tf_op jit(solution)/shard_map/ppermute | solution.py:429
  27.1 0.4 collective-permute-done.5.refs_6_
  27.5 0.9 copy-done.1
  28.5 9.9 %fine.2 = (bf16[8,144,128]{2,1,0:T(8,128)(2,1)S(1)}, bf16[8,256,512]{2,1,0:T(8,128)(2,1)S(1)}, bf16[4,256,256]{2,1,0:T(8,128)(2,1)S(1)}, f32[8,8,128]{2,1,0:T(8,...) custom-call(bf16[5,144,128]{2,1,0:T(8,128)(2,1)S(1)} %copy-done.1, ...), custom_call_target="tpu_custom_call" | custom-call | tf_op jit(solution)/shard_map/fine/pallas_call | solution.py:451
  38.4 1.9 %collective-permute-start.10 = (bf16[8,144,128]{2,1,0:T(8,128)(2,1)S(1)}, bf16[8,144,128]{2,1,0:T(8,128)(2,1)S(1)}, u32[]{:S(2)}, u32[]{:S(2)}) collective-permute-start(bf16[8,144,128]{2,1,0:T(8,128)(2,1)S(1)} %get-tuple-element.30.refs_6_), channel_id=1, source_target_pairs={{0,4},{4,2},{2,6},{6,9},{9,13},{13,11},{11,15},{15,16},{16,20},{20... | collective-permute-start | bytes 884744 | tf_op jit(solution)/shard_map/ppermute | solution.py:472
  40.3 2.8 %collective-permute-start.9 = (bf16[8,144,128]{2,1,0:T(8,128)(2,1)S(1)}, bf16[8,144,128]{2,1,0:T(8,128)(2,1)S(1)}, u32[]{:S(2)}, u32[]{:S(2)}) collective-permute-start(bf16[8,144,128]{2,1,0:T(8,128)(2,1)S(1)} %get-tuple-element.30.refs_6_), channel_id=1, source_target_pairs={{0,2},{4,6},{2,9},{6,13},{9,11},{13,15},{11,16},{15,20},{16,18},{2... | collective-permute-start | bytes 884744 | tf_op jit(solution)/shard_map/ppermute | solution.py:472
  43.1 1.9 %collective-permute-start.8 = (bf16[8,144,128]{2,1,0:T(8,128)(2,1)S(1)}, bf16[8,144,128]{2,1,0:T(8,128)(2,1)S(1)}, u32[]{:S(2)}, u32[]{:S(2)}) collective-permute-start(bf16[8,144,128]{2,1,0:T(8,128)(2,1)S(1)} %get-tuple-element.30.refs_6_), channel_id=1, source_target_pairs={{0,6},{4,9},{2,13},{6,11},{9,15},{13,16},{11,20},{15,18},{16,22},{... | collective-permute-start | bytes 884744 | tf_op jit(solution)/shard_map/ppermute | solution.py:472
  45.0 1.3 %collective-permute-start.7 = (bf16[8,144,128]{2,1,0:T(8,128)(2,1)S(1)}, bf16[8,144,128]{2,1,0:T(8,128)(2,1)S(1)}, u32[]{:S(2)}, u32[]{:S(2)}) collective-permute-start(bf16[8,144,128]{2,1,0:T(8,128)(2,1)S(1)} %get-tuple-element.30.refs_6_), channel_id=1, source_target_pairs={{0,9},{4,13},{2,11},{6,15},{9,16},{13,20},{11,18},{15,22},{16,25},... | collective-permute-start | bytes 884744 | tf_op jit(solution)/shard_map/ppermute | solution.py:472
  46.3 3.0 %collective-permute-done.10.refs_3_ = bf16[8,144,128]{2,1,0:T(8,128)(2,1)S(1)} collective-permute-done((bf16[8,144,128]{2,1,0:T(8,128)(2,1)S(1)}, bf16[8,144,128]{2,1,0:T(8,128)(2,1)S(1)}, u32[]{:S(2)}, u32[]{:S(2)}) %collective-permute-start.10) | collective-permute-done | bytes 294944 | tf_op jit(solution)/shard_map/ppermute | solution.py:472
  49.3 5.2 %collective-permute-done.9.refs_2_ = bf16[8,144,128]{2,1,0:T(8,128)(2,1)S(1)} collective-permute-done((bf16[8,144,128]{2,1,0:T(8,128)(2,1)S(1)}, bf16[8,144,128]{2,1,0:T(8,128)(2,1)S(1)}, u32[]{:S(2)}, u32[]{:S(2)}) %collective-permute-start.9) | collective-permute-done | bytes 294944 | tf_op jit(solution)/shard_map/ppermute | solution.py:472
  54.5 2.3 %collective-permute-done.8.refs_1_ = bf16[8,144,128]{2,1,0:T(8,128)(2,1)S(1)} collective-permute-done((bf16[8,144,128]{2,1,0:T(8,128)(2,1)S(1)}, bf16[8,144,128]{2,1,0:T(8,128)(2,1)S(1)}, u32[]{:S(2)}, u32[]{:S(2)}) %collective-permute-start.8) | collective-permute-done | bytes 294944 | tf_op jit(solution)/shard_map/ppermute | solution.py:472
  56.8 1.9 %collective-permute-done.7.refs_0_ = bf16[8,144,128]{2,1,0:T(8,128)(2,1)S(1)} collective-permute-done((bf16[8,144,128]{2,1,0:T(8,128)(2,1)S(1)}, bf16[8,144,128]{2,1,0:T(8,128)(2,1)S(1)}, u32[]{:S(2)}, u32[]{:S(2)}) %collective-permute-start.7) | collective-permute-done | bytes 294944 | tf_op jit(solution)/shard_map/ppermute | solution.py:472
  58.7 1.3 %collective-permute-start.11 = (bf16[8,144,128]{2,1,0:T(8,128)(2,1)S(1)}, bf16[8,144,128]{2,1,0:T(8,128)(2,1)S(1)}, u32[]{:S(2)}, u32[]{:S(2)}) collective-permute-start(bf16[8,144,128]{2,1,0:T(8,128)(2,1)S(1)} %near.1), channel_id=1, source_target_pairs={{0,25},{4,29},{2,27},{6,31}} | collective-permute-start | bytes 884744 | tf_op jit(solution)/shard_map/ppermute | solution.py:472
  60.0 1.3 %collective-permute-start.12 = (bf16[8,144,128]{2,1,0:T(8,128)(2,1)S(1)}, bf16[8,144,128]{2,1,0:T(8,128)(2,1)S(1)}, u32[]{:S(2)}, u32[]{:S(2)}) collective-permute-start(bf16[8,144,128]{2,1,0:T(8,128)(2,1)S(1)} %near.1), channel_id=1, source_target_pairs={{0,16},{4,20},{2,18},{6,22},{9,25},{13,29},{11,27},{15,31}} | collective-permute-start | bytes 884744 | tf_op jit(solution)/shard_map/ppermute | solution.py:472
  61.3 1.3 %collective-permute-start.13 = (bf16[8,144,128]{2,1,0:T(8,128)(2,1)S(1)}, bf16[8,144,128]{2,1,0:T(8,128)(2,1)S(1)}, u32[]{:S(2)}, u32[]{:S(2)}) collective-permute-start(bf16[8,144,128]{2,1,0:T(8,128)(2,1)S(1)} %near.1), channel_id=1, source_target_pairs={{0,9},{4,13},{2,11},{6,15},{9,16},{13,20},{11,18},{15,22},{16,25},... | collective-permute-start | bytes 884744 | tf_op jit(solution)/shard_map/ppermute | solution.py:472
  62.6 5.0 %collective-permute-done.11.refs_0_ = bf16[8,144,128]{2,1,0:T(8,128)(2,1)S(1)} collective-permute-done((bf16[8,144,128]{2,1,0:T(8,128)(2,1)S(1)}, bf16[8,144,128]{2,1,0:T(8,128)(2,1)S(1)}, u32[]{:S(2)}, u32[]{:S(2)}) %collective-permute-start.11) | collective-permute-done | bytes 294944 | tf_op jit(solution)/shard_map/ppermute | solution.py:472
  67.6 9.1 %far.2.refs_0_ = bf16[8,144,128]{2,1,0:T(8,128)(2,1)S(1)} custom-call(bf16[8,144,128]{2,1,0:T(8,128)(2,1)S(1)} %collective-permute-done.11.refs_0_, bf16[240,1008]{1,0:T(8,128)(2,1)S(1)} %get-tuple-element.31.refs_4_.refs_1_.refs_2_.refs_10_, bf16[8,256,512]{2,1,0:T(8,128)(2,1)S(1)} %get-tuple-element.32.refs_5_.refs_2_.refs_3_.refs_11_, ...), custom_call_target="tpu_custom_call" | custom-call | tf_op jit(solution)/shard_map/far/pallas_call | solution.py:475
  76.7 0.0 collective-permute-done.12.refs_1_
  76.7 9.2 %far.3.refs_4_ = bf16[8,144,128]{2,1,0:T(8,128)(2,1)S(1)} custom-call(bf16[8,144,128]{2,1,0:T(8,128)(2,1)S(1)} %far.2.refs_0_, bf16[8,144,128]{2,1,0:T(8,128)(2,1)S(1)} %collective-permute-done.12.refs_1_, bf16[240,1008]{1,0:T(8,128)(2,1)S(1)} %get-tuple-element.31.refs_4_.refs_1_.refs_2_.refs_10_, ...), custom_call_target="tpu_custom_call" | custom-call | tf_op jit(solution)/shard_map/far/pallas_call | solution.py:475
  85.9 0.0 collective-permute-done.13.refs_5_
  85.9 18.5 %final.1 = (bf16[4,135,128]{2,1,0:T(8,128)(2,1)S(1)}, bf16[4,135,128]{2,1,0:T(8,128)(2,1)S(1)}, bf16[4,135,128]{2,1,0:T(8,128)(2,1)S(1)}, bf16[4,135,128]{2,1,0:...) custom-call(bf16[8,144,128]{2,1,0:T(8,128)(2,1)S(1)} %collective-per, ...), custom_call_target="tpu_custom_call" | custom-call | tf_op jit(solution)/shard_map/final/pallas_call | solution.py:495
  104.4 1.3 %collective-permute-start.14 = (bf16[4,135,128]{2,1,0:T(8,128)(2,1)S(1)}, bf16[4,135,128]{2,1,0:T(8,128)(2,1)S(1)}, u32[]{:S(2)}, u32[]{:S(2)}) collective-permute-start(bf16[4,135,128]{2,1,0:T(8,128)(2,1)S(1)} %get-tuple-element.38), channel_id=1, source_target_pairs={{0,1},{4,5},{2,3},{6,7},{9,8},{13,12},{11,10},{15,14},{16,17},{20,... | collective-permute-start | bytes 414728 | tf_op jit(solution)/shard_map/ppermute | solution.py:530
  105.7 1.3 %collective-permute-start.15 = (bf16[4,135,128]{2,1,0:T(8,128)(2,1)S(1)}, bf16[4,135,128]{2,1,0:T(8,128)(2,1)S(1)}, u32[]{:S(2)}, u32[]{:S(2)}) collective-permute-start(bf16[4,135,128]{2,1,0:T(8,128)(2,1)S(1)} %get-tuple-element.39), channel_id=1, source_target_pairs={{0,3},{4,7},{2,5},{6,1},{9,14},{13,10},{11,8},{15,12},{16,19},{20,... | collective-permute-start | bytes 414728 | tf_op jit(solution)/shard_map/ppermute | solution.py:530
  107.0 1.3 %collective-permute-start.16 = (bf16[4,135,128]{2,1,0:T(8,128)(2,1)S(1)}, bf16[4,135,128]{2,1,0:T(8,128)(2,1)S(1)}, u32[]{:S(2)}, u32[]{:S(2)}) collective-permute-start(bf16[4,135,128]{2,1,0:T(8,128)(2,1)S(1)} %get-tuple-element.40), channel_id=1, source_target_pairs={{0,5},{4,1},{2,7},{6,3},{9,12},{13,8},{11,14},{15,10},{16,21},{20,... | collective-permute-start | bytes 414728 | tf_op jit(solution)/shard_map/ppermute | solution.py:530
  108.3 1.3 %collective-permute-start.17 = (bf16[4,135,128]{2,1,0:T(8,128)(2,1)S(1)}, bf16[4,135,128]{2,1,0:T(8,128)(2,1)S(1)}, u32[]{:S(2)}, u32[]{:S(2)}) collective-permute-start(bf16[4,135,128]{2,1,0:T(8,128)(2,1)S(1)} %get-tuple-element.41), channel_id=1, source_target_pairs={{0,7},{4,3},{2,1},{6,5},{9,10},{13,14},{11,12},{15,8},{16,23},{20,... | collective-permute-start | bytes 414728 | tf_op jit(solution)/shard_map/ppermute | solution.py:530
  109.6 4.1 %collective-permute-start.18 = (bf16[4,135,128]{2,1,0:T(8,128)(2,1)S(1)}, bf16[4,135,128]{2,1,0:T(8,128)(2,1)S(1)}, u32[]{:S(2)}, u32[]{:S(2)}) collective-permute-start(bf16[4,135,128]{2,1,0:T(8,128)(2,1)S(1)} %get-tuple-element.42), channel_id=1, source_target_pairs={{0,2},{4,6},{2,4},{6,0},{9,15},{13,11},{11,9},{15,13},{16,18},{20,... | collective-permute-start | bytes 414728 | tf_op jit(solution)/shard_map/ppermute | solution.py:530
  113.7 1.9 %collective-permute-start.19 = (bf16[4,135,128]{2,1,0:T(8,128)(2,1)S(1)}, bf16[4,135,128]{2,1,0:T(8,128)(2,1)S(1)}, u32[]{:S(2)}, u32[]{:S(2)}) collective-permute-start(bf16[4,135,128]{2,1,0:T(8,128)(2,1)S(1)} %get-tuple-element.43), channel_id=1, source_target_pairs={{0,4},{4,0},{2,6},{6,2},{9,13},{13,9},{11,15},{15,11},{16,20},{20,... | collective-permute-start | bytes 414728 | tf_op jit(solution)/shard_map/ppermute | solution.py:530
  115.7 2.2 %collective-permute-start.20 = (bf16[4,135,128]{2,1,0:T(8,128)(2,1)S(1)}, bf16[4,135,128]{2,1,0:T(8,128)(2,1)S(1)}, u32[]{:S(2)}, u32[]{:S(2)}) collective-permute-start(bf16[4,135,128]{2,1,0:T(8,128)(2,1)S(1)} %get-tuple-element.44), channel_id=1, source_target_pairs={{0,6},{4,2},{2,0},{6,4},{9,11},{13,15},{11,13},{15,9},{16,22},{20,... | collective-permute-start | bytes 414728 | tf_op jit(solution)/shard_map/ppermute | solution.py:530
  117.9 3.0 %collective-permute-done.19.refs_6_ = bf16[4,135,128]{2,1,0:T(8,128)(2,1)S(1)} collective-permute-done((bf16[4,135,128]{2,1,0:T(8,128)(2,1)S(1)}, bf16[4,135,128]{2,1,0:T(8,128)(2,1)S(1)}, u32[]{:S(2)}, u32[]{:S(2)}) %collective-permute-start.19) | collective-permute-done | bytes 138272 | tf_op jit(solution)/shard_map/ppermute | solution.py:530
  120.9 2.4 %collective-permute-done.20.refs_7_ = bf16[4,135,128]{2,1,0:T(8,128)(2,1)S(1)} collective-permute-done((bf16[4,135,128]{2,1,0:T(8,128)(2,1)S(1)}, bf16[4,135,128]{2,1,0:T(8,128)(2,1)S(1)}, u32[]{:S(2)}, u32[]{:S(2)}) %collective-permute-start.20) | collective-permute-done | bytes 138272 | tf_op jit(solution)/shard_map/ppermute | solution.py:530
  123.3 0.9 place.1
  124.2 0.9 copy.12
  (9 shorter events, 0.0 us)
Async XLA Ops:
  3.0 11.3 %collective-permute-start = (bf16[5,144,128]{2,1,0:T(8,128)(2,1)}, bf16[5,144,128]{2,1,0:T(8,128)(2,1)S(1)}, u32[]{:S(2)}, u32[]{:S(2)}) collective-permute-start(bf16[5,144,128]{2,1,0:T(8,128)(2,1)} %get-tuple-element.25.refs_0_), channel_id=1, source_target_pairs={{1,0},{5,4},{3,2},{7,6},{8,9},{12,13},{10,11},{14,15},{17,16},{21,... | collective-permute-start | bytes 552968 | tf_op jit(solution)/shard_map/ppermute | solution.py:429
  4.3 11.3 %collective-permute-start.2 = (bf16[5,144,128]{2,1,0:T(8,128)(2,1)}, bf16[5,144,128]{2,1,0:T(8,128)(2,1)S(1)}, u32[]{:S(2)}, u32[]{:S(2)}) collective-permute-start(bf16[5,144,128]{2,1,0:T(8,128)(2,1)} %get-tuple-element.26), channel_id=1, source_target_pairs={{3,0},{7,4},{5,2},{1,6},{14,9},{10,13},{8,11},{12,15},{19,16},{23,... | collective-permute-start | bytes 552968 | tf_op jit(solution)/shard_map/ppermute | solution.py:429
  5.6 16.7 %collective-permute-start.1 = (bf16[5,144,128]{2,1,0:T(8,128)(2,1)}, bf16[5,144,128]{2,1,0:T(8,128)(2,1)S(1)}, u32[]{:S(2)}, u32[]{:S(2)}) collective-permute-start(bf16[5,144,128]{2,1,0:T(8,128)(2,1)} %get-tuple-element.26), channel_id=1, source_target_pairs={{2,0},{6,4},{4,2},{0,6},{15,9},{11,13},{9,11},{13,15},{18,16},{22,... | collective-permute-start | bytes 552968 | tf_op jit(solution)/shard_map/ppermute | solution.py:429
  8.8 14.4 %collective-permute-start.4 = (bf16[5,144,128]{2,1,0:T(8,128)(2,1)}, bf16[5,144,128]{2,1,0:T(8,128)(2,1)S(1)}, u32[]{:S(2)}, u32[]{:S(2)}) collective-permute-start(bf16[5,144,128]{2,1,0:T(8,128)(2,1)} %get-tuple-element.27), channel_id=1, source_target_pairs={{5,0},{1,4},{7,2},{3,6},{12,9},{8,13},{14,11},{10,15},{21,16},{17,... | collective-permute-start | bytes 552968 | tf_op jit(solution)/shard_map/ppermute | solution.py:429
  10.1 15.3 %collective-permute-start.3 = (bf16[5,144,128]{2,1,0:T(8,128)(2,1)}, bf16[5,144,128]{2,1,0:T(8,128)(2,1)S(1)}, u32[]{:S(2)}, u32[]{:S(2)}) collective-permute-start(bf16[5,144,128]{2,1,0:T(8,128)(2,1)} %get-tuple-element.27), channel_id=1, source_target_pairs={{4,0},{0,4},{6,2},{2,6},{13,9},{9,13},{15,11},{11,15},{20,16},{16,... | collective-permute-start | bytes 552968 | tf_op jit(solution)/shard_map/ppermute | solution.py:429
  14.3 12.8 %collective-permute-start.6 = (bf16[5,144,128]{2,1,0:T(8,128)(2,1)}, bf16[5,144,128]{2,1,0:T(8,128)(2,1)S(1)}, u32[]{:S(2)}, u32[]{:S(2)}) collective-permute-start(bf16[5,144,128]{2,1,0:T(8,128)(2,1)} %get-tuple-element.28), channel_id=1, source_target_pairs={{7,0},{3,4},{1,2},{5,6},{10,9},{14,13},{12,11},{8,15},{23,16},{19,... | collective-permute-start | bytes 552968 | tf_op jit(solution)/shard_map/ppermute | solution.py:429
  15.6 11.9 %collective-permute-start.5 = (bf16[5,144,128]{2,1,0:T(8,128)(2,1)}, bf16[5,144,128]{2,1,0:T(8,128)(2,1)S(1)}, u32[]{:S(2)}, u32[]{:S(2)}) collective-permute-start(bf16[5,144,128]{2,1,0:T(8,128)(2,1)} %get-tuple-element.28), channel_id=1, source_target_pairs={{6,0},{2,4},{0,2},{4,6},{11,9},{15,13},{13,11},{9,15},{22,16},{18,... | collective-permute-start | bytes 552968 | tf_op jit(solution)/shard_map/ppermute | solution.py:429
  20.5 1.0 copy-start
  27.5 0.9 copy-start.1
  38.4 10.9 %collective-permute-start.10 = (bf16[8,144,128]{2,1,0:T(8,128)(2,1)S(1)}, bf16[8,144,128]{2,1,0:T(8,128)(2,1)S(1)}, u32[]{:S(2)}, u32[]{:S(2)}) collective-permute-start(bf16[8,144,128]{2,1,0:T(8,128)(2,1)S(1)} %get-tuple-element.30.refs_6_), channel_id=1, source_target_pairs={{0,4},{4,2},{2,6},{6,9},{9,13},{13,11},{11,15},{15,16},{16,20},{20... | collective-permute-start | bytes 884744 | tf_op jit(solution)/shard_map/ppermute | solution.py:472
  40.3 14.2 %collective-permute-start.9 = (bf16[8,144,128]{2,1,0:T(8,128)(2,1)S(1)}, bf16[8,144,128]{2,1,0:T(8,128)(2,1)S(1)}, u32[]{:S(2)}, u32[]{:S(2)}) collective-permute-start(bf16[8,144,128]{2,1,0:T(8,128)(2,1)S(1)} %get-tuple-element.30.refs_6_), channel_id=1, source_target_pairs={{0,2},{4,6},{2,9},{6,13},{9,11},{13,15},{11,16},{15,20},{16,18},{2... | collective-permute-start | bytes 884744 | tf_op jit(solution)/shard_map/ppermute | solution.py:472
  43.1 13.7 %collective-permute-start.8 = (bf16[8,144,128]{2,1,0:T(8,128)(2,1)S(1)}, bf16[8,144,128]{2,1,0:T(8,128)(2,1)S(1)}, u32[]{:S(2)}, u32[]{:S(2)}) collective-permute-start(bf16[8,144,128]{2,1,0:T(8,128)(2,1)S(1)} %get-tuple-element.30.refs_6_), channel_id=1, source_target_pairs={{0,6},{4,9},{2,13},{6,11},{9,15},{13,16},{11,20},{15,18},{16,22},{... | collective-permute-start | bytes 884744 | tf_op jit(solution)/shard_map/ppermute | solution.py:472
  45.0 13.6 %collective-permute-start.7 = (bf16[8,144,128]{2,1,0:T(8,128)(2,1)S(1)}, bf16[8,144,128]{2,1,0:T(8,128)(2,1)S(1)}, u32[]{:S(2)}, u32[]{:S(2)}) collective-permute-start(bf16[8,144,128]{2,1,0:T(8,128)(2,1)S(1)} %get-tuple-element.30.refs_6_), channel_id=1, source_target_pairs={{0,9},{4,13},{2,11},{6,15},{9,16},{13,20},{11,18},{15,22},{16,25},... | collective-permute-start | bytes 884744 | tf_op jit(solution)/shard_map/ppermute | solution.py:472
  58.7 8.9 %collective-permute-start.11 = (bf16[8,144,128]{2,1,0:T(8,128)(2,1)S(1)}, bf16[8,144,128]{2,1,0:T(8,128)(2,1)S(1)}, u32[]{:S(2)}, u32[]{:S(2)}) collective-permute-start(bf16[8,144,128]{2,1,0:T(8,128)(2,1)S(1)} %near.1), channel_id=1, source_target_pairs={{0,25},{4,29},{2,27},{6,31}} | collective-permute-start | bytes 884744 | tf_op jit(solution)/shard_map/ppermute | solution.py:472
  60.0 16.8 %collective-permute-start.12 = (bf16[8,144,128]{2,1,0:T(8,128)(2,1)S(1)}, bf16[8,144,128]{2,1,0:T(8,128)(2,1)S(1)}, u32[]{:S(2)}, u32[]{:S(2)}) collective-permute-start(bf16[8,144,128]{2,1,0:T(8,128)(2,1)S(1)} %near.1), channel_id=1, source_target_pairs={{0,16},{4,20},{2,18},{6,22},{9,25},{13,29},{11,27},{15,31}} | collective-permute-start | bytes 884744 | tf_op jit(solution)/shard_map/ppermute | solution.py:472
  61.3 24.6 %collective-permute-start.13 = (bf16[8,144,128]{2,1,0:T(8,128)(2,1)S(1)}, bf16[8,144,128]{2,1,0:T(8,128)(2,1)S(1)}, u32[]{:S(2)}, u32[]{:S(2)}) collective-permute-start(bf16[8,144,128]{2,1,0:T(8,128)(2,1)S(1)} %near.1), channel_id=1, source_target_pairs={{0,9},{4,13},{2,11},{6,15},{9,16},{13,20},{11,18},{15,22},{16,25},... | collective-permute-start | bytes 884744 | tf_op jit(solution)/shard_map/ppermute | solution.py:472
  104.4 9.3 %collective-permute-start.14 = (bf16[4,135,128]{2,1,0:T(8,128)(2,1)S(1)}, bf16[4,135,128]{2,1,0:T(8,128)(2,1)S(1)}, u32[]{:S(2)}, u32[]{:S(2)}) collective-permute-start(bf16[4,135,128]{2,1,0:T(8,128)(2,1)S(1)} %get-tuple-element.38), channel_id=1, source_target_pairs={{0,1},{4,5},{2,3},{6,7},{9,8},{13,12},{11,10},{15,14},{16,17},{20,... | collective-permute-start | bytes 414728 | tf_op jit(solution)/shard_map/ppermute | solution.py:530
  105.7 10.0 %collective-permute-start.15 = (bf16[4,135,128]{2,1,0:T(8,128)(2,1)S(1)}, bf16[4,135,128]{2,1,0:T(8,128)(2,1)S(1)}, u32[]{:S(2)}, u32[]{:S(2)}) collective-permute-start(bf16[4,135,128]{2,1,0:T(8,128)(2,1)S(1)} %get-tuple-element.39), channel_id=1, source_target_pairs={{0,3},{4,7},{2,5},{6,1},{9,14},{13,10},{11,8},{15,12},{16,19},{20,... | collective-permute-start | bytes 414728 | tf_op jit(solution)/shard_map/ppermute | solution.py:530
  107.0 10.9 %collective-permute-start.16 = (bf16[4,135,128]{2,1,0:T(8,128)(2,1)S(1)}, bf16[4,135,128]{2,1,0:T(8,128)(2,1)S(1)}, u32[]{:S(2)}, u32[]{:S(2)}) collective-permute-start(bf16[4,135,128]{2,1,0:T(8,128)(2,1)S(1)} %get-tuple-element.40), channel_id=1, source_target_pairs={{0,5},{4,1},{2,7},{6,3},{9,12},{13,8},{11,14},{15,10},{16,21},{20,... | collective-permute-start | bytes 414728 | tf_op jit(solution)/shard_map/ppermute | solution.py:530
  108.3 9.6 %collective-permute-start.17 = (bf16[4,135,128]{2,1,0:T(8,128)(2,1)S(1)}, bf16[4,135,128]{2,1,0:T(8,128)(2,1)S(1)}, u32[]{:S(2)}, u32[]{:S(2)}) collective-permute-start(bf16[4,135,128]{2,1,0:T(8,128)(2,1)S(1)} %get-tuple-element.41), channel_id=1, source_target_pairs={{0,7},{4,3},{2,1},{6,5},{9,10},{13,14},{11,12},{15,8},{16,23},{20,... | collective-permute-start | bytes 414728 | tf_op jit(solution)/shard_map/ppermute | solution.py:530
  109.6 8.3 %collective-permute-start.18 = (bf16[4,135,128]{2,1,0:T(8,128)(2,1)S(1)}, bf16[4,135,128]{2,1,0:T(8,128)(2,1)S(1)}, u32[]{:S(2)}, u32[]{:S(2)}) collective-permute-start(bf16[4,135,128]{2,1,0:T(8,128)(2,1)S(1)} %get-tuple-element.42), channel_id=1, source_target_pairs={{0,2},{4,6},{2,4},{6,0},{9,15},{13,11},{11,9},{15,13},{16,18},{20,... | collective-permute-start | bytes 414728 | tf_op jit(solution)/shard_map/ppermute | solution.py:530
  113.7 7.2 %collective-permute-start.19 = (bf16[4,135,128]{2,1,0:T(8,128)(2,1)S(1)}, bf16[4,135,128]{2,1,0:T(8,128)(2,1)S(1)}, u32[]{:S(2)}, u32[]{:S(2)}) collective-permute-start(bf16[4,135,128]{2,1,0:T(8,128)(2,1)S(1)} %get-tuple-element.43), channel_id=1, source_target_pairs={{0,4},{4,0},{2,6},{6,2},{9,13},{13,9},{11,15},{15,11},{16,20},{20,... | collective-permute-start | bytes 414728 | tf_op jit(solution)/shard_map/ppermute | solution.py:530
  115.7 7.6 %collective-permute-start.20 = (bf16[4,135,128]{2,1,0:T(8,128)(2,1)S(1)}, bf16[4,135,128]{2,1,0:T(8,128)(2,1)S(1)}, u32[]{:S(2)}, u32[]{:S(2)}) collective-permute-start(bf16[4,135,128]{2,1,0:T(8,128)(2,1)S(1)} %get-tuple-element.44), channel_id=1, source_target_pairs={{0,6},{4,2},{2,0},{6,4},{9,11},{13,15},{11,13},{15,9},{16,22},{20,... | collective-permute-start | bytes 414728 | tf_op jit(solution)/shard_map/ppermute | solution.py:530

commit v6 on v5

--- a/solution.py
+++ b/solution.py
@@ -178,7 +178,8 @@
         copy.wait()
     forcing, initial, damping, send_index, conn = held
     steps = forcing.shape[1]
-    wide[...] = forcing[...].astype(F32).reshape(wide.shape)
+    lines = forcing.shape[0] * steps
+    wide[:lines] = forcing[...].astype(F32).reshape(lines, LANES)
     place = Place(space, intervals)
     width = initial.shape[0]
     faces = conn.shape[0]
@@ -409,7 +410,7 @@
         out_specs=[hbm] * intervals,
         scratch_shapes=[pltpu.VMEM(array.shape, array.dtype) for array in packing]
         + [
-            pltpu.VMEM((width * steps, LANES), F32),
+            pltpu.VMEM(((width + 1) * steps, LANES), F32),
             pltpu.VMEM((intervals, COARSEN + 1, ROWS, LANES), BF),
             pltpu.SemaphoreType.DMA((5,)),
             pltpu.SemaphoreType.DMA((intervals,)),

time: 126 us -> 126 us (level)
  no operation moved by 1% of the time
where the time goes in v6:
time: 126 us; the launch traced here: 125 us
  Pallas kernels  50.6 us (40%)
  starting transfers between devices  40.8 us (32%)
  waiting for transfers between devices  28 us (22%)
  local copies, waits for them, and re-layouts  4.65 us (4%)
    pallas_call x1, Pallas kernels, shards(): pl.pallas_call(functools.partial(final_kernel, space, intervals, width, f...  18.5 us
    pallas_call x3, Pallas kernels, chain(): pl.pallas_call(functools.partial(kernel, space, intervals, number, faces)...  18.3 us
    ppermute x7, waiting for transfers between devices, from_earlier(): return lax.ppermute(value, ('tm', 'space'), pairs)  17.4 us
    ppermute x7, starting transfers between devices, shards(): lax.ppermute(messages[turn // stride], ('tm', 'space'), pairs)  15.6 us
    ppermute x7, starting transfers between devices, shards(): returned[turn] = lax.ppermute(pieces[turn], ('tm', 'space'), pairs)  13.4 us
    ppermute x7, starting transfers between devices, from_earlier(): return lax.ppermute(value, ('tm', 'space'), pairs)  11.8 us
    pallas_call x1, Pallas kernels, shards(): pl.pallas_call(functools.partial(fine_kernel, space, intervals, width, fa...  9.9 us
    ppermute x7, waiting for transfers between devices, shards(): returned[turn] = lax.ppermute(pieces[turn], ('tm', 'space'), pairs)  5.38 us
  transfers between devices with their start and end apart: 21, of which 11 were waited for; matrix products, arithmetic and copies ran while one was open for 1% of the time, Pallas kernels for 15%

profile of v6, /device:TPU:7, one launch (start us, length us, event | category | flops | bytes accessed | tf_op | source)
XLA Modules:
  0.0 125.1 jit_solution(9484089348831665131)
XLA Ops:
  0.7 2.3 %pack.1 = (bf16[5,144,128]{2,1,0:T(8,128)(2,1)}, bf16[5,144,128]{2,1,0:T(8,128)(2,1)}, bf16[5,144,128]{2,1,0:T(8,128)(2,1)}, bf16[5,144,128]{2,1,0:T(8,128)(2,1)}) custom-call(s32[1]{0:T(128)S(6)} %copy.13.etype, bf16[135,16,128]{2,1,0:T(8,128)(2,1)} %bitcast.3, bf16[135,128]{1,0:T(8,128)(2,1)} %refs_1_.1, f32[1,128]{1,0:T(1,128)} %bitcast.4, ...), custom_call_target="tpu_custom_call" | custom-call | tf_op jit(solution)/shard_map/pack/pallas_call | solution.py:406
  3.0 1.3 %collective-permute-start = (bf16[5,144,128]{2,1,0:T(8,128)(2,1)}, bf16[5,144,128]{2,1,0:T(8,128)(2,1)S(1)}, u32[]{:S(2)}, u32[]{:S(2)}) collective-permute-start(bf16[5,144,128]{2,1,0:T(8,128)(2,1)} %get-tuple-element.25.refs_0_), channel_id=1, source_target_pairs={{1,0},{5,4},{3,2},{7,6},{8,9},{12,13},{10,11},{14,15},{17,16},{21,... | collective-permute-start | bytes 552968 | tf_op jit(solution)/shard_map/ppermute | solution.py:430
  4.3 1.3 %collective-permute-start.2 = (bf16[5,144,128]{2,1,0:T(8,128)(2,1)}, bf16[5,144,128]{2,1,0:T(8,128)(2,1)S(1)}, u32[]{:S(2)}, u32[]{:S(2)}) collective-permute-start(bf16[5,144,128]{2,1,0:T(8,128)(2,1)} %get-tuple-element.26), channel_id=1, source_target_pairs={{3,0},{7,4},{5,2},{1,6},{14,9},{10,13},{8,11},{12,15},{19,16},{23,... | collective-permute-start | bytes 552968 | tf_op jit(solution)/shard_map/ppermute | solution.py:430
  5.6 3.2 %collective-permute-start.1 = (bf16[5,144,128]{2,1,0:T(8,128)(2,1)}, bf16[5,144,128]{2,1,0:T(8,128)(2,1)S(1)}, u32[]{:S(2)}, u32[]{:S(2)}) collective-permute-start(bf16[5,144,128]{2,1,0:T(8,128)(2,1)} %get-tuple-element.26), channel_id=1, source_target_pairs={{2,0},{6,4},{4,2},{0,6},{15,9},{11,13},{9,11},{13,15},{18,16},{22,... | collective-permute-start | bytes 552968 | tf_op jit(solution)/shard_map/ppermute | solution.py:430
  8.8 1.3 %collective-permute-start.4 = (bf16[5,144,128]{2,1,0:T(8,128)(2,1)}, bf16[5,144,128]{2,1,0:T(8,128)(2,1)S(1)}, u32[]{:S(2)}, u32[]{:S(2)}) collective-permute-start(bf16[5,144,128]{2,1,0:T(8,128)(2,1)} %get-tuple-element.27), channel_id=1, source_target_pairs={{5,0},{1,4},{7,2},{3,6},{12,9},{8,13},{14,11},{10,15},{21,16},{17,... | collective-permute-start | bytes 552968 | tf_op jit(solution)/shard_map/ppermute | solution.py:430
  10.1 4.2 %collective-permute-start.3 = (bf16[5,144,128]{2,1,0:T(8,128)(2,1)}, bf16[5,144,128]{2,1,0:T(8,128)(2,1)S(1)}, u32[]{:S(2)}, u32[]{:S(2)}) collective-permute-start(bf16[5,144,128]{2,1,0:T(8,128)(2,1)} %get-tuple-element.27), channel_id=1, source_target_pairs={{4,0},{0,4},{6,2},{2,6},{13,9},{9,13},{15,11},{11,15},{20,16},{16,... | collective-permute-start | bytes 552968 | tf_op jit(solution)/shard_map/ppermute | solution.py:430
  14.3 0.0 collective-permute-done.refs_1_
  14.3 1.3 %collective-permute-start.6 = (bf16[5,144,128]{2,1,0:T(8,128)(2,1)}, bf16[5,144,128]{2,1,0:T(8,128)(2,1)S(1)}, u32[]{:S(2)}, u32[]{:S(2)}) collective-permute-start(bf16[5,144,128]{2,1,0:T(8,128)(2,1)} %get-tuple-element.28), channel_id=1, source_target_pairs={{7,0},{3,4},{1,2},{5,6},{10,9},{14,13},{12,11},{8,15},{23,16},{19,... | collective-permute-start | bytes 552968 | tf_op jit(solution)/shard_map/ppermute | solution.py:430
  15.6 3.0 %collective-permute-start.5 = (bf16[5,144,128]{2,1,0:T(8,128)(2,1)}, bf16[5,144,128]{2,1,0:T(8,128)(2,1)S(1)}, u32[]{:S(2)}, u32[]{:S(2)}) collective-permute-start(bf16[5,144,128]{2,1,0:T(8,128)(2,1)} %get-tuple-element.28), channel_id=1, source_target_pairs={{6,0},{2,4},{0,2},{4,6},{11,9},{15,13},{13,11},{9,15},{22,16},{18,... | collective-permute-start | bytes 552968 | tf_op jit(solution)/shard_map/ppermute | solution.py:430
  18.6 0.9 copy.10.fine
  19.6 0.9 copy.11.coarse
  20.5 0.0 copy-start
  20.5 1.0 copy-done
  21.5 0.8 fold.1
  22.3 0.0 collective-permute-done.1.refs_2_
  22.3 0.9 collective-permute-done.4.refs_5_
  23.2 2.2 %collective-permute-done.3.refs_4_ = bf16[5,144,128]{2,1,0:T(8,128)(2,1)S(1)} collective-permute-done((bf16[5,144,128]{2,1,0:T(8,128)(2,1)}, bf16[5,144,128]{2,1,0:T(8,128)(2,1)S(1)}, u32[]{:S(2)}, u32[]{:S(2)}) %collective-permute-start.3) | collective-permute-done | bytes 184352 | tf_op jit(solution)/shard_map/ppermute | solution.py:430
  25.4 1.7 %collective-permute-done.6.refs_7_ = bf16[5,144,128]{2,1,0:T(8,128)(2,1)S(1)} collective-permute-done((bf16[5,144,128]{2,1,0:T(8,128)(2,1)}, bf16[5,144,128]{2,1,0:T(8,128)(2,1)S(1)}, u32[]{:S(2)}, u32[]{:S(2)}) %collective-permute-start.6) | collective-permute-done | bytes 184352 | tf_op jit(solution)/shard_map/ppermute | solution.py:430
  27.1 0.4 collective-permute-done.5.refs_6_
  27.5 0.9 copy-done.1
  28.5 9.9 %fine.2 = (bf16[8,144,128]{2,1,0:T(8,128)(2,1)S(1)}, bf16[8,256,512]{2,1,0:T(8,128)(2,1)S(1)}, bf16[4,256,256]{2,1,0:T(8,128)(2,1)S(1)}, f32[8,8,128]{2,1,0:T(8,...) custom-call(bf16[5,144,128]{2,1,0:T(8,128)(2,1)S(1)} %copy-done.1, ...), custom_call_target="tpu_custom_call" | custom-call | tf_op jit(solution)/shard_map/fine/pallas_call | solution.py:452
  38.4 1.9 %collective-permute-start.10 = (bf16[8,144,128]{2,1,0:T(8,128)(2,1)S(1)}, bf16[8,144,128]{2,1,0:T(8,128)(2,1)S(1)}, u32[]{:S(2)}, u32[]{:S(2)}) collective-permute-start(bf16[8,144,128]{2,1,0:T(8,128)(2,1)S(1)} %get-tuple-element.30.refs_6_), channel_id=1, source_target_pairs={{0,4},{4,2},{2,6},{6,9},{9,13},{13,11},{11,15},{15,16},{16,20},{20... | collective-permute-start | bytes 884744 | tf_op jit(solution)/shard_map/ppermute | solution.py:473
  40.3 2.8 %collective-permute-start.9 = (bf16[8,144,128]{2,1,0:T(8,128)(2,1)S(1)}, bf16[8,144,128]{2,1,0:T(8,128)(2,1)S(1)}, u32[]{:S(2)}, u32[]{:S(2)}) collective-permute-start(bf16[8,144,128]{2,1,0:T(8,128)(2,1)S(1)} %get-tuple-element.30.refs_6_), channel_id=1, source_target_pairs={{0,2},{4,6},{2,9},{6,13},{9,11},{13,15},{11,16},{15,20},{16,18},{2... | collective-permute-start | bytes 884744 | tf_op jit(solution)/shard_map/ppermute | solution.py:473
  43.1 1.9 %collective-permute-start.8 = (bf16[8,144,128]{2,1,0:T(8,128)(2,1)S(1)}, bf16[8,144,128]{2,1,0:T(8,128)(2,1)S(1)}, u32[]{:S(2)}, u32[]{:S(2)}) collective-permute-start(bf16[8,144,128]{2,1,0:T(8,128)(2,1)S(1)} %get-tuple-element.30.refs_6_), channel_id=1, source_target_pairs={{0,6},{4,9},{2,13},{6,11},{9,15},{13,16},{11,20},{15,18},{16,22},{... | collective-permute-start | bytes 884744 | tf_op jit(solution)/shard_map/ppermute | solution.py:473
  45.0 1.3 %collective-permute-start.7 = (bf16[8,144,128]{2,1,0:T(8,128)(2,1)S(1)}, bf16[8,144,128]{2,1,0:T(8,128)(2,1)S(1)}, u32[]{:S(2)}, u32[]{:S(2)}) collective-permute-start(bf16[8,144,128]{2,1,0:T(8,128)(2,1)S(1)} %get-tuple-element.30.refs_6_), channel_id=1, source_target_pairs={{0,9},{4,13},{2,11},{6,15},{9,16},{13,20},{11,18},{15,22},{16,25},... | collective-permute-start | bytes 884744 | tf_op jit(solution)/shard_map/ppermute | solution.py:473
  46.3 3.0 %collective-permute-done.10.refs_3_ = bf16[8,144,128]{2,1,0:T(8,128)(2,1)S(1)} collective-permute-done((bf16[8,144,128]{2,1,0:T(8,128)(2,1)S(1)}, bf16[8,144,128]{2,1,0:T(8,128)(2,1)S(1)}, u32[]{:S(2)}, u32[]{:S(2)}) %collective-permute-start.10) | collective-permute-done | bytes 294944 | tf_op jit(solution)/shard_map/ppermute | solution.py:473
  49.3 5.2 %collective-permute-done.9.refs_2_ = bf16[8,144,128]{2,1,0:T(8,128)(2,1)S(1)} collective-permute-done((bf16[8,144,128]{2,1,0:T(8,128)(2,1)S(1)}, bf16[8,144,128]{2,1,0:T(8,128)(2,1)S(1)}, u32[]{:S(2)}, u32[]{:S(2)}) %collective-permute-start.9) | collective-permute-done | bytes 294944 | tf_op jit(solution)/shard_map/ppermute | solution.py:473
  54.5 2.3 %collective-permute-done.8.refs_1_ = bf16[8,144,128]{2,1,0:T(8,128)(2,1)S(1)} collective-permute-done((bf16[8,144,128]{2,1,0:T(8,128)(2,1)S(1)}, bf16[8,144,128]{2,1,0:T(8,128)(2,1)S(1)}, u32[]{:S(2)}, u32[]{:S(2)}) %collective-permute-start.8) | collective-permute-done | bytes 294944 | tf_op jit(solution)/shard_map/ppermute | solution.py:473
  56.8 1.9 %collective-permute-done.7.refs_0_ = bf16[8,144,128]{2,1,0:T(8,128)(2,1)S(1)} collective-permute-done((bf16[8,144,128]{2,1,0:T(8,128)(2,1)S(1)}, bf16[8,144,128]{2,1,0:T(8,128)(2,1)S(1)}, u32[]{:S(2)}, u32[]{:S(2)}) %collective-permute-start.7) | collective-permute-done | bytes 294944 | tf_op jit(solution)/shard_map/ppermute | solution.py:473
  58.7 1.3 %collective-permute-start.11 = (bf16[8,144,128]{2,1,0:T(8,128)(2,1)S(1)}, bf16[8,144,128]{2,1,0:T(8,128)(2,1)S(1)}, u32[]{:S(2)}, u32[]{:S(2)}) collective-permute-start(bf16[8,144,128]{2,1,0:T(8,128)(2,1)S(1)} %near.1), channel_id=1, source_target_pairs={{0,25},{4,29},{2,27},{6,31}} | collective-permute-start | bytes 884744 | tf_op jit(solution)/shard_map/ppermute | solution.py:473
  60.0 1.3 %collective-permute-start.12 = (bf16[8,144,128]{2,1,0:T(8,128)(2,1)S(1)}, bf16[8,144,128]{2,1,0:T(8,128)(2,1)S(1)}, u32[]{:S(2)}, u32[]{:S(2)}) collective-permute-start(bf16[8,144,128]{2,1,0:T(8,128)(2,1)S(1)} %near.1), channel_id=1, source_target_pairs={{0,16},{4,20},{2,18},{6,22},{9,25},{13,29},{11,27},{15,31}} | collective-permute-start | bytes 884744 | tf_op jit(solution)/shard_map/ppermute | solution.py:473
  61.3 1.3 %collective-permute-start.13 = (bf16[8,144,128]{2,1,0:T(8,128)(2,1)S(1)}, bf16[8,144,128]{2,1,0:T(8,128)(2,1)S(1)}, u32[]{:S(2)}, u32[]{:S(2)}) collective-permute-start(bf16[8,144,128]{2,1,0:T(8,128)(2,1)S(1)} %near.1), channel_id=1, source_target_pairs={{0,9},{4,13},{2,11},{6,15},{9,16},{13,20},{11,18},{15,22},{16,25},... | collective-permute-start | bytes 884744 | tf_op jit(solution)/shard_map/ppermute | solution.py:473
  62.6 5.0 %collective-permute-done.11.refs_0_ = bf16[8,144,128]{2,1,0:T(8,128)(2,1)S(1)} collective-permute-done((bf16[8,144,128]{2,1,0:T(8,128)(2,1)S(1)}, bf16[8,144,128]{2,1,0:T(8,128)(2,1)S(1)}, u32[]{:S(2)}, u32[]{:S(2)}) %collective-permute-start.11) | collective-permute-done | bytes 294944 | tf_op jit(solution)/shard_map/ppermute | solution.py:473
  67.6 9.1 %far.2.refs_0_ = bf16[8,144,128]{2,1,0:T(8,128)(2,1)S(1)} custom-call(bf16[8,144,128]{2,1,0:T(8,128)(2,1)S(1)} %collective-permute-done.11.refs_0_, bf16[240,1008]{1,0:T(8,128)(2,1)S(1)} %get-tuple-element.31.refs_4_.refs_1_.refs_2_.refs_10_, bf16[8,256,512]{2,1,0:T(8,128)(2,1)S(1)} %get-tuple-element.32.refs_5_.refs_2_.refs_3_.refs_11_, ...), custom_call_target="tpu_custom_call" | custom-call | tf_op jit(solution)/shard_map/far/pallas_call | solution.py:476
  76.7 9.2 %far.3.refs_4_ = bf16[8,144,128]{2,1,0:T(8,128)(2,1)S(1)} custom-call(bf16[8,144,128]{2,1,0:T(8,128)(2,1)S(1)} %far.2.refs_0_, bf16[8,144,128]{2,1,0:T(8,128)(2,1)S(1)} %collective-permute-done.12.refs_1_, bf16[240,1008]{1,0:T(8,128)(2,1)S(1)} %get-tuple-element.31.refs_4_.refs_1_.refs_2_.refs_10_, ...), custom_call_target="tpu_custom_call" | custom-call | tf_op jit(solution)/shard_map/far/pallas_call | solution.py:476
  85.9 0.0 collective-permute-done.13.refs_5_
  85.9 18.5 %final.1 = (bf16[4,135,128]{2,1,0:T(8,128)(2,1)S(1)}, bf16[4,135,128]{2,1,0:T(8,128)(2,1)S(1)}, bf16[4,135,128]{2,1,0:T(8,128)(2,1)S(1)}, bf16[4,135,128]{2,1,0:...) custom-call(bf16[8,144,128]{2,1,0:T(8,128)(2,1)S(1)} %collective-per, ...), custom_call_target="tpu_custom_call" | custom-call | tf_op jit(solution)/shard_map/final/pallas_call | solution.py:496
  104.4 1.3 %collective-permute-start.14 = (bf16[4,135,128]{2,1,0:T(8,128)(2,1)S(1)}, bf16[4,135,128]{2,1,0:T(8,128)(2,1)S(1)}, u32[]{:S(2)}, u32[]{:S(2)}) collective-permute-start(bf16[4,135,128]{2,1,0:T(8,128)(2,1)S(1)} %get-tuple-element.38), channel_id=1, source_target_pairs={{0,1},{4,5},{2,3},{6,7},{9,8},{13,12},{11,10},{15,14},{16,17},{20,... | collective-permute-start | bytes 414728 | tf_op jit(solution)/shard_map/ppermute | solution.py:531
  105.7 1.3 %collective-permute-start.15 = (bf16[4,135,128]{2,1,0:T(8,128)(2,1)S(1)}, bf16[4,135,128]{2,1,0:T(8,128)(2,1)S(1)}, u32[]{:S(2)}, u32[]{:S(2)}) collective-permute-start(bf16[4,135,128]{2,1,0:T(8,128)(2,1)S(1)} %get-tuple-element.39), channel_id=1, source_target_pairs={{0,3},{4,7},{2,5},{6,1},{9,14},{13,10},{11,8},{15,12},{16,19},{20,... | collective-permute-start | bytes 414728 | tf_op jit(solution)/shard_map/ppermute | solution.py:531
  107.0 1.3 %collective-permute-start.16 = (bf16[4,135,128]{2,1,0:T(8,128)(2,1)S(1)}, bf16[4,135,128]{2,1,0:T(8,128)(2,1)S(1)}, u32[]{:S(2)}, u32[]{:S(2)}) collective-permute-start(bf16[4,135,128]{2,1,0:T(8,128)(2,1)S(1)} %get-tuple-element.40), channel_id=1, source_target_pairs={{0,5},{4,1},{2,7},{6,3},{9,12},{13,8},{11,14},{15,10},{16,21},{20,... | collective-permute-start | bytes 414728 | tf_op jit(solution)/shard_map/ppermute | solution.py:531
  108.3 1.3 %collective-permute-start.17 = (bf16[4,135,128]{2,1,0:T(8,128)(2,1)S(1)}, bf16[4,135,128]{2,1,0:T(8,128)(2,1)S(1)}, u32[]{:S(2)}, u32[]{:S(2)}) collective-permute-start(bf16[4,135,128]{2,1,0:T(8,128)(2,1)S(1)} %get-tuple-element.41), channel_id=1, source_target_pairs={{0,7},{4,3},{2,1},{6,5},{9,10},{13,14},{11,12},{15,8},{16,23},{20,... | collective-permute-start | bytes 414728 | tf_op jit(solution)/shard_map/ppermute | solution.py:531
  109.6 4.1 %collective-permute-start.18 = (bf16[4,135,128]{2,1,0:T(8,128)(2,1)S(1)}, bf16[4,135,128]{2,1,0:T(8,128)(2,1)S(1)}, u32[]{:S(2)}, u32[]{:S(2)}) collective-permute-start(bf16[4,135,128]{2,1,0:T(8,128)(2,1)S(1)} %get-tuple-element.42), channel_id=1, source_target_pairs={{0,2},{4,6},{2,4},{6,0},{9,15},{13,11},{11,9},{15,13},{16,18},{20,... | collective-permute-start | bytes 414728 | tf_op jit(solution)/shard_map/ppermute | solution.py:531
  113.8 1.9 %collective-permute-start.19 = (bf16[4,135,128]{2,1,0:T(8,128)(2,1)S(1)}, bf16[4,135,128]{2,1,0:T(8,128)(2,1)S(1)}, u32[]{:S(2)}, u32[]{:S(2)}) collective-permute-start(bf16[4,135,128]{2,1,0:T(8,128)(2,1)S(1)} %get-tuple-element.43), channel_id=1, source_target_pairs={{0,4},{4,0},{2,6},{6,2},{9,13},{13,9},{11,15},{15,11},{16,20},{20,... | collective-permute-start | bytes 414728 | tf_op jit(solution)/shard_map/ppermute | solution.py:531
  115.7 2.2 %collective-permute-start.20 = (bf16[4,135,128]{2,1,0:T(8,128)(2,1)S(1)}, bf16[4,135,128]{2,1,0:T(8,128)(2,1)S(1)}, u32[]{:S(2)}, u32[]{:S(2)}) collective-permute-start(bf16[4,135,128]{2,1,0:T(8,128)(2,1)S(1)} %get-tuple-element.44), channel_id=1, source_target_pairs={{0,6},{4,2},{2,0},{6,4},{9,11},{13,15},{11,13},{15,9},{16,22},{20,... | collective-permute-start | bytes 414728 | tf_op jit(solution)/shard_map/ppermute | solution.py:531
  117.9 3.0 %collective-permute-done.19.refs_6_ = bf16[4,135,128]{2,1,0:T(8,128)(2,1)S(1)} collective-permute-done((bf16[4,135,128]{2,1,0:T(8,128)(2,1)S(1)}, bf16[4,135,128]{2,1,0:T(8,128)(2,1)S(1)}, u32[]{:S(2)}, u32[]{:S(2)}) %collective-permute-start.19) | collective-permute-done | bytes 138272 | tf_op jit(solution)/shard_map/ppermute | solution.py:531
  120.9 2.4 %collective-permute-done.20.refs_7_ = bf16[4,135,128]{2,1,0:T(8,128)(2,1)S(1)} collective-permute-done((bf16[4,135,128]{2,1,0:T(8,128)(2,1)S(1)}, bf16[4,135,128]{2,1,0:T(8,128)(2,1)S(1)}, u32[]{:S(2)}, u32[]{:S(2)}) %collective-permute-start.20) | collective-permute-done | bytes 138272 | tf_op jit(solution)/shard_map/ppermute | solution.py:531
  123.3 0.9 place.1
  124.2 0.9 copy.12
  (9 shorter events, 0.0 us)
Async XLA Ops:
  3.0 11.3 %collective-permute-start = (bf16[5,144,128]{2,1,0:T(8,128)(2,1)}, bf16[5,144,128]{2,1,0:T(8,128)(2,1)S(1)}, u32[]{:S(2)}, u32[]{:S(2)}) collective-permute-start(bf16[5,144,128]{2,1,0:T(8,128)(2,1)} %get-tuple-element.25.refs_0_), channel_id=1, source_target_pairs={{1,0},{5,4},{3,2},{7,6},{8,9},{12,13},{10,11},{14,15},{17,16},{21,... | collective-permute-start | bytes 552968 | tf_op jit(solution)/shard_map/ppermute | solution.py:430
  4.3 11.3 %collective-permute-start.2 = (bf16[5,144,128]{2,1,0:T(8,128)(2,1)}, bf16[5,144,128]{2,1,0:T(8,128)(2,1)S(1)}, u32[]{:S(2)}, u32[]{:S(2)}) collective-permute-start(bf16[5,144,128]{2,1,0:T(8,128)(2,1)} %get-tuple-element.26), channel_id=1, source_target_pairs={{3,0},{7,4},{5,2},{1,6},{14,9},{10,13},{8,11},{12,15},{19,16},{23,... | collective-permute-start | bytes 552968 | tf_op jit(solution)/shard_map/ppermute | solution.py:430
  5.6 16.7 %collective-permute-start.1 = (bf16[5,144,128]{2,1,0:T(8,128)(2,1)}, bf16[5,144,128]{2,1,0:T(8,128)(2,1)S(1)}, u32[]{:S(2)}, u32[]{:S(2)}) collective-permute-start(bf16[5,144,128]{2,1,0:T(8,128)(2,1)} %get-tuple-element.26), channel_id=1, source_target_pairs={{2,0},{6,4},{4,2},{0,6},{15,9},{11,13},{9,11},{13,15},{18,16},{22,... | collective-permute-start | bytes 552968 | tf_op jit(solution)/shard_map/ppermute | solution.py:430
  8.8 14.4 %collective-permute-start.4 = (bf16[5,144,128]{2,1,0:T(8,128)(2,1)}, bf16[5,144,128]{2,1,0:T(8,128)(2,1)S(1)}, u32[]{:S(2)}, u32[]{:S(2)}) collective-permute-start(bf16[5,144,128]{2,1,0:T(8,128)(2,1)} %get-tuple-element.27), channel_id=1, source_target_pairs={{5,0},{1,4},{7,2},{3,6},{12,9},{8,13},{14,11},{10,15},{21,16},{17,... | collective-permute-start | bytes 552968 | tf_op jit(solution)/shard_map/ppermute | solution.py:430
  10.1 15.3 %collective-permute-start.3 = (bf16[5,144,128]{2,1,0:T(8,128)(2,1)}, bf16[5,144,128]{2,1,0:T(8,128)(2,1)S(1)}, u32[]{:S(2)}, u32[]{:S(2)}) collective-permute-start(bf16[5,144,128]{2,1,0:T(8,128)(2,1)} %get-tuple-element.27), channel_id=1, source_target_pairs={{4,0},{0,4},{6,2},{2,6},{13,9},{9,13},{15,11},{11,15},{20,16},{16,... | collective-permute-start | bytes 552968 | tf_op jit(solution)/shard_map/ppermute | solution.py:430
  14.3 12.8 %collective-permute-start.6 = (bf16[5,144,128]{2,1,0:T(8,128)(2,1)}, bf16[5,144,128]{2,1,0:T(8,128)(2,1)S(1)}, u32[]{:S(2)}, u32[]{:S(2)}) collective-permute-start(bf16[5,144,128]{2,1,0:T(8,128)(2,1)} %get-tuple-element.28), channel_id=1, source_target_pairs={{7,0},{3,4},{1,2},{5,6},{10,9},{14,13},{12,11},{8,15},{23,16},{19,... | collective-permute-start | bytes 552968 | tf_op jit(solution)/shard_map/ppermute | solution.py:430
  15.6 11.9 %collective-permute-start.5 = (bf16[5,144,128]{2,1,0:T(8,128)(2,1)}, bf16[5,144,128]{2,1,0:T(8,128)(2,1)S(1)}, u32[]{:S(2)}, u32[]{:S(2)}) collective-permute-start(bf16[5,144,128]{2,1,0:T(8,128)(2,1)} %get-tuple-element.28), channel_id=1, source_target_pairs={{6,0},{2,4},{0,2},{4,6},{11,9},{15,13},{13,11},{9,15},{22,16},{18,... | collective-permute-start | bytes 552968 | tf_op jit(solution)/shard_map/ppermute | solution.py:430
  20.5 1.0 copy-start
  27.5 0.9 copy-start.1
  38.4 10.9 %collective-permute-start.10 = (bf16[8,144,128]{2,1,0:T(8,128)(2,1)S(1)}, bf16[8,144,128]{2,1,0:T(8,128)(2,1)S(1)}, u32[]{:S(2)}, u32[]{:S(2)}) collective-permute-start(bf16[8,144,128]{2,1,0:T(8,128)(2,1)S(1)} %get-tuple-element.30.refs_6_), channel_id=1, source_target_pairs={{0,4},{4,2},{2,6},{6,9},{9,13},{13,11},{11,15},{15,16},{16,20},{20... | collective-permute-start | bytes 884744 | tf_op jit(solution)/shard_map/ppermute | solution.py:473
  40.3 14.2 %collective-permute-start.9 = (bf16[8,144,128]{2,1,0:T(8,128)(2,1)S(1)}, bf16[8,144,128]{2,1,0:T(8,128)(2,1)S(1)}, u32[]{:S(2)}, u32[]{:S(2)}) collective-permute-start(bf16[8,144,128]{2,1,0:T(8,128)(2,1)S(1)} %get-tuple-element.30.refs_6_), channel_id=1, source_target_pairs={{0,2},{4,6},{2,9},{6,13},{9,11},{13,15},{11,16},{15,20},{16,18},{2... | collective-permute-start | bytes 884744 | tf_op jit(solution)/shard_map/ppermute | solution.py:473
  43.1 13.7 %collective-permute-start.8 = (bf16[8,144,128]{2,1,0:T(8,128)(2,1)S(1)}, bf16[8,144,128]{2,1,0:T(8,128)(2,1)S(1)}, u32[]{:S(2)}, u32[]{:S(2)}) collective-permute-start(bf16[8,144,128]{2,1,0:T(8,128)(2,1)S(1)} %get-tuple-element.30.refs_6_), channel_id=1, source_target_pairs={{0,6},{4,9},{2,13},{6,11},{9,15},{13,16},{11,20},{15,18},{16,22},{... | collective-permute-start | bytes 884744 | tf_op jit(solution)/shard_map/ppermute | solution.py:473
  45.0 13.6 %collective-permute-start.7 = (bf16[8,144,128]{2,1,0:T(8,128)(2,1)S(1)}, bf16[8,144,128]{2,1,0:T(8,128)(2,1)S(1)}, u32[]{:S(2)}, u32[]{:S(2)}) collective-permute-start(bf16[8,144,128]{2,1,0:T(8,128)(2,1)S(1)} %get-tuple-element.30.refs_6_), channel_id=1, source_target_pairs={{0,9},{4,13},{2,11},{6,15},{9,16},{13,20},{11,18},{15,22},{16,25},... | collective-permute-start | bytes 884744 | tf_op jit(solution)/shard_map/ppermute | solution.py:473
  58.7 8.9 %collective-permute-start.11 = (bf16[8,144,128]{2,1,0:T(8,128)(2,1)S(1)}, bf16[8,144,128]{2,1,0:T(8,128)(2,1)S(1)}, u32[]{:S(2)}, u32[]{:S(2)}) collective-permute-start(bf16[8,144,128]{2,1,0:T(8,128)(2,1)S(1)} %near.1), channel_id=1, source_target_pairs={{0,25},{4,29},{2,27},{6,31}} | collective-permute-start | bytes 884744 | tf_op jit(solution)/shard_map/ppermute | solution.py:473
  60.0 16.8 %collective-permute-start.12 = (bf16[8,144,128]{2,1,0:T(8,128)(2,1)S(1)}, bf16[8,144,128]{2,1,0:T(8,128)(2,1)S(1)}, u32[]{:S(2)}, u32[]{:S(2)}) collective-permute-start(bf16[8,144,128]{2,1,0:T(8,128)(2,1)S(1)} %near.1), channel_id=1, source_target_pairs={{0,16},{4,20},{2,18},{6,22},{9,25},{13,29},{11,27},{15,31}} | collective-permute-start | bytes 884744 | tf_op jit(solution)/shard_map/ppermute | solution.py:473
  61.3 24.6 %collective-permute-start.13 = (bf16[8,144,128]{2,1,0:T(8,128)(2,1)S(1)}, bf16[8,144,128]{2,1,0:T(8,128)(2,1)S(1)}, u32[]{:S(2)}, u32[]{:S(2)}) collective-permute-start(bf16[8,144,128]{2,1,0:T(8,128)(2,1)S(1)} %near.1), channel_id=1, source_target_pairs={{0,9},{4,13},{2,11},{6,15},{9,16},{13,20},{11,18},{15,22},{16,25},... | collective-permute-start | bytes 884744 | tf_op jit(solution)/shard_map/ppermute | solution.py:473
  104.4 9.4 %collective-permute-start.14 = (bf16[4,135,128]{2,1,0:T(8,128)(2,1)S(1)}, bf16[4,135,128]{2,1,0:T(8,128)(2,1)S(1)}, u32[]{:S(2)}, u32[]{:S(2)}) collective-permute-start(bf16[4,135,128]{2,1,0:T(8,128)(2,1)S(1)} %get-tuple-element.38), channel_id=1, source_target_pairs={{0,1},{4,5},{2,3},{6,7},{9,8},{13,12},{11,10},{15,14},{16,17},{20,... | collective-permute-start | bytes 414728 | tf_op jit(solution)/shard_map/ppermute | solution.py:531
  105.7 10.0 %collective-permute-start.15 = (bf16[4,135,128]{2,1,0:T(8,128)(2,1)S(1)}, bf16[4,135,128]{2,1,0:T(8,128)(2,1)S(1)}, u32[]{:S(2)}, u32[]{:S(2)}) collective-permute-start(bf16[4,135,128]{2,1,0:T(8,128)(2,1)S(1)} %get-tuple-element.39), channel_id=1, source_target_pairs={{0,3},{4,7},{2,5},{6,1},{9,14},{13,10},{11,8},{15,12},{16,19},{20,... | collective-permute-start | bytes 414728 | tf_op jit(solution)/shard_map/ppermute | solution.py:531
  107.0 10.9 %collective-permute-start.16 = (bf16[4,135,128]{2,1,0:T(8,128)(2,1)S(1)}, bf16[4,135,128]{2,1,0:T(8,128)(2,1)S(1)}, u32[]{:S(2)}, u32[]{:S(2)}) collective-permute-start(bf16[4,135,128]{2,1,0:T(8,128)(2,1)S(1)} %get-tuple-element.40), channel_id=1, source_target_pairs={{0,5},{4,1},{2,7},{6,3},{9,12},{13,8},{11,14},{15,10},{16,21},{20,... | collective-permute-start | bytes 414728 | tf_op jit(solution)/shard_map/ppermute | solution.py:531
  108.3 9.6 %collective-permute-start.17 = (bf16[4,135,128]{2,1,0:T(8,128)(2,1)S(1)}, bf16[4,135,128]{2,1,0:T(8,128)(2,1)S(1)}, u32[]{:S(2)}, u32[]{:S(2)}) collective-permute-start(bf16[4,135,128]{2,1,0:T(8,128)(2,1)S(1)} %get-tuple-element.41), channel_id=1, source_target_pairs={{0,7},{4,3},{2,1},{6,5},{9,10},{13,14},{11,12},{15,8},{16,23},{20,... | collective-permute-start | bytes 414728 | tf_op jit(solution)/shard_map/ppermute | solution.py:531
  109.6 8.3 %collective-permute-start.18 = (bf16[4,135,128]{2,1,0:T(8,128)(2,1)S(1)}, bf16[4,135,128]{2,1,0:T(8,128)(2,1)S(1)}, u32[]{:S(2)}, u32[]{:S(2)}) collective-permute-start(bf16[4,135,128]{2,1,0:T(8,128)(2,1)S(1)} %get-tuple-element.42), channel_id=1, source_target_pairs={{0,2},{4,6},{2,4},{6,0},{9,15},{13,11},{11,9},{15,13},{16,18},{20,... | collective-permute-start | bytes 414728 | tf_op jit(solution)/shard_map/ppermute | solution.py:531
  113.8 7.2 %collective-permute-start.19 = (bf16[4,135,128]{2,1,0:T(8,128)(2,1)S(1)}, bf16[4,135,128]{2,1,0:T(8,128)(2,1)S(1)}, u32[]{:S(2)}, u32[]{:S(2)}) collective-permute-start(bf16[4,135,128]{2,1,0:T(8,128)(2,1)S(1)} %get-tuple-element.43), channel_id=1, source_target_pairs={{0,4},{4,0},{2,6},{6,2},{9,13},{13,9},{11,15},{15,11},{16,20},{20,... | collective-permute-start | bytes 414728 | tf_op jit(solution)/shard_map/ppermute | solution.py:531
  115.7 7.6 %collective-permute-start.20 = (bf16[4,135,128]{2,1,0:T(8,128)(2,1)S(1)}, bf16[4,135,128]{2,1,0:T(8,128)(2,1)S(1)}, u32[]{:S(2)}, u32[]{:S(2)}) collective-permute-start(bf16[4,135,128]{2,1,0:T(8,128)(2,1)S(1)} %get-tuple-element.44), channel_id=1, source_target_pairs={{0,6},{4,2},{2,0},{6,4},{9,11},{13,15},{11,13},{15,9},{16,22},{20,... | collective-permute-start | bytes 414728 | tf_op jit(solution)/shard_map/ppermute | solution.py:531

commit v7 on v6

--- a/solution.py
+++ b/solution.py
@@ -374,8 +374,9 @@
         ).wait()
 
 
-def fold_kernel(fine, coarse, coupling, fine_table, coarse_table, wide):
+def fold_kernel(fine, coarse, coupling, message, fine_table, coarse_table, own, wide):
     faces, width, _ = coupling.shape
+    own[...] = message[...]
     wide[...] = jnp.zeros(wide.shape, F32)
     for face in range(faces):
         wide[:width, face * ROWS : face * ROWS + width] = -coupling[face].astype(F32)
@@ -430,15 +431,15 @@
         received[turn] = lax.ppermute(messages[turn // stride], ("tm", "space"), pairs)
 
     table_shape = jax.ShapeDtypeStruct((ROWS + PROWS, (faces + 1) * ROWS), BF)
-    fine_table, coarse_table = pl.pallas_call(
+    fine_table, coarse_table, received[0] = pl.pallas_call(
         fold_kernel,
-        out_shape=[table_shape] * 2,
-        in_specs=[VMEM] * 3,
-        out_specs=[VMEM] * 2,
+        out_shape=[table_shape] * 2 + [message_shape],
+        in_specs=[VMEM] * 4,
+        out_specs=[VMEM] * 3,
         scratch_shapes=[pltpu.VMEM((ROWS, (faces + 1) * ROWS), F32)],
         compiler_params=params,
         name="fold",
-    )(block_inv, coarse_inv, coupling)
+    )(block_inv, coarse_inv, coupling, messages[0])
 
     gather_shape = jax.ShapeDtypeStruct((space, 2 * LANES, (faces - PICKED) * LANES), BF)
     listing_shape = jax.ShapeDtypeStruct((space // 2, 2 * LANES, 2 * LANES), BF)

time: 126 us -> 125 us (level)
  transfers between devices with their start and end apart: 21 -> 21, of which waited for: 11 -> 10; matrix products, arithmetic and copies ran while one was open for 1% -> 1% of each run, Pallas kernels for 15% -> 15%
where the time goes in v7:
time: 125 us; the launch traced here: 124 us
  Pallas kernels  50.6 us (40%)
  starting transfers between devices  40.9 us (33%)
  waiting for transfers between devices  27 us (22%)
  local copies, waits for them, and re-layouts  4.65 us (4%)
    pallas_call x1, Pallas kernels, shards(): pl.pallas_call(functools.partial(final_kernel, space, intervals, width, f...  18.5 us
    pallas_call x3, Pallas kernels, chain(): pl.pallas_call(functools.partial(kernel, space, intervals, number, faces)...  18.3 us
    ppermute x7, waiting for transfers between devices, from_earlier(): return lax.ppermute(value, ('tm', 'space'), pairs)  17.3 us
    ppermute x7, starting transfers between devices, shards(): lax.ppermute(messages[turn // stride], ('tm', 'space'), pairs)  15.6 us
    ppermute x7, starting transfers between devices, shards(): returned[turn] = lax.ppermute(pieces[turn], ('tm', 'space'), pairs)  13.5 us
    ppermute x7, starting transfers between devices, from_earlier(): return lax.ppermute(value, ('tm', 'space'), pairs)  11.9 us
    pallas_call x1, Pallas kernels, shards(): pl.pallas_call(functools.partial(fine_kernel, space, intervals, width, fa...  9.88 us
    ppermute x7, waiting for transfers between devices, shards(): returned[turn] = lax.ppermute(pieces[turn], ('tm', 'space'), pairs)  5.38 us
  transfers between devices with their start and end apart: 21, of which 10 were waited for; matrix products, arithmetic and copies ran while one was open for 1% of the time, Pallas kernels for 15%

profile of v7, /device:TPU:7, one launch (start us, length us, event | category | flops | bytes accessed | tf_op | source)
XLA Modules:
  0.0 124.2 jit_solution(5333954173901459453)
XLA Ops:
  0.7 2.3 %pack.1 = (bf16[5,144,128]{2,1,0:T(8,128)(2,1)}, bf16[5,144,128]{2,1,0:T(8,128)(2,1)}, bf16[5,144,128]{2,1,0:T(8,128)(2,1)}, bf16[5,144,128]{2,1,0:T(8,128)(2,1)}) custom-call(s32[1]{0:T(128)S(6)} %copy.13.etype, bf16[135,16,128]{2,1,0:T(8,128)(2,1)} %bitcast.3, bf16[135,128]{1,0:T(8,128)(2,1)} %refs_1_.1, f32[1,128]{1,0:T(1,128)} %bitcast.4, ...), custom_call_target="tpu_custom_call" | custom-call | tf_op jit(solution)/shard_map/pack/pallas_call | solution.py:407
  3.0 1.3 %collective-permute-start = (bf16[5,144,128]{2,1,0:T(8,128)(2,1)}, bf16[5,144,128]{2,1,0:T(8,128)(2,1)S(1)}, u32[]{:S(2)}, u32[]{:S(2)}) collective-permute-start(bf16[5,144,128]{2,1,0:T(8,128)(2,1)} %get-tuple-element.26.message), channel_id=1, source_target_pairs={{1,0},{5,4},{3,2},{7,6},{8,9},{12,13},{10,11},{14,15},{17,16},{21,... | collective-permute-start | bytes 552968 | tf_op jit(solution)/shard_map/ppermute | solution.py:431
  4.3 1.3 %collective-permute-start.2 = (bf16[5,144,128]{2,1,0:T(8,128)(2,1)}, bf16[5,144,128]{2,1,0:T(8,128)(2,1)S(1)}, u32[]{:S(2)}, u32[]{:S(2)}) collective-permute-start(bf16[5,144,128]{2,1,0:T(8,128)(2,1)} %get-tuple-element.28), channel_id=1, source_target_pairs={{3,0},{7,4},{5,2},{1,6},{14,9},{10,13},{8,11},{12,15},{19,16},{23,... | collective-permute-start | bytes 552968 | tf_op jit(solution)/shard_map/ppermute | solution.py:431
  5.6 3.2 %collective-permute-start.1 = (bf16[5,144,128]{2,1,0:T(8,128)(2,1)}, bf16[5,144,128]{2,1,0:T(8,128)(2,1)S(1)}, u32[]{:S(2)}, u32[]{:S(2)}) collective-permute-start(bf16[5,144,128]{2,1,0:T(8,128)(2,1)} %get-tuple-element.28), channel_id=1, source_target_pairs={{2,0},{6,4},{4,2},{0,6},{15,9},{11,13},{9,11},{13,15},{18,16},{22,... | collective-permute-start | bytes 552968 | tf_op jit(solution)/shard_map/ppermute | solution.py:431
  8.8 1.3 %collective-permute-start.4 = (bf16[5,144,128]{2,1,0:T(8,128)(2,1)}, bf16[5,144,128]{2,1,0:T(8,128)(2,1)S(1)}, u32[]{:S(2)}, u32[]{:S(2)}) collective-permute-start(bf16[5,144,128]{2,1,0:T(8,128)(2,1)} %get-tuple-element.29), channel_id=1, source_target_pairs={{5,0},{1,4},{7,2},{3,6},{12,9},{8,13},{14,11},{10,15},{21,16},{17,... | collective-permute-start | bytes 552968 | tf_op jit(solution)/shard_map/ppermute | solution.py:431
  10.1 4.2 %collective-permute-start.3 = (bf16[5,144,128]{2,1,0:T(8,128)(2,1)}, bf16[5,144,128]{2,1,0:T(8,128)(2,1)S(1)}, u32[]{:S(2)}, u32[]{:S(2)}) collective-permute-start(bf16[5,144,128]{2,1,0:T(8,128)(2,1)} %get-tuple-element.29), channel_id=1, source_target_pairs={{4,0},{0,4},{6,2},{2,6},{13,9},{9,13},{15,11},{11,15},{20,16},{16,... | collective-permute-start | bytes 552968 | tf_op jit(solution)/shard_map/ppermute | solution.py:431
  14.3 0.0 collective-permute-done.refs_1_
  14.3 1.3 %collective-permute-start.6 = (bf16[5,144,128]{2,1,0:T(8,128)(2,1)}, bf16[5,144,128]{2,1,0:T(8,128)(2,1)S(1)}, u32[]{:S(2)}, u32[]{:S(2)}) collective-permute-start(bf16[5,144,128]{2,1,0:T(8,128)(2,1)} %get-tuple-element.30), channel_id=1, source_target_pairs={{7,0},{3,4},{1,2},{5,6},{10,9},{14,13},{12,11},{8,15},{23,16},{19,... | collective-permute-start | bytes 552968 | tf_op jit(solution)/shard_map/ppermute | solution.py:431
  15.6 3.0 %collective-permute-start.5 = (bf16[5,144,128]{2,1,0:T(8,128)(2,1)}, bf16[5,144,128]{2,1,0:T(8,128)(2,1)S(1)}, u32[]{:S(2)}, u32[]{:S(2)}) collective-permute-start(bf16[5,144,128]{2,1,0:T(8,128)(2,1)} %get-tuple-element.30), channel_id=1, source_target_pairs={{6,0},{2,4},{0,2},{4,6},{11,9},{15,13},{13,11},{9,15},{22,16},{18,... | collective-permute-start | bytes 552968 | tf_op jit(solution)/shard_map/ppermute | solution.py:431
  18.6 0.9 copy.10.fine
  19.6 0.9 copy.11.coarse
  20.5 0.0 copy-start
  20.5 1.0 copy-done
  21.5 0.9 copy-done.1
  22.4 0.8 fold.1
  23.2 0.0 collective-permute-done.4.refs_5_
  23.2 2.2 %collective-permute-done.3.refs_4_ = bf16[5,144,128]{2,1,0:T(8,128)(2,1)S(1)} collective-permute-done((bf16[5,144,128]{2,1,0:T(8,128)(2,1)}, bf16[5,144,128]{2,1,0:T(8,128)(2,1)S(1)}, u32[]{:S(2)}, u32[]{:S(2)}) %collective-permute-start.3) | collective-permute-done | bytes 184352 | tf_op jit(solution)/shard_map/ppermute | solution.py:431
  25.4 1.7 %collective-permute-done.6.refs_7_ = bf16[5,144,128]{2,1,0:T(8,128)(2,1)S(1)} collective-permute-done((bf16[5,144,128]{2,1,0:T(8,128)(2,1)}, bf16[5,144,128]{2,1,0:T(8,128)(2,1)S(1)}, u32[]{:S(2)}, u32[]{:S(2)}) %collective-permute-start.6) | collective-permute-done | bytes 184352 | tf_op jit(solution)/shard_map/ppermute | solution.py:431
  27.1 0.4 collective-permute-done.5.refs_6_
  27.5 9.9 %fine.2 = (bf16[8,144,128]{2,1,0:T(8,128)(2,1)S(1)}, bf16[8,256,512]{2,1,0:T(8,128)(2,1)S(1)}, bf16[4,256,256]{2,1,0:T(8,128)(2,1)S(1)}, f32[8,8,128]{2,1,0:T(8,...) custom-call(bf16[5,144,128]{2,1,0:T(8,128)(2,1)S(1)} %get-tuple-element.27.refs_0_, ...), custom_call_target="tpu_custom_call" | custom-call | tf_op jit(solution)/shard_map/fine/pallas_call | solution.py:453
  37.4 1.9 %collective-permute-start.10 = (bf16[8,144,128]{2,1,0:T(8,128)(2,1)S(1)}, bf16[8,144,128]{2,1,0:T(8,128)(2,1)S(1)}, u32[]{:S(2)}, u32[]{:S(2)}) collective-permute-start(bf16[8,144,128]{2,1,0:T(8,128)(2,1)S(1)} %get-tuple-element.32.refs_6_), channel_id=1, source_target_pairs={{0,4},{4,2},{2,6},{6,9},{9,13},{13,11},{11,15},{15,16},{16,20},{20... | collective-permute-start | bytes 884744 | tf_op jit(solution)/shard_map/ppermute | solution.py:474
  39.4 2.9 %collective-permute-start.9 = (bf16[8,144,128]{2,1,0:T(8,128)(2,1)S(1)}, bf16[8,144,128]{2,1,0:T(8,128)(2,1)S(1)}, u32[]{:S(2)}, u32[]{:S(2)}) collective-permute-start(bf16[8,144,128]{2,1,0:T(8,128)(2,1)S(1)} %get-tuple-element.32.refs_6_), channel_id=1, source_target_pairs={{0,2},{4,6},{2,9},{6,13},{9,11},{13,15},{11,16},{15,20},{16,18},{2... | collective-permute-start | bytes 884744 | tf_op jit(solution)/shard_map/ppermute | solution.py:474
  42.2 1.9 %collective-permute-start.8 = (bf16[8,144,128]{2,1,0:T(8,128)(2,1)S(1)}, bf16[8,144,128]{2,1,0:T(8,128)(2,1)S(1)}, u32[]{:S(2)}, u32[]{:S(2)}) collective-permute-start(bf16[8,144,128]{2,1,0:T(8,128)(2,1)S(1)} %get-tuple-element.32.refs_6_), channel_id=1, source_target_pairs={{0,6},{4,9},{2,13},{6,11},{9,15},{13,16},{11,20},{15,18},{16,22},{... | collective-permute-start | bytes 884744 | tf_op jit(solution)/shard_map/ppermute | solution.py:474
  44.2 1.3 %collective-permute-start.7 = (bf16[8,144,128]{2,1,0:T(8,128)(2,1)S(1)}, bf16[8,144,128]{2,1,0:T(8,128)(2,1)S(1)}, u32[]{:S(2)}, u32[]{:S(2)}) collective-permute-start(bf16[8,144,128]{2,1,0:T(8,128)(2,1)S(1)} %get-tuple-element.32.refs_6_), channel_id=1, source_target_pairs={{0,9},{4,13},{2,11},{6,15},{9,16},{13,20},{11,18},{15,22},{16,25},... | collective-permute-start | bytes 884744 | tf_op jit(solution)/shard_map/ppermute | solution.py:474
  45.5 2.9 %collective-permute-done.10.refs_3_ = bf16[8,144,128]{2,1,0:T(8,128)(2,1)S(1)} collective-permute-done((bf16[8,144,128]{2,1,0:T(8,128)(2,1)S(1)}, bf16[8,144,128]{2,1,0:T(8,128)(2,1)S(1)}, u32[]{:S(2)}, u32[]{:S(2)}) %collective-permute-start.10) | collective-permute-done | bytes 294944 | tf_op jit(solution)/shard_map/ppermute | solution.py:474
  48.4 5.2 %collective-permute-done.9.refs_2_ = bf16[8,144,128]{2,1,0:T(8,128)(2,1)S(1)} collective-permute-done((bf16[8,144,128]{2,1,0:T(8,128)(2,1)S(1)}, bf16[8,144,128]{2,1,0:T(8,128)(2,1)S(1)}, u32[]{:S(2)}, u32[]{:S(2)}) %collective-permute-start.9) | collective-permute-done | bytes 294944 | tf_op jit(solution)/shard_map/ppermute | solution.py:474
  53.5 2.3 %collective-permute-done.8.refs_1_ = bf16[8,144,128]{2,1,0:T(8,128)(2,1)S(1)} collective-permute-done((bf16[8,144,128]{2,1,0:T(8,128)(2,1)S(1)}, bf16[8,144,128]{2,1,0:T(8,128)(2,1)S(1)}, u32[]{:S(2)}, u32[]{:S(2)}) %collective-permute-start.8) | collective-permute-done | bytes 294944 | tf_op jit(solution)/shard_map/ppermute | solution.py:474
  55.9 1.9 %collective-permute-done.7.refs_0_ = bf16[8,144,128]{2,1,0:T(8,128)(2,1)S(1)} collective-permute-done((bf16[8,144,128]{2,1,0:T(8,128)(2,1)S(1)}, bf16[8,144,128]{2,1,0:T(8,128)(2,1)S(1)}, u32[]{:S(2)}, u32[]{:S(2)}) %collective-permute-start.7) | collective-permute-done | bytes 294944 | tf_op jit(solution)/shard_map/ppermute | solution.py:474
  57.7 1.3 %collective-permute-start.11 = (bf16[8,144,128]{2,1,0:T(8,128)(2,1)S(1)}, bf16[8,144,128]{2,1,0:T(8,128)(2,1)S(1)}, u32[]{:S(2)}, u32[]{:S(2)}) collective-permute-start(bf16[8,144,128]{2,1,0:T(8,128)(2,1)S(1)} %near.1), channel_id=1, source_target_pairs={{0,25},{4,29},{2,27},{6,31}} | collective-permute-start | bytes 884744 | tf_op jit(solution)/shard_map/ppermute | solution.py:474
  59.0 1.3 %collective-permute-start.12 = (bf16[8,144,128]{2,1,0:T(8,128)(2,1)S(1)}, bf16[8,144,128]{2,1,0:T(8,128)(2,1)S(1)}, u32[]{:S(2)}, u32[]{:S(2)}) collective-permute-start(bf16[8,144,128]{2,1,0:T(8,128)(2,1)S(1)} %near.1), channel_id=1, source_target_pairs={{0,16},{4,20},{2,18},{6,22},{9,25},{13,29},{11,27},{15,31}} | collective-permute-start | bytes 884744 | tf_op jit(solution)/shard_map/ppermute | solution.py:474
  60.3 1.3 %collective-permute-start.13 = (bf16[8,144,128]{2,1,0:T(8,128)(2,1)S(1)}, bf16[8,144,128]{2,1,0:T(8,128)(2,1)S(1)}, u32[]{:S(2)}, u32[]{:S(2)}) collective-permute-start(bf16[8,144,128]{2,1,0:T(8,128)(2,1)S(1)} %near.1), channel_id=1, source_target_pairs={{0,9},{4,13},{2,11},{6,15},{9,16},{13,20},{11,18},{15,22},{16,25},... | collective-permute-start | bytes 884744 | tf_op jit(solution)/shard_map/ppermute | solution.py:474
  61.6 5.0 %collective-permute-done.11.refs_0_ = bf16[8,144,128]{2,1,0:T(8,128)(2,1)S(1)} collective-permute-done((bf16[8,144,128]{2,1,0:T(8,128)(2,1)S(1)}, bf16[8,144,128]{2,1,0:T(8,128)(2,1)S(1)}, u32[]{:S(2)}, u32[]{:S(2)}) %collective-permute-start.11) | collective-permute-done | bytes 294944 | tf_op jit(solution)/shard_map/ppermute | solution.py:474
  66.7 9.1 %far.2.refs_0_ = bf16[8,144,128]{2,1,0:T(8,128)(2,1)S(1)} custom-call(bf16[8,144,128]{2,1,0:T(8,128)(2,1)S(1)} %collective-permute-done.11.refs_0_, bf16[240,1008]{1,0:T(8,128)(2,1)S(1)} %get-tuple-element.33.refs_4_.refs_1_.refs_2_.refs_10_, bf16[8,256,512]{2,1,0:T(8,128)(2,1)S(1)} %get-tuple-element.34.refs_5_.refs_2_.refs_3_.refs_11_, ...), custom_call_target="tpu_custom_call" | custom-call | tf_op jit(solution)/shard_map/far/pallas_call | solution.py:477
  75.8 0.0 collective-permute-done.12.refs_1_
  75.8 9.2 %far.3.refs_4_ = bf16[8,144,128]{2,1,0:T(8,128)(2,1)S(1)} custom-call(bf16[8,144,128]{2,1,0:T(8,128)(2,1)S(1)} %far.2.refs_0_, bf16[8,144,128]{2,1,0:T(8,128)(2,1)S(1)} %collective-permute-done.12.refs_1_, bf16[240,1008]{1,0:T(8,128)(2,1)S(1)} %get-tuple-element.33.refs_4_.refs_1_.refs_2_.refs_10_, ...), custom_call_target="tpu_custom_call" | custom-call | tf_op jit(solution)/shard_map/far/pallas_call | solution.py:477
  85.0 18.5 %final.1 = (bf16[4,135,128]{2,1,0:T(8,128)(2,1)S(1)}, bf16[4,135,128]{2,1,0:T(8,128)(2,1)S(1)}, bf16[4,135,128]{2,1,0:T(8,128)(2,1)S(1)}, bf16[4,135,128]{2,1,0:...) custom-call(bf16[8,144,128]{2,1,0:T(8,128)(2,1)S(1)} %collective-per, ...), custom_call_target="tpu_custom_call" | custom-call | tf_op jit(solution)/shard_map/final/pallas_call | solution.py:497
  103.5 1.3 %collective-permute-start.14 = (bf16[4,135,128]{2,1,0:T(8,128)(2,1)S(1)}, bf16[4,135,128]{2,1,0:T(8,128)(2,1)S(1)}, u32[]{:S(2)}, u32[]{:S(2)}) collective-permute-start(bf16[4,135,128]{2,1,0:T(8,128)(2,1)S(1)} %get-tuple-element.40), channel_id=1, source_target_pairs={{0,1},{4,5},{2,3},{6,7},{9,8},{13,12},{11,10},{15,14},{16,17},{20,... | collective-permute-start | bytes 414728 | tf_op jit(solution)/shard_map/ppermute | solution.py:532
  104.8 1.3 %collective-permute-start.15 = (bf16[4,135,128]{2,1,0:T(8,128)(2,1)S(1)}, bf16[4,135,128]{2,1,0:T(8,128)(2,1)S(1)}, u32[]{:S(2)}, u32[]{:S(2)}) collective-permute-start(bf16[4,135,128]{2,1,0:T(8,128)(2,1)S(1)} %get-tuple-element.41), channel_id=1, source_target_pairs={{0,3},{4,7},{2,5},{6,1},{9,14},{13,10},{11,8},{15,12},{16,19},{20,... | collective-permute-start | bytes 414728 | tf_op jit(solution)/shard_map/ppermute | solution.py:532
  106.1 1.3 %collective-permute-start.16 = (bf16[4,135,128]{2,1,0:T(8,128)(2,1)S(1)}, bf16[4,135,128]{2,1,0:T(8,128)(2,1)S(1)}, u32[]{:S(2)}, u32[]{:S(2)}) collective-permute-start(bf16[4,135,128]{2,1,0:T(8,128)(2,1)S(1)} %get-tuple-element.42), channel_id=1, source_target_pairs={{0,5},{4,1},{2,7},{6,3},{9,12},{13,8},{11,14},{15,10},{16,21},{20,... | collective-permute-start | bytes 414728 | tf_op jit(solution)/shard_map/ppermute | solution.py:532
  107.4 1.3 %collective-permute-start.17 = (bf16[4,135,128]{2,1,0:T(8,128)(2,1)S(1)}, bf16[4,135,128]{2,1,0:T(8,128)(2,1)S(1)}, u32[]{:S(2)}, u32[]{:S(2)}) collective-permute-start(bf16[4,135,128]{2,1,0:T(8,128)(2,1)S(1)} %get-tuple-element.43), channel_id=1, source_target_pairs={{0,7},{4,3},{2,1},{6,5},{9,10},{13,14},{11,12},{15,8},{16,23},{20,... | collective-permute-start | bytes 414728 | tf_op jit(solution)/shard_map/ppermute | solution.py:532
  108.7 4.2 %collective-permute-start.18 = (bf16[4,135,128]{2,1,0:T(8,128)(2,1)S(1)}, bf16[4,135,128]{2,1,0:T(8,128)(2,1)S(1)}, u32[]{:S(2)}, u32[]{:S(2)}) collective-permute-start(bf16[4,135,128]{2,1,0:T(8,128)(2,1)S(1)} %get-tuple-element.44), channel_id=1, source_target_pairs={{0,2},{4,6},{2,4},{6,0},{9,15},{13,11},{11,9},{15,13},{16,18},{20,... | collective-permute-start | bytes 414728 | tf_op jit(solution)/shard_map/ppermute | solution.py:532
  112.9 1.9 %collective-permute-start.19 = (bf16[4,135,128]{2,1,0:T(8,128)(2,1)S(1)}, bf16[4,135,128]{2,1,0:T(8,128)(2,1)S(1)}, u32[]{:S(2)}, u32[]{:S(2)}) collective-permute-start(bf16[4,135,128]{2,1,0:T(8,128)(2,1)S(1)} %get-tuple-element.45), channel_id=1, source_target_pairs={{0,4},{4,0},{2,6},{6,2},{9,13},{13,9},{11,15},{15,11},{16,20},{20,... | collective-permute-start | bytes 414728 | tf_op jit(solution)/shard_map/ppermute | solution.py:532
  114.8 0.0 collective-permute-done.15.refs_2_
  114.8 2.2 %collective-permute-start.20 = (bf16[4,135,128]{2,1,0:T(8,128)(2,1)S(1)}, bf16[4,135,128]{2,1,0:T(8,128)(2,1)S(1)}, u32[]{:S(2)}, u32[]{:S(2)}) collective-permute-start(bf16[4,135,128]{2,1,0:T(8,128)(2,1)S(1)} %get-tuple-element.46), channel_id=1, source_target_pairs={{0,6},{4,2},{2,0},{6,4},{9,11},{13,15},{11,13},{15,9},{16,22},{20,... | collective-permute-start | bytes 414728 | tf_op jit(solution)/shard_map/ppermute | solution.py:532
  117.0 3.0 %collective-permute-done.19.refs_6_ = bf16[4,135,128]{2,1,0:T(8,128)(2,1)S(1)} collective-permute-done((bf16[4,135,128]{2,1,0:T(8,128)(2,1)S(1)}, bf16[4,135,128]{2,1,0:T(8,128)(2,1)S(1)}, u32[]{:S(2)}, u32[]{:S(2)}) %collective-permute-start.19) | collective-permute-done | bytes 138272 | tf_op jit(solution)/shard_map/ppermute | solution.py:532
  120.0 2.4 %collective-permute-done.20.refs_7_ = bf16[4,135,128]{2,1,0:T(8,128)(2,1)S(1)} collective-permute-done((bf16[4,135,128]{2,1,0:T(8,128)(2,1)S(1)}, bf16[4,135,128]{2,1,0:T(8,128)(2,1)S(1)}, u32[]{:S(2)}, u32[]{:S(2)}) %collective-permute-start.20) | collective-permute-done | bytes 138272 | tf_op jit(solution)/shard_map/ppermute | solution.py:532
  122.4 0.9 place.1
  123.3 0.9 copy.12
  (9 shorter events, 0.0 us)
Async XLA Ops:
  3.0 11.3 %collective-permute-start = (bf16[5,144,128]{2,1,0:T(8,128)(2,1)}, bf16[5,144,128]{2,1,0:T(8,128)(2,1)S(1)}, u32[]{:S(2)}, u32[]{:S(2)}) collective-permute-start(bf16[5,144,128]{2,1,0:T(8,128)(2,1)} %get-tuple-element.26.message), channel_id=1, source_target_pairs={{1,0},{5,4},{3,2},{7,6},{8,9},{12,13},{10,11},{14,15},{17,16},{21,... | collective-permute-start | bytes 552968 | tf_op jit(solution)/shard_map/ppermute | solution.py:431
  4.3 11.3 %collective-permute-start.2 = (bf16[5,144,128]{2,1,0:T(8,128)(2,1)}, bf16[5,144,128]{2,1,0:T(8,128)(2,1)S(1)}, u32[]{:S(2)}, u32[]{:S(2)}) collective-permute-start(bf16[5,144,128]{2,1,0:T(8,128)(2,1)} %get-tuple-element.28), channel_id=1, source_target_pairs={{3,0},{7,4},{5,2},{1,6},{14,9},{10,13},{8,11},{12,15},{19,16},{23,... | collective-permute-start | bytes 552968 | tf_op jit(solution)/shard_map/ppermute | solution.py:431
  5.6 17.6 %collective-permute-start.1 = (bf16[5,144,128]{2,1,0:T(8,128)(2,1)}, bf16[5,144,128]{2,1,0:T(8,128)(2,1)S(1)}, u32[]{:S(2)}, u32[]{:S(2)}) collective-permute-start(bf16[5,144,128]{2,1,0:T(8,128)(2,1)} %get-tuple-element.28), channel_id=1, source_target_pairs={{2,0},{6,4},{4,2},{0,6},{15,9},{11,13},{9,11},{13,15},{18,16},{22,... | collective-permute-start | bytes 552968 | tf_op jit(solution)/shard_map/ppermute | solution.py:431
  8.8 14.4 %collective-permute-start.4 = (bf16[5,144,128]{2,1,0:T(8,128)(2,1)}, bf16[5,144,128]{2,1,0:T(8,128)(2,1)S(1)}, u32[]{:S(2)}, u32[]{:S(2)}) collective-permute-start(bf16[5,144,128]{2,1,0:T(8,128)(2,1)} %get-tuple-element.29), channel_id=1, source_target_pairs={{5,0},{1,4},{7,2},{3,6},{12,9},{8,13},{14,11},{10,15},{21,16},{17,... | collective-permute-start | bytes 552968 | tf_op jit(solution)/shard_map/ppermute | solution.py:431
  10.1 15.3 %collective-permute-start.3 = (bf16[5,144,128]{2,1,0:T(8,128)(2,1)}, bf16[5,144,128]{2,1,0:T(8,128)(2,1)S(1)}, u32[]{:S(2)}, u32[]{:S(2)}) collective-permute-start(bf16[5,144,128]{2,1,0:T(8,128)(2,1)} %get-tuple-element.29), channel_id=1, source_target_pairs={{4,0},{0,4},{6,2},{2,6},{13,9},{9,13},{15,11},{11,15},{20,16},{16,... | collective-permute-start | bytes 552968 | tf_op jit(solution)/shard_map/ppermute | solution.py:431
  14.3 12.8 %collective-permute-start.6 = (bf16[5,144,128]{2,1,0:T(8,128)(2,1)}, bf16[5,144,128]{2,1,0:T(8,128)(2,1)S(1)}, u32[]{:S(2)}, u32[]{:S(2)}) collective-permute-start(bf16[5,144,128]{2,1,0:T(8,128)(2,1)} %get-tuple-element.30), channel_id=1, source_target_pairs={{7,0},{3,4},{1,2},{5,6},{10,9},{14,13},{12,11},{8,15},{23,16},{19,... | collective-permute-start | bytes 552968 | tf_op jit(solution)/shard_map/ppermute | solution.py:431
  15.6 11.9 %collective-permute-start.5 = (bf16[5,144,128]{2,1,0:T(8,128)(2,1)}, bf16[5,144,128]{2,1,0:T(8,128)(2,1)S(1)}, u32[]{:S(2)}, u32[]{:S(2)}) collective-permute-start(bf16[5,144,128]{2,1,0:T(8,128)(2,1)} %get-tuple-element.30), channel_id=1, source_target_pairs={{6,0},{2,4},{0,2},{4,6},{11,9},{15,13},{13,11},{9,15},{22,16},{18,... | collective-permute-start | bytes 552968 | tf_op jit(solution)/shard_map/ppermute | solution.py:431
  20.5 1.0 copy-start
  21.5 0.9 copy-start.1
  37.4 10.9 %collective-permute-start.10 = (bf16[8,144,128]{2,1,0:T(8,128)(2,1)S(1)}, bf16[8,144,128]{2,1,0:T(8,128)(2,1)S(1)}, u32[]{:S(2)}, u32[]{:S(2)}) collective-permute-start(bf16[8,144,128]{2,1,0:T(8,128)(2,1)S(1)} %get-tuple-element.32.refs_6_), channel_id=1, source_target_pairs={{0,4},{4,2},{2,6},{6,9},{9,13},{13,11},{11,15},{15,16},{16,20},{20... | collective-permute-start | bytes 884744 | tf_op jit(solution)/shard_map/ppermute | solution.py:474
  39.4 14.2 %collective-permute-start.9 = (bf16[8,144,128]{2,1,0:T(8,128)(2,1)S(1)}, bf16[8,144,128]{2,1,0:T(8,128)(2,1)S(1)}, u32[]{:S(2)}, u32[]{:S(2)}) collective-permute-start(bf16[8,144,128]{2,1,0:T(8,128)(2,1)S(1)} %get-tuple-element.32.refs_6_), channel_id=1, source_target_pairs={{0,2},{4,6},{2,9},{6,13},{9,11},{13,15},{11,16},{15,20},{16,18},{2... | collective-permute-start | bytes 884744 | tf_op jit(solution)/shard_map/ppermute | solution.py:474
  42.2 13.6 %collective-permute-start.8 = (bf16[8,144,128]{2,1,0:T(8,128)(2,1)S(1)}, bf16[8,144,128]{2,1,0:T(8,128)(2,1)S(1)}, u32[]{:S(2)}, u32[]{:S(2)}) collective-permute-start(bf16[8,144,128]{2,1,0:T(8,128)(2,1)S(1)} %get-tuple-element.32.refs_6_), channel_id=1, source_target_pairs={{0,6},{4,9},{2,13},{6,11},{9,15},{13,16},{11,20},{15,18},{16,22},{... | collective-permute-start | bytes 884744 | tf_op jit(solution)/shard_map/ppermute | solution.py:474
  44.2 13.6 %collective-permute-start.7 = (bf16[8,144,128]{2,1,0:T(8,128)(2,1)S(1)}, bf16[8,144,128]{2,1,0:T(8,128)(2,1)S(1)}, u32[]{:S(2)}, u32[]{:S(2)}) collective-permute-start(bf16[8,144,128]{2,1,0:T(8,128)(2,1)S(1)} %get-tuple-element.32.refs_6_), channel_id=1, source_target_pairs={{0,9},{4,13},{2,11},{6,15},{9,16},{13,20},{11,18},{15,22},{16,25},... | collective-permute-start | bytes 884744 | tf_op jit(solution)/shard_map/ppermute | solution.py:474
  57.7 8.9 %collective-permute-start.11 = (bf16[8,144,128]{2,1,0:T(8,128)(2,1)S(1)}, bf16[8,144,128]{2,1,0:T(8,128)(2,1)S(1)}, u32[]{:S(2)}, u32[]{:S(2)}) collective-permute-start(bf16[8,144,128]{2,1,0:T(8,128)(2,1)S(1)} %near.1), channel_id=1, source_target_pairs={{0,25},{4,29},{2,27},{6,31}} | collective-permute-start | bytes 884744 | tf_op jit(solution)/shard_map/ppermute | solution.py:474
  59.0 16.8 %collective-permute-start.12 = (bf16[8,144,128]{2,1,0:T(8,128)(2,1)S(1)}, bf16[8,144,128]{2,1,0:T(8,128)(2,1)S(1)}, u32[]{:S(2)}, u32[]{:S(2)}) collective-permute-start(bf16[8,144,128]{2,1,0:T(8,128)(2,1)S(1)} %near.1), channel_id=1, source_target_pairs={{0,16},{4,20},{2,18},{6,22},{9,25},{13,29},{11,27},{15,31}} | collective-permute-start | bytes 884744 | tf_op jit(solution)/shard_map/ppermute | solution.py:474
  60.3 24.6 %collective-permute-start.13 = (bf16[8,144,128]{2,1,0:T(8,128)(2,1)S(1)}, bf16[8,144,128]{2,1,0:T(8,128)(2,1)S(1)}, u32[]{:S(2)}, u32[]{:S(2)}) collective-permute-start(bf16[8,144,128]{2,1,0:T(8,128)(2,1)S(1)} %near.1), channel_id=1, source_target_pairs={{0,9},{4,13},{2,11},{6,15},{9,16},{13,20},{11,18},{15,22},{16,25},... | collective-permute-start | bytes 884744 | tf_op jit(solution)/shard_map/ppermute | solution.py:474
  103.5 9.4 %collective-permute-start.14 = (bf16[4,135,128]{2,1,0:T(8,128)(2,1)S(1)}, bf16[4,135,128]{2,1,0:T(8,128)(2,1)S(1)}, u32[]{:S(2)}, u32[]{:S(2)}) collective-permute-start(bf16[4,135,128]{2,1,0:T(8,128)(2,1)S(1)} %get-tuple-element.40), channel_id=1, source_target_pairs={{0,1},{4,5},{2,3},{6,7},{9,8},{13,12},{11,10},{15,14},{16,17},{20,... | collective-permute-start | bytes 414728 | tf_op jit(solution)/shard_map/ppermute | solution.py:532
  104.8 10.0 %collective-permute-start.15 = (bf16[4,135,128]{2,1,0:T(8,128)(2,1)S(1)}, bf16[4,135,128]{2,1,0:T(8,128)(2,1)S(1)}, u32[]{:S(2)}, u32[]{:S(2)}) collective-permute-start(bf16[4,135,128]{2,1,0:T(8,128)(2,1)S(1)} %get-tuple-element.41), channel_id=1, source_target_pairs={{0,3},{4,7},{2,5},{6,1},{9,14},{13,10},{11,8},{15,12},{16,19},{20,... | collective-permute-start | bytes 414728 | tf_op jit(solution)/shard_map/ppermute | solution.py:532
  106.1 10.9 %collective-permute-start.16 = (bf16[4,135,128]{2,1,0:T(8,128)(2,1)S(1)}, bf16[4,135,128]{2,1,0:T(8,128)(2,1)S(1)}, u32[]{:S(2)}, u32[]{:S(2)}) collective-permute-start(bf16[4,135,128]{2,1,0:T(8,128)(2,1)S(1)} %get-tuple-element.42), channel_id=1, source_target_pairs={{0,5},{4,1},{2,7},{6,3},{9,12},{13,8},{11,14},{15,10},{16,21},{20,... | collective-permute-start | bytes 414728 | tf_op jit(solution)/shard_map/ppermute | solution.py:532
  107.4 9.6 %collective-permute-start.17 = (bf16[4,135,128]{2,1,0:T(8,128)(2,1)S(1)}, bf16[4,135,128]{2,1,0:T(8,128)(2,1)S(1)}, u32[]{:S(2)}, u32[]{:S(2)}) collective-permute-start(bf16[4,135,128]{2,1,0:T(8,128)(2,1)S(1)} %get-tuple-element.43), channel_id=1, source_target_pairs={{0,7},{4,3},{2,1},{6,5},{9,10},{13,14},{11,12},{15,8},{16,23},{20,... | collective-permute-start | bytes 414728 | tf_op jit(solution)/shard_map/ppermute | solution.py:532
  108.7 8.3 %collective-permute-start.18 = (bf16[4,135,128]{2,1,0:T(8,128)(2,1)S(1)}, bf16[4,135,128]{2,1,0:T(8,128)(2,1)S(1)}, u32[]{:S(2)}, u32[]{:S(2)}) collective-permute-start(bf16[4,135,128]{2,1,0:T(8,128)(2,1)S(1)} %get-tuple-element.44), channel_id=1, source_target_pairs={{0,2},{4,6},{2,4},{6,0},{9,15},{13,11},{11,9},{15,13},{16,18},{20,... | collective-permute-start | bytes 414728 | tf_op jit(solution)/shard_map/ppermute | solution.py:532
  112.9 7.1 %collective-permute-start.19 = (bf16[4,135,128]{2,1,0:T(8,128)(2,1)S(1)}, bf16[4,135,128]{2,1,0:T(8,128)(2,1)S(1)}, u32[]{:S(2)}, u32[]{:S(2)}) collective-permute-start(bf16[4,135,128]{2,1,0:T(8,128)(2,1)S(1)} %get-tuple-element.45), channel_id=1, source_target_pairs={{0,4},{4,0},{2,6},{6,2},{9,13},{13,9},{11,15},{15,11},{16,20},{20,... | collective-permute-start | bytes 414728 | tf_op jit(solution)/shard_map/ppermute | solution.py:532
  114.8 7.6 %collective-permute-start.20 = (bf16[4,135,128]{2,1,0:T(8,128)(2,1)S(1)}, bf16[4,135,128]{2,1,0:T(8,128)(2,1)S(1)}, u32[]{:S(2)}, u32[]{:S(2)}) collective-permute-start(bf16[4,135,128]{2,1,0:T(8,128)(2,1)S(1)} %get-tuple-element.46), channel_id=1, source_target_pairs={{0,6},{4,2},{2,0},{6,4},{9,11},{13,15},{11,13},{15,9},{16,22},{20,... | collective-permute-start | bytes 414728 | tf_op jit(solution)/shard_map/ppermute | solution.py:532
